TPU v7x, 128 devices: a whole 4x4x4 slice. The times are simulated.
128 devices in a mesh: row: 32 (over y, x, core), col: 4 (over z).
Axes of the slice: x: 4, y: 4, z: 4, core: 2. Of those that a mesh axis runs over, the one named last changes fastest.
Arguments:
- acts: bfloat16 [122880, 6144], P(('row', 'col')), may hold values from -6 to 6
- out_grads: bfloat16 [122880, 6144], P(('row', 'col')), may hold values from -6 to 6
- test_matrix: bfloat16 [6144, 64], replicated, may hold values from -6 to 6
- weight: bfloat16 [6144, 6144], P('row', 'col'), may hold values from -6 to 6
Outputs:
- frozen: float32 [6144, 6144], P('row', 'col')
- adapter_left_factor: float32 [6144, 64], P('row')
- adapter_right_factor: float32 [64, 6144], P(None, 'col')
All inputs are finite; a program needn't handle non-finite values.
Results may differ from a plain program's by a relative error of at most 0.0035.
Values may be sent and summed in bfloat16 or wider, within the bound.
No kernel may reach another device: no remote copies, remote signals or barrier semaphores. Data moves between devices by JAX's collectives and lax.ppermute only.
A program may use at most 128 MiB of HBM per device.

v0:
```python
import math

import jax
import jax.numpy as jnp
from jax import lax
from jax.sharding import PartitionSpec as P


def contract(left_factor, right_factor):
    return jnp.einsum("tn,tr->nr", left_factor, right_factor, preferred_element_type=jnp.float32)


def solve_factor(block, gram):
    lower = jnp.linalg.cholesky(gram)
    return jax.scipy.linalg.solve_triangular(lower, block.T, lower=True).T


def local_gram(block):
    return jnp.dot(
        block.T, block, precision=lax.Precision.HIGHEST, preferred_element_type=jnp.float32
    )


def reduce_terms(left_factor, right_factor):
    block = lax.psum_scatter(
        contract(left_factor, right_factor), "row", scatter_dimension=0, tiled=True
    )
    return lax.psum(block, "col")


def orthonormal(block):
    gram = lax.psum(local_gram(block), "row")
    return solve_factor(block, gram)


def spread_basis(block):
    lowered = block.astype(jnp.bfloat16)
    return lax.all_gather(lowered, "row", axis=0, tiled=True)


def applied(left_factor, right_factor):
    return jnp.dot(left_factor, right_factor, preferred_element_type=jnp.float32).astype(
        jnp.bfloat16
    )


def local(acts, out_grads, test_matrix, weight):
    output_features = out_grads.shape[1]
    input_features = acts.shape[1]
    rank = test_matrix.shape[1]
    probe = applied(acts, test_matrix)
    basis = orthonormal(reduce_terms(out_grads, probe))
    back = applied(out_grads, spread_basis(basis))
    cobasis = orthonormal(reduce_terms(acts, back))
    forth = applied(acts, spread_basis(cobasis))
    left_factor = orthonormal(reduce_terms(out_grads, forth))
    again = applied(out_grads, spread_basis(left_factor))
    right_factor = orthonormal(reduce_terms(acts, again))
    col_count = weight.shape[1]
    right_full = lax.all_gather(right_factor, "row", axis=0, tiled=True)
    right_columns = lax.dynamic_slice_in_dim(
        right_full, lax.axis_index("col") * col_count, col_count, 0
    )
    adapter_left_factor = left_factor * math.sqrt(output_features)
    adapter_right_factor = right_columns.T * math.sqrt(input_features)
    product_matrix = jnp.dot(
        adapter_left_factor,
        adapter_right_factor,
        precision=lax.Precision.HIGHEST,
        preferred_element_type=jnp.float32,
    )
    frozen = weight.astype(jnp.float32) - product_matrix / math.sqrt(rank)
    return (frozen, adapter_left_factor, adapter_right_factor)


def solution(mesh):
    in_specs = (P(("row", "col"), None), P(("row", "col"), None), P(), P("row", "col"))
    out_specs = (P("row", "col"), P("row", None), P(None, "col"))
    return jax.shard_map(local, mesh=mesh, in_specs=in_specs, out_specs=out_specs, check_vma=False)
```

profile of v0, /device:TPU:1, one launch (start us, length us, event | category | flops | bytes accessed | tf_op | source)
XLA Modules:
  0.0 1140.3 jit_solution(6932769582674309952)
XLA Ops:
  7.2 1.1 copy-done
  8.3 13.4 %convolution_bitcast_fusion.3 = f32[6144,64]{0,1:T(8,128)S(1)} fusion(bf16[960,6144]{1,0:T(8,128)(2,1)} %param.8, bf16[960,6144]{1,0:T(8,128)(2,1)} %param.7, bf16[6144,64]{0,1:T(8,128)(2,1)S(1)} %copy-done), kind=kOutput, calls=%fused_computation.3 | convolution fusion | flops 1510010880 | bytes 25952256 | tf_op jit(solution)/shard_map/tn,tr->nr/dot_general | solution.py:10
  21.7 2.3 copy.43
  24.1 81.9 %reduce-scatter.13.cloned.1.call-done = f32[192,64]{1,0:T(8,128)} async-done(((f32[6144,64]{1,0:T(8,128)}), f32[192,64]{1,0:T(8,128)}) %reduce-scatter.13.cloned.1.call-update) | async-done | bytes 49168
  106.0 1.0 copy.44
  107.0 14.0 %psum.56 = f32[192,64]{0,1:T(8,128)S(1)} all-reduce(f32[192,64]{0,1:T(8,128)S(1)} %copy.44), channel_id=1, replica_groups=mesh['row'=32,'col'=4] {'col'}, use_global_device_ids=true, to_apply=%region_1.0 | all-reduce | flops 12288 | bytes 98304 | tf_op jit(solution)/shard_map/psum | solution.py:28
  121.2 124.2 %psum.57 = f32[64,64]{0,1:T(8,128)S(1)} all-reduce(f32[64,64]{0,1:T(8,128)S(1)} %fusion.30), channel_id=1, replica_groups=mesh['row'=32,'col'=4] {'row'}, use_global_device_ids=true, to_apply=%region_2.0 | all-reduce | flops 4096 | bytes 32768 | tf_op jit(solution)/shard_map/psum | solution.py:32
  245.4 5.8 cholesky.74
  251.9 0.7 fusion.11
  252.6 4.9 custom-call.8
  257.8 28.0 %all-gather = bf16[32,192,64]{1,2,0:T(8,128)(2,1)S(1)} all-gather(bf16[1,192,64]{1,2,0:T(8,128)(2,1)S(1)} %fusion.1), channel_id=1, replica_groups=mesh['row'=32,'col'=4] {'row'}, dimensions={0}, use_global_device_ids=true | all-gather | bytes 811008 | tf_op jit(solution)/shard_map/all_gather | solution.py:38
  286.4 1.1 reshape.15
  287.5 13.4 %convolution_bitcast_fusion.2 = f32[6144,64]{0,1:T(8,128)S(1)} fusion(bf16[960,6144]{1,0:T(8,128)(2,1)} %param.7, bf16[6144,64]{0,1:T(8,128)(2,1)S(1)} %reshape.15, bf16[960,6144]{1,0:T(8,128)(2,1)} %param.8), kind=kOutput, calls=%fused_computation.2 | convolution fusion | flops 1510010880 | bytes 25952256 | tf_op jit(solution)/shard_map/tn,tr->nr/dot_general | solution.py:10
  300.9 2.3 copy.45
  303.3 76.4 %reduce-scatter.15.cloned.1.call-done = f32[192,64]{1,0:T(8,128)} async-done(((f32[6144,64]{1,0:T(8,128)}), f32[192,64]{1,0:T(8,128)}) %reduce-scatter.15.cloned.1.call-update) | async-done | bytes 49168
  379.7 1.0 copy.46
  380.7 13.9 %psum.58 = f32[192,64]{0,1:T(8,128)S(1)} all-reduce(f32[192,64]{0,1:T(8,128)S(1)} %copy.46), channel_id=1, replica_groups=mesh['row'=32,'col'=4] {'col'}, use_global_device_ids=true, to_apply=%region_6.0 | all-reduce | flops 12288 | bytes 98304 | tf_op jit(solution)/shard_map/psum | solution.py:28
  394.9 124.1 %psum.59 = f32[64,64]{0,1:T(8,128)S(1)} all-reduce(f32[64,64]{0,1:T(8,128)S(1)} %fusion.31), channel_id=1, replica_groups=mesh['row'=32,'col'=4] {'row'}, use_global_device_ids=true, to_apply=%region_7.0 | all-reduce | flops 4096 | bytes 32768 | tf_op jit(solution)/shard_map/psum | solution.py:32
  519.1 5.8 cholesky.85
  525.6 0.7 fusion.12
  526.3 4.9 custom-call.9
  531.5 27.6 %all-gather.1 = bf16[32,192,64]{1,2,0:T(8,128)(2,1)S(1)} all-gather(bf16[1,192,64]{1,2,0:T(8,128)(2,1)S(1)} %fusion.2), channel_id=1, replica_groups=mesh['row'=32,'col'=4] {'row'}, dimensions={0}, use_global_device_ids=true | all-gather | bytes 811008 | tf_op jit(solution)/shard_map/all_gather | solution.py:38
  559.7 1.1 reshape.17
  560.8 13.4 %convolution_bitcast_fusion.1 = f32[6144,64]{0,1:T(8,128)S(1)} fusion(bf16[960,6144]{1,0:T(8,128)(2,1)} %param.8, bf16[6144,64]{0,1:T(8,128)(2,1)S(1)} %reshape.17, bf16[960,6144]{1,0:T(8,128)(2,1)} %param.7), kind=kOutput, calls=%fused_computation.1 | convolution fusion | flops 1510010880 | bytes 25952256 | tf_op jit(solution)/shard_map/tn,tr->nr/dot_general | solution.py:10
  574.3 2.3 copy.47
  576.6 76.4 %reduce-scatter.17.cloned.1.call-done = f32[192,64]{1,0:T(8,128)} async-done(((f32[6144,64]{1,0:T(8,128)}), f32[192,64]{1,0:T(8,128)}) %reduce-scatter.17.cloned.1.call-update) | async-done | bytes 49168
  653.1 1.0 copy.48
  654.0 14.0 %psum.60 = f32[192,64]{0,1:T(8,128)S(1)} all-reduce(f32[192,64]{0,1:T(8,128)S(1)} %copy.48), channel_id=1, replica_groups=mesh['row'=32,'col'=4] {'col'}, use_global_device_ids=true, to_apply=%region_9.0 | all-reduce | flops 12288 | bytes 98304 | tf_op jit(solution)/shard_map/psum | solution.py:28
  668.2 124.2 %psum.61 = f32[64,64]{0,1:T(8,128)S(1)} all-reduce(f32[64,64]{0,1:T(8,128)S(1)} %fusion.32), channel_id=1, replica_groups=mesh['row'=32,'col'=4] {'row'}, use_global_device_ids=true, to_apply=%region_10.0 | all-reduce | flops 4096 | bytes 32768 | tf_op jit(solution)/shard_map/psum | solution.py:32
  792.5 5.8 cholesky.96
  799.7 4.9 custom-call.10
  805.5 27.6 %all-gather.2 = bf16[32,192,64]{1,2,0:T(8,128)(2,1)S(1)} all-gather(bf16[1,192,64]{1,2,0:T(8,128)(2,1)S(1)} %get-tuple-element.6), channel_id=1, replica_groups=mesh['row'=32,'col'=4] {'row'}, dimensions={0}, use_global_device_ids=true | all-gather | bytes 811008 | tf_op jit(solution)/shard_map/all_gather | solution.py:38
  833.7 1.1 reshape.19
  834.9 13.4 %convolution_bitcast_fusion = f32[6144,64]{0,1:T(8,128)S(1)} fusion(bf16[960,6144]{1,0:T(8,128)(2,1)} %param.7, bf16[6144,64]{0,1:T(8,128)(2,1)S(1)} %reshape.19, bf16[960,6144]{1,0:T(8,128)(2,1)} %param.8), kind=kOutput, calls=%fused_computation | convolution fusion | flops 1510010880 | bytes 25952256 | tf_op jit(solution)/shard_map/tn,tr->nr/dot_general | solution.py:10
  848.3 2.3 copy.49
  850.7 76.4 %reduce-scatter.19.cloned.1.call-done = f32[192,64]{1,0:T(8,128)} async-done(((f32[6144,64]{1,0:T(8,128)}), f32[192,64]{1,0:T(8,128)}) %reduce-scatter.19.cloned.1.call-update) | async-done | bytes 49168
  927.1 1.0 copy.50
  928.0 14.0 %psum.62 = f32[192,64]{0,1:T(8,128)S(1)} all-reduce(f32[192,64]{0,1:T(8,128)S(1)} %copy.50), channel_id=1, replica_groups=mesh['row'=32,'col'=4] {'col'}, use_global_device_ids=true, to_apply=%region_12.15 | all-reduce | flops 12288 | bytes 98304 | tf_op jit(solution)/shard_map/psum | solution.py:28
  942.2 124.4 %psum.63 = f32[64,64]{0,1:T(8,128)S(1)} all-reduce(f32[64,64]{0,1:T(8,128)S(1)} %fusion.33), channel_id=1, replica_groups=mesh['row'=32,'col'=4] {'row'}, use_global_device_ids=true, to_apply=%region_13.16 | all-reduce | flops 4096 | bytes 32768 | tf_op jit(solution)/shard_map/psum | solution.py:32
  1066.7 5.8 cholesky.107
  1073.3 0.7 fusion.14
  1073.9 4.9 custom-call.11
  1078.8 0.9 convolution_bitcast_fusion.4
  1079.7 44.0 %all-gather.6.cloned.1.call-done = f32[32,192,64]{1,2,0:T(8,128)} async-done(((f32[1,192,64]{1,2,0:T(8,128)}), f32[32,192,64]{1,2,0:T(8,128)}) %all-gather.6.cloned.1.call-update) | async-done | bytes 1572880 | tf_op jit(solution)/shard_map/all_gather | solution.py:60
  1123.7 2.8 copy.38
  1126.5 2.0 reshape.21
  1128.5 1.8 fusion.3
  1130.3 3.2 fusion
  (41 shorter events, 8.0 us)
Async XLA Ops:
  7.2 1.1 copy-start
  7.2 98.8 %reduce-scatter.13.cloned.1.call-start = ((), (), s32[]{:S(2)}) async-start(), calls=%async_computation.5 | async-start | bytes 3244032
  24.0 355.7 %reduce-scatter.15.cloned.1.call-start = ((), (), s32[]{:S(2)}) async-start(), calls=%async_computation.6 | async-start | bytes 3244032
  303.2 349.8 %reduce-scatter.17.cloned.1.call-start = ((), (), s32[]{:S(2)}) async-start(), calls=%async_computation.7 | async-start | bytes 3244032
  576.6 350.5 %reduce-scatter.19.cloned.1.call-start = ((), (), s32[]{:S(2)}) async-start(), calls=%async_computation.8 | async-start | bytes 3244032
  848.3 282.0 %copy-start.1 = (bf16[192,1536]{1,0:T(8,128)(2,1)S(1)}, bf16[192,1536]{1,0:T(8,128)(2,1)}, u32[]{:S(2)}) copy-start(bf16[192,1536]{1,0:T(8,128)(2,1)} %param.10) | copy-start | bytes 1769476
  850.6 273.1 %all-gather.6.cloned.1.call-start = ((), (), s32[]{:S(2)}) async-start(), calls=%async_computation.4 | async-start | bytes 2162688 | tf_op jit(solution)/shard_map/all_gather | solution.py:60
Sparse Core Ops, SparseCore 0:
  24.2 81.7 reduce-scatter.12
  303.4 76.3 reduce-scatter.14
  576.7 76.3 reduce-scatter.16
  850.7 76.2 reduce-scatter.18
  1079.9 43.8 all-gather.5
where the time goes:
time: 1150 us; the launch traced here: 1140 us
  blocking collectives  636 us (55%)
  waiting for transfers between devices  355 us (31%)
  matrix products  59.5 us (5%)
  other arithmetic  50.7 us (4%)
  local copies, waits for them, and re-layouts  24.3 us (2%)
  between operations  14.3 us (1%)
    psum x4, blocking collectives, orthonormal(): gram = lax.psum(local_gram(block), 'row')  497 us
    unnamed x9, waiting for transfers between devices  311 us
    all_gather x3, blocking collectives, spread_basis(): return lax.all_gather(lowered, 'row', axis=0, tiled=True)  83.3 us
    psum x4, blocking collectives, reduce_terms(): return lax.psum(block, 'col')  55.8 us
    dot_general x4, matrix products, contract(): jnp.einsum('tn,tr->nr', left_factor, right_factor, preferred_element_type...  53.8 us
    all_gather x1, waiting for transfers between devices, local(): right_full = lax.all_gather(right_factor, 'row', axis=0, tiled=True)  44 us
    another operation x12, other arithmetic, solve_factor(): lower = jnp.linalg.cholesky(gram)  26.1 us
  transfers between devices with their start and end apart: 5, of which 5 were waited for; matrix products, arithmetic and copies ran while one was open for 0% of the time, Pallas kernels for 0%

commit v1 on v0

v1 whole, which is shorter than its diff:
```python
import math

import jax
import jax.numpy as jnp
from jax import lax
from jax.sharding import Mesh, PartitionSpec as P

CHIPS = ("y", "x", "z")
HIGHEST = lax.Precision.HIGHEST


def to_parts(wide):
    rank, n = wide.shape
    parts = wide.reshape(2, 4, 8, 16, n // 16).transpose(0, 1, 3, 2, 4)
    return parts.reshape(2, 64, 8, n // 16)


def from_parts(parts):
    _, _, rows, lanes = parts.shape
    wide = parts.reshape(2, 4, 16, rows, lanes).transpose(0, 1, 3, 2, 4)
    return wide.reshape(8 * rows, 16 * lanes)


def swap_cores(value):
    return lax.ppermute(value, "core", [(0, 1), (1, 0)])


def total(wide):
    parts = to_parts(wide)
    core = lax.axis_index("core")
    own = lax.dynamic_index_in_dim(parts, core, 0, keepdims=False)
    other = lax.dynamic_index_in_dim(parts, 1 - core, 0, keepdims=False)
    got = swap_cores(other.astype(jnp.bfloat16))
    pair = (own + got.astype(jnp.float32)).astype(jnp.bfloat16)
    terms = lax.all_to_all(pair, CHIPS, 0, 0, tiled=True)
    mine = jnp.sum(terms.astype(jnp.float32), axis=0)
    copies = jnp.broadcast_to(mine[None], terms.shape)
    half = lax.all_to_all(copies, CHIPS, 0, 0, tiled=True)
    return from_parts(lax.all_gather(half, "core", axis=0, tiled=False))


def inverse_factor(wide):
    wide = wide.astype(jnp.float32)
    gram = lax.dot_general(
        wide, wide, (((1,), (1,)), ((), ())), precision=HIGHEST,
        preferred_element_type=jnp.float32,
    )
    lower = jnp.linalg.cholesky(gram)
    return jax.scipy.linalg.solve_triangular(lower, jnp.eye(64, dtype=jnp.float32), lower=True)


def product(left, right, contract):
    return lax.dot_general(
        left, right, ((contract[:1], contract[1:]), ((), ())),
        preferred_element_type=jnp.float32,
    )


def exact(left, right):
    return jnp.dot(left, right, precision=HIGHEST, preferred_element_type=jnp.float32)


def step(tokens, wide, other):
    basis = exact(inverse_factor(wide), wide).astype(jnp.bfloat16)
    applied = product(basis, tokens, (1, 1)).astype(jnp.bfloat16)
    return product(applied, other, (1, 0))


def local(acts, out_grads, test_matrix, weight):
    rows, cols = weight.shape
    n = acts.shape[1]
    row = (lax.axis_index("y") * 4 + lax.axis_index("x")) * 2 + lax.axis_index("core")
    col = lax.axis_index("z")
    probe = product(test_matrix, acts, (0, 1)).astype(jnp.bfloat16)
    sketch = total(product(probe, out_grads, (1, 0)))
    cosketch = total(step(out_grads, sketch, acts))
    power = total(step(acts, cosketch, out_grads))
    project = total(step(out_grads, power, acts))
    left = exact(
        inverse_factor(power), lax.dynamic_slice_in_dim(power, row * rows, rows, 1)
    )
    right = exact(
        inverse_factor(project), lax.dynamic_slice_in_dim(project, col * cols, cols, 1)
    )
    left = left.T * math.sqrt(n)
    right = right * math.sqrt(n)
    frozen = weight.astype(jnp.float32) - exact(left, right) / math.sqrt(64)
    return (frozen, left, right)


def solution(mesh):
    mesh = Mesh(mesh.devices.reshape(4, 4, 2, 4), ("y", "x", "core", "z"))
    row = ("y", "x", "core")
    tokens = P((*row, "z"), None)
    return jax.shard_map(
        local, mesh=mesh, in_specs=(tokens, tokens, P(), P(row, "z")),
        out_specs=(P(row, "z"), P(row, None), P(None, "z")), check_vma=False,
    )
```

time: 1150 us -> 363 us (0.32)
  blocking collectives: 636 us -> 159 us
  waiting for transfers between devices: 355 us -> 49.6 us
  local copies, waits for them, and re-layouts: 24.3 us -> 2.96 us
  matrix products: 59.5 us -> 78 us
    psum x8 -> x0, blocking collectives: 553 us -> none  [the longest x4 497 us: orthonormal(): gram = lax.psum(local_gram(block), 'row')]
    unnamed x9 -> x4, waiting for transfers between devices: 311 us -> 0.07 us
    all_to_all x0 -> x8, blocking collectives: none -> 159 us  [the longest x4 85 us: total(): terms = lax.all_to_all(pair, CHIPS, 0, 0, tiled=True)]
    all_gather x3 -> x0, blocking collectives: 83.3 us -> none  [spread_basis(): return lax.all_gather(lowered, 'row', axis=0, tiled=True)]
    dot_general x9 -> x14, matrix products: 57.8 us -> 77 us  [the longest x4 54.9 us: product(): lax.dot_general(left, right, ((contract[:1], contract[1:]), ((), ())), pr...]
    unnamed x16 -> x14, local copies, waits for them, and re-layouts: 19.4 us -> 1.11 us
    all_gather x1 -> x4, waiting for transfers between devices: 44 us -> 43.6 us  [total(): return from_parts(lax.all_gather(half, 'core', axis=0, tiled=False))]
  transfers between devices with their start and end apart: 5 -> 8, of which waited for: 5 -> 8; matrix products, arithmetic and copies ran while one was open for 0% -> 0% of each run, Pallas kernels for 0% -> 0%
where the time goes in v1:
time: 363 us; the launch traced here: 357 us
  blocking collectives  159 us (44%)
  matrix products  78 us (21%)
  other arithmetic  50.1 us (14%)
  waiting for transfers between devices  49.6 us (14%)
  between operations  14.3 us (4%)
    all_to_all x4, blocking collectives, total(): terms = lax.all_to_all(pair, CHIPS, 0, 0, tiled=True)  85 us
    all_to_all x4, blocking collectives, total(): half = lax.all_to_all(copies, CHIPS, 0, 0, tiled=True)  74.1 us
    dot_general x4, matrix products, product(): lax.dot_general(left, right, ((contract[:1], contract[1:]), ((), ())), pr...  54.9 us
    all_gather x4, waiting for transfers between devices, total(): return from_parts(lax.all_gather(half, 'core', axis=0, tiled=False))  43.6 us
    another operation x12, other arithmetic, inverse_factor(): lower = jnp.linalg.cholesky(gram)  26.1 us
    another operation x8, other arithmetic, inverse_factor(): jax.scipy.linalg.solve_triangular(lower, jnp.eye(64, dtype=jnp.float32),...  22.2 us
    dot_general x4, matrix products, inverse_factor(): lax.dot_general(wide, wide, (((1,), (1,)), ((), ())), precision=HIGHEST,...  13.6 us
    dot_general x6, matrix products, exact(): jnp.dot(left, right, precision=HIGHEST, preferred_element_type=jnp.float32)  8.45 us
  transfers between devices with their start and end apart: 8, of which 8 were waited for; matrix products, arithmetic and copies ran while one was open for 0% of the time, Pallas kernels for 0%

profile of v1, /device:TPU:1, one launch (start us, length us, event | category | flops | bytes accessed | tf_op | source)
XLA Modules:
  0.0 357.4 jit_solution(15549112865157608712)
XLA Ops:
  7.2 1.1 copy-done
  8.3 13.4 %fusion.5 = f32[64,6144]{1,0:T(8,128)S(1)} fusion(bf16[960,6144]{1,0:T(8,128)(2,1)} %param.8, bf16[6144,64]{0,1:T(8,128)(2,1)S(1)} %copy-done, bf16[960,6144]{1,0:T(8,128)(2,1)} %param.7), kind=kOutput, calls=%fused_computation.27 | convolution fusion | flops 1510010880 | bytes 25952256 | tf_op jit(solution)/shard_map/dot_general | solution.py:53
  21.8 1.5 collective-permute-start
  23.3 1.3 collective-permute-done
  24.7 22.0 %all_to_all.40 = bf16[64,8,384]{2,1,0:T(8,128)(2,1)S(1)} all-to-all(bf16[64,8,384]{2,1,0:T(8,128)(2,1)S(1)} %fusion.4), channel_id=1, replica_groups=mesh['y'=4,'x'=4,'core'=2,'z'=4] {'y','x','z'}, dimensions={0} | all-to-all | bytes 786432 | tf_op jit(solution)/shard_map/all_to_all | solution.py:35
  46.9 18.4 %all_to_all.41 = f32[64,8,384]{2,1,0:T(8,128)} all-to-all(f32[64,8,384]{2,1,0:T(8,128)S(1)} %broadcast_in_dim.9), channel_id=1, replica_groups=mesh['y'=4,'x'=4,'core'=2,'z'=4] {'y','x','z'}, dimensions={0} | all-to-all | bytes 1572864 | tf_op jit(solution)/shard_map/all_to_all | solution.py:38
  65.5 11.0 %all-gather.9.cloned.1.call-done = f32[128,8,384]{2,1,0:T(8,128)} async-done(((f32[64,8,384]{2,1,0:T(8,128)}), f32[128,8,384]{2,1,0:T(8,128)}) %all-gather.9.cloned.1.call-update) | async-done | bytes 1572880 | tf_op jit(solution)/shard_map/all_gather | solution.py:39
  76.6 3.4 fusion.39
  80.1 5.8 %cholesky.74 = f32[64,64]{1,0:T(8,128)S(1)} custom-call(f32[64,64]{1,0:T(8,128)S(1)} %fusion.34), custom_call_target="Cholesky" | custom-call | tf_op jit(solution)/shard_map/jit(cholesky)/cholesky | solution.py:48
  86.0 0.6 compare_reduce_fusion.3
  86.6 0.7 fusion.23
  87.3 4.9 %custom-call.8 = f32[1,64,64]{1,2,0:T(8,128)S(1)} custom-call(f32[1,64,64]{2,1,0:T(8,128)S(1)} %fusion.23), custom_call_target="InvertDiagBlocksLowerTriangular" | custom-call | tf_op jit(solution)/shard_map/jit(_solve_triangular)/triangular_solve | solution.py:49
  92.4 1.5 convolution_convert_fusion.2
  93.9 13.4 %fusion.6 = f32[64,6144]{1,0:T(8,128)S(1)} fusion(bf16[960,6144]{1,0:T(8,128)(2,1)} %param.7, bf16[64,6144]{1,0:T(8,128)(2,1)S(1)} %convolution_convert_fusion.2, bf16[960,6144]{1,0:T(8,128)(2,1)} %param.8), kind=kOutput, calls=%fused_computation.28 | convolution fusion | flops 1510010880 | bytes 25952256 | tf_op jit(solution)/shard_map/dot_general | solution.py:53
  107.7 1.5 collective-permute-done.1
  109.3 21.0 %all_to_all.42 = bf16[64,8,384]{2,1,0:T(8,128)(2,1)S(1)} all-to-all(bf16[64,8,384]{2,1,0:T(8,128)(2,1)S(1)} %fusion.3), channel_id=1, replica_groups=mesh['y'=4,'x'=4,'core'=2,'z'=4] {'y','x','z'}, dimensions={0} | all-to-all | bytes 786432 | tf_op jit(solution)/shard_map/all_to_all | solution.py:35
  130.5 18.5 %all_to_all.43 = f32[64,8,384]{2,1,0:T(8,128)} all-to-all(f32[64,8,384]{2,1,0:T(8,128)S(1)} %broadcast_in_dim.10), channel_id=1, replica_groups=mesh['y'=4,'x'=4,'core'=2,'z'=4] {'y','x','z'}, dimensions={0} | all-to-all | bytes 1572864 | tf_op jit(solution)/shard_map/all_to_all | solution.py:38
  149.3 11.0 %all-gather.11.cloned.1.call-done = f32[128,8,384]{2,1,0:T(8,128)} async-done(((f32[64,8,384]{2,1,0:T(8,128)}), f32[128,8,384]{2,1,0:T(8,128)}) %all-gather.11.cloned.1.call-update) | async-done | bytes 1572880 | tf_op jit(solution)/shard_map/all_gather | solution.py:39
  160.2 3.4 fusion.40
  163.7 5.8 %cholesky.85 = f32[64,64]{1,0:T(8,128)S(1)} custom-call(f32[64,64]{1,0:T(8,128)S(1)} %fusion.32), custom_call_target="Cholesky" | custom-call | tf_op jit(solution)/shard_map/jit(cholesky)/cholesky | solution.py:48
  170.3 0.7 fusion.24
  170.9 4.9 %custom-call.9 = f32[1,64,64]{1,2,0:T(8,128)S(1)} custom-call(f32[1,64,64]{2,1,0:T(8,128)S(1)} %fusion.24), custom_call_target="InvertDiagBlocksLowerTriangular" | custom-call | tf_op jit(solution)/shard_map/jit(_solve_triangular)/triangular_solve | solution.py:49
  176.1 1.5 convolution_convert_fusion.1
  177.6 13.4 %fusion.7 = f32[64,6144]{1,0:T(8,128)S(1)} fusion(bf16[960,6144]{1,0:T(8,128)(2,1)} %param.8, bf16[64,6144]{1,0:T(8,128)(2,1)S(1)} %convolution_convert_fusion.1, bf16[960,6144]{1,0:T(8,128)(2,1)} %param.7), kind=kOutput, calls=%fused_computation.29 | convolution fusion | flops 1510010880 | bytes 25952256 | tf_op jit(solution)/shard_map/dot_general | solution.py:53
  191.4 1.5 collective-permute-done.2
  193.0 21.0 %all_to_all.44 = bf16[64,8,384]{2,1,0:T(8,128)(2,1)S(1)} all-to-all(bf16[64,8,384]{2,1,0:T(8,128)(2,1)S(1)} %fusion.2), channel_id=1, replica_groups=mesh['y'=4,'x'=4,'core'=2,'z'=4] {'y','x','z'}, dimensions={0} | all-to-all | bytes 786432 | tf_op jit(solution)/shard_map/all_to_all | solution.py:35
  214.2 18.5 %all_to_all.45 = f32[64,8,384]{2,1,0:T(8,128)} all-to-all(f32[64,8,384]{2,1,0:T(8,128)S(1)} %broadcast_in_dim.11), channel_id=1, replica_groups=mesh['y'=4,'x'=4,'core'=2,'z'=4] {'y','x','z'}, dimensions={0} | all-to-all | bytes 1572864 | tf_op jit(solution)/shard_map/all_to_all | solution.py:38
  233.2 10.8 %all-gather.13.cloned.1.call-done = f32[128,8,384]{2,1,0:T(8,128)} async-done(((f32[64,8,384]{2,1,0:T(8,128)}), f32[128,8,384]{2,1,0:T(8,128)}) %all-gather.13.cloned.1.call-update) | async-done | bytes 1572880 | tf_op jit(solution)/shard_map/all_gather | solution.py:39
  243.9 3.4 fusion.41
  247.4 5.8 %cholesky.96 = f32[64,64]{1,0:T(8,128)S(1)} custom-call(f32[64,64]{1,0:T(8,128)S(1)} %fusion.30), custom_call_target="Cholesky" | custom-call | tf_op jit(solution)/shard_map/jit(cholesky)/cholesky | solution.py:48
  253.3 0.6 compare_reduce_fusion.1
  254.0 0.7 fusion.25
  254.6 4.9 %custom-call.10 = f32[1,64,64]{1,2,0:T(8,128)S(1)} custom-call(f32[1,64,64]{2,1,0:T(8,128)S(1)} %fusion.25), custom_call_target="InvertDiagBlocksLowerTriangular" | custom-call | tf_op jit(solution)/shard_map/jit(_solve_triangular)/triangular_solve | solution.py:49
  259.8 1.5 convolution_convert_fusion
  261.3 14.6 %fusion.8 = f32[64,6144]{1,0:T(8,128)} fusion(bf16[960,6144]{1,0:T(8,128)(2,1)} %param.7, bf16[64,6144]{1,0:T(8,128)(2,1)S(1)} %convolution_convert_fusion, bf16[960,6144]{1,0:T(8,128)(2,1)} %param.8), kind=kOutput, calls=%fused_computation.30 | convolution fusion | flops 1510010880 | bytes 25952256 | tf_op jit(solution)/shard_map/dot_general | solution.py:53
  275.9 1.2 fusion.12
  277.4 1.5 collective-permute-done.3
  278.9 1.2 fusion.1
  280.1 21.0 %all_to_all.46 = bf16[64,8,384]{2,1,0:T(8,128)(2,1)S(1)} all-to-all(bf16[64,8,384]{2,1,0:T(8,128)(2,1)S(1)} %fusion.1), channel_id=1, replica_groups=mesh['y'=4,'x'=4,'core'=2,'z'=4] {'y','x','z'}, dimensions={0} | all-to-all | bytes 786432 | tf_op jit(solution)/shard_map/all_to_all | solution.py:35
  301.3 18.7 %all_to_all.47 = f32[64,8,384]{2,1,0:T(8,128)} all-to-all(f32[64,8,384]{2,1,0:T(8,128)S(1)} %broadcast_in_dim.12), channel_id=1, replica_groups=mesh['y'=4,'x'=4,'core'=2,'z'=4] {'y','x','z'}, dimensions={0} | all-to-all | bytes 1572864 | tf_op jit(solution)/shard_map/all_to_all | solution.py:38
  320.3 10.9 %all-gather.15.cloned.1.call-done = f32[128,8,384]{2,1,0:T(8,128)} async-done(((f32[64,8,384]{2,1,0:T(8,128)}), f32[128,8,384]{2,1,0:T(8,128)}) %all-gather.15.cloned.1.call-update) | async-done | bytes 1572880 | tf_op jit(solution)/shard_map/all_gather | solution.py:39
  331.2 3.3 fusion.42
  334.6 5.8 %cholesky.107 = f32[64,64]{1,0:T(8,128)S(1)} custom-call(f32[64,64]{1,0:T(8,128)S(1)} %fusion.28), custom_call_target="Cholesky" | custom-call | tf_op jit(solution)/shard_map/jit(cholesky)/cholesky | solution.py:48
  340.5 0.6 compare_reduce_fusion
  341.1 0.7 fusion.26
  341.8 4.9 %custom-call.11 = f32[1,64,64]{1,2,0:T(8,128)S(1)} custom-call(f32[1,64,64]{2,1,0:T(8,128)S(1)} %fusion.26), custom_call_target="InvertDiagBlocksLowerTriangular" | custom-call | tf_op jit(solution)/shard_map/jit(_solve_triangular)/triangular_solve | solution.py:49
  347.0 1.5 convolution_multiply_fusion.1
  348.5 2.2 fusion
  (56 shorter events, 5.2 us)
Async XLA Ops:
  7.2 1.1 copy-start
  7.2 69.4 %all-gather.9.cloned.1.call-start = ((), (), s32[]{:S(2)}) async-start(), calls=%async_computation.8 | async-start | bytes 2359296 | tf_op jit(solution)/shard_map/all_gather | solution.py:39
  21.8 2.9 collective-permute-start
  65.3 94.9 %all-gather.11.cloned.1.call-start = ((), (), s32[]{:S(2)}) async-start(), calls=%async_computation.9 | async-start | bytes 2359296 | tf_op jit(solution)/shard_map/all_gather | solution.py:39
  76.6 15.9 %copy-start.2 = (f32[128,8,384]{2,1,0:T(8,128)S(1)}, f32[128,8,384]{2,1,0:T(8,128)}, u32[]{:S(2)}) copy-start(f32[128,8,384]{2,1,0:T(8,128)} %all-gather.9.cloned.1.call-done) | copy-start | bytes 4718596
  107.5 1.8 collective-permute-start.1
  149.0 94.9 %all-gather.13.cloned.1.call-start = ((), (), s32[]{:S(2)}) async-start(), calls=%async_computation.10 | async-start | bytes 2359296 | tf_op jit(solution)/shard_map/all_gather | solution.py:39
  160.2 15.9 %copy-start.3 = (f32[128,8,384]{2,1,0:T(8,128)S(1)}, f32[128,8,384]{2,1,0:T(8,128)}, u32[]{:S(2)}) copy-start(f32[128,8,384]{2,1,0:T(8,128)} %all-gather.11.cloned.1.call-done) | copy-start | bytes 4718596
  191.1 1.8 collective-permute-start.2
  232.7 98.5 %all-gather.15.cloned.1.call-start = ((), (), s32[]{:S(2)}) async-start(), calls=%async_computation.11 | async-start | bytes 2359296 | tf_op jit(solution)/shard_map/all_gather | solution.py:39
  243.9 15.9 %copy-start.1 = (f32[128,8,384]{2,1,0:T(8,128)S(1)}, f32[128,8,384]{2,1,0:T(8,128)}, u32[]{:S(2)}) copy-start(f32[128,8,384]{2,1,0:T(8,128)} %all-gather.13.cloned.1.call-done) | copy-start | bytes 4718596
  277.1 1.8 collective-permute-start.3
  320.3 28.2 %copy-start.6 = (f32[192,64]{0,1:T(8,128)}, f32[192,64]{0,1:T(8,128)S(1)}, u32[]{:S(2)}) copy-start(f32[192,64]{0,1:T(8,128)S(1)} %convolution_multiply_fusion.2) | copy-start | bytes 147460
  331.2 17.3 %copy-start.5 = (bf16[192,1536]{1,0:T(8,128)(2,1)S(1)}, bf16[192,1536]{1,0:T(8,128)(2,1)}, u32[]{:S(2)}) copy-start(bf16[192,1536]{1,0:T(8,128)(2,1)} %param.10) | copy-start | bytes 1769476
  348.5 2.2 copy-start.4
Sparse Core Ops, SparseCore 0:
  65.4 11.0 all-gather.8
  149.1 11.0 all-gather.10
  232.8 11.0 all-gather.12
  320.1 11.0 all-gather.14

commit v2 on v1

v2 whole, which is shorter than its diff:
```python
import math

import jax
import jax.numpy as jnp
from jax import lax
from jax.experimental import pallas as pl
from jax.experimental.pallas import tpu as pltpu
from jax.sharding import Mesh, PartitionSpec as P

CHIPS = ("y", "x", "z")
F32 = jnp.float32
BF16 = jnp.bfloat16
RANK = 64
VMEM = pl.BlockSpec(memory_space=pltpu.VMEM)
ANY = pl.BlockSpec(memory_space=pl.ANY)
PARAMS = pltpu.CompilerParams(vmem_limit_bytes=56 * 2**20)
GROUPS = 4
LANES = 16


def dot(left, right, contract):
    dims = (((contract[0],), (contract[1],)), ((), ()))
    return lax.dot_general(left, right, dims, preferred_element_type=F32)


def split(value):
    high = value.astype(BF16)
    return high, (value - high.astype(F32)).astype(BF16)


def exact(left, right):
    left_high, left_low = split(left)
    right_high, right_low = split(right)
    return dot(
        jnp.concatenate([left_high, left_high, left_low], 1),
        jnp.concatenate([right_high, right_low, right_high], 0),
        (1, 0),
    )


def inverse_factor(gram):
    shape = (RANK, RANK)
    eye = lax.broadcasted_iota(jnp.int32, shape, 0) == lax.broadcasted_iota(jnp.int32, shape, 1)
    both = jnp.concatenate([gram, eye.astype(F32)], 1)
    work = [both[8 * i : 8 * i + 8] for i in range(8)]
    tile = (8, 2 * RANK)
    sub = lax.broadcasted_iota(jnp.int32, tile, 0)
    done = []
    for p in range(8):
        cols = {
            i: [jnp.broadcast_to(work[i][:, k : k + 1], tile) for k in range(8 * p, 8 * p + 8)]
            for i in range(p, 8)
        }
        pivots = jnp.zeros(tile, F32)
        for j in range(8):
            pivot = jnp.broadcast_to(cols[p][j][j : j + 1], tile)
            inverse = 1.0 / pivot
            pivots = jnp.where(sub == j, pivot, pivots)
            row = jnp.broadcast_to(work[p][j : j + 1], tile)
            ahead = {q: jnp.broadcast_to(cols[p][q][j : j + 1], tile) for q in range(j + 1, 8)}
            for i in range(p, 8):
                scale = cols[i][j] * inverse
                if i == p:
                    scale = jnp.where(sub > j, scale, 0.0)
                work[i] = work[i] - scale * row
                for q in range(j + 1, 8):
                    cols[i][q] = cols[i][q] - scale * ahead[q]
        done.append(work[p] * lax.rsqrt(pivots))
    return jnp.concatenate(done, 0)[:, RANK:]


def wide_block(first, own_ref, other_ref, lane):
    own = [own_ref[g * LANES + lane] for g in range(GROUPS)]
    other = [other_ref[g * LANES + lane] for g in range(GROUPS)]
    low = [jnp.where(first, a, b) for a, b in zip(own, other)]
    high = [jnp.where(first, b, a) for a, b in zip(own, other)]
    return jnp.concatenate(low + high, 0)


def gram_of(first, own_ref, other_ref, split_ref=None):
    width = own_ref.shape[2]
    gram = jnp.zeros((2 * RANK, 2 * RANK), F32)
    for lane in range(LANES):
        terms = jnp.concatenate(split(wide_block(first, own_ref, other_ref, lane)), 0)
        if split_ref is not None:
            split_ref[:, lane * width : (lane + 1) * width] = terms
        gram = gram + dot(terms, terms, (1, 1))
    cross = gram[:RANK, RANK:] + gram[RANK:, :RANK]
    return gram[:RANK, :RANK] + (gram[RANK:, RANK:] + cross)


def store_parts(first, part, index, keep_ref, send_ref):
    width = keep_ref.shape[2]
    for h in range(2):
        for g in range(GROUPS):
            low = part[8 * g : 8 * g + 8, h * width : (h + 1) * width]
            high = part[32 + 8 * g : 40 + 8 * g, h * width : (h + 1) * width]
            at = g * LANES + 2 * index + h
            keep_ref[at] = jnp.where(first, low, high)
            send_ref[at] = jnp.where(first, high, low).astype(BF16)


def chunks(total, size):
    return [(s, min(size, total - s)) for s in range(0, total, size)]


def row_copies(ref, held, sems):
    return [
        pltpu.make_async_copy(ref.at[pl.ds(s, n), :], held.at[pl.ds(s, n), :], sems.at[i])
        for i, (s, n) in enumerate(chunks(ref.shape[0], 256))
    ]


def col_copies(ref, held, sems):
    return [
        pltpu.make_async_copy(ref.at[:, pl.ds(s, n)], held.at[:, pl.ds(s, n)], sems.at[i])
        for i, (s, n) in enumerate(chunks(ref.shape[1], ref.shape[1] // 8))
    ]


def first_kernel(test_ref, a_ref, b_ref, keep_ref, send_ref, a_held, b_held, a_sems, b_sems):
    first = lax.axis_index("core") == 0
    a_copies = row_copies(a_ref, a_held, a_sems)
    b_copies = col_copies(b_ref, b_held, b_sems)
    for copy in a_copies + b_copies:
        copy.start()
    test = test_ref[...]
    applied = []
    for copy, (s, n) in zip(a_copies, chunks(a_ref.shape[0], 256)):
        copy.wait()
        applied.append(dot(a_held[s : s + n, :], test, (1, 0)).astype(BF16))
    applied = jnp.concatenate(applied, 0)
    for i, (copy, (s, n)) in enumerate(zip(b_copies, chunks(b_ref.shape[1], b_ref.shape[1] // 8))):
        copy.wait()
        store_parts(first, dot(applied, b_held[:, s : s + n], (0, 0)), i, keep_ref, send_ref)


def next_kernel(
    own_ref, other_ref, a_ref, b_ref, keep_ref, send_ref, *rest
):
    left_ref = rest[0] if len(rest) == 7 else None
    a_held, b_held, split_held, left_held, a_sems, b_sems = rest[-6:]
    core = lax.axis_index("core")
    first = core == 0
    a_copies = row_copies(a_ref, a_held, a_sems)
    b_copies = col_copies(b_ref, b_held, b_sems)
    for copy in a_copies + b_copies:
        copy.start()
    gram = gram_of(first, own_ref, other_ref, split_held)
    for copy in a_copies:
        copy.wait()
    inverse = inverse_factor(gram)
    raw = dot(split_held[...], a_held[...], (1, 1))
    applied = exact(inverse, raw[:RANK] + raw[RANK:]).astype(BF16)
    for i, (copy, (s, n)) in enumerate(zip(b_copies, chunks(b_ref.shape[1], b_ref.shape[1] // 8))):
        copy.wait()
        store_parts(first, dot(applied, b_held[:, s : s + n], (1, 0)), i, keep_ref, send_ref)
    if left_ref is not None:
        lane = lax.axis_index("y") * 4 + lax.axis_index("x")
        rows = left_ref.shape[0]
        left = exact(inverse, wide_block(first, own_ref, other_ref, lane)).T
        left_held[...] = left * math.sqrt(a_ref.shape[1])
        left_ref[...] = left_held[pl.ds(pl.multiple_of(core * rows, rows), rows), :]


def last_kernel(own_ref, other_ref, left_ref, weight_ref, frozen_ref, right_ref):
    first = lax.axis_index("core") == 0
    inverse = inverse_factor(gram_of(first, own_ref, other_ref))
    width = own_ref.shape[2]
    left = left_ref[...]
    for q in range(4):
        block = wide_block(first, own_ref, other_ref, lax.axis_index("z") * 4 + q)
        right = exact(inverse, block) * math.sqrt(LANES * width)
        at = slice(q * width, (q + 1) * width)
        right_ref[:, at] = right
        frozen_ref[:, at] = weight_ref[:, at].astype(F32) - exact(left, right) / math.sqrt(RANK)


def total(keep, send):
    got = lax.ppermute(send, "core", [(0, 1), (1, 0)])
    pair = (keep + got.astype(F32)).astype(BF16)
    terms = lax.all_to_all(pair, CHIPS, 0, 0, tiled=True)
    mine = jnp.sum(terms.astype(F32), axis=0)
    copies = jnp.broadcast_to(mine[None], terms.shape)
    own = lax.all_to_all(copies, CHIPS, 0, 0, tiled=True)
    return own, lax.ppermute(own, "core", [(0, 1), (1, 0)])


def local(acts, out_grads, test_matrix, weight):
    tokens, n = acts.shape
    rows, cols = weight.shape
    parts = (LANES * GROUPS, 8, n // LANES)
    partial = (jax.ShapeDtypeStruct(parts, F32), jax.ShapeDtypeStruct(parts, BF16))
    held = [pltpu.VMEM((tokens, n), BF16)] * 2
    sems = [pltpu.SemaphoreType.DMA((len(chunks(tokens, 256)),)), pltpu.SemaphoreType.DMA((8,))]
    sketch = total(*pl.pallas_call(
        first_kernel, out_shape=partial, in_specs=[VMEM, ANY, ANY], out_specs=(VMEM, VMEM),
        scratch_shapes=[*held, *sems], compiler_params=PARAMS, name="first",
    )(test_matrix, acts, out_grads))

    def step(name, wide, a, b, *more):
        return pl.pallas_call(
            next_kernel, out_shape=(*partial, *more), in_specs=[VMEM, VMEM, ANY, ANY],
            out_specs=(VMEM,) * (2 + len(more)),
            scratch_shapes=[
                *held, pltpu.VMEM((2 * RANK, n), BF16), pltpu.VMEM((n // LANES, RANK), F32), *sems,
            ],
            compiler_params=PARAMS, name=name,
        )(*wide, a, b)

    cosketch = total(*step("second", sketch, out_grads, acts))
    power = total(*step("third", cosketch, acts, out_grads))
    *project, left = step(
        "fourth", power, out_grads, acts, jax.ShapeDtypeStruct((rows, RANK), F32)
    )
    frozen, right = pl.pallas_call(
        last_kernel,
        out_shape=(
            jax.ShapeDtypeStruct((rows, cols), F32), jax.ShapeDtypeStruct((RANK, cols), F32),
        ),
        in_specs=[VMEM] * 4, out_specs=(VMEM, VMEM), compiler_params=PARAMS, name="last",
    )(*total(*project), left, weight)
    return (frozen, left, right)


def solution(mesh):
    mesh = Mesh(mesh.devices.reshape(4, 4, 2, 4), ("y", "x", "core", "z"))
    row = ("y", "x", "core")
    tokens = P((*row, "z"), None)
    return jax.shard_map(
        local, mesh=mesh, in_specs=(tokens, tokens, P(), P(row, "z")),
        out_specs=(P(row, "z"), P(row, None), P(None, "z")), check_vma=False,
    )
```

time: 363 us -> 257 us (0.71); the launches traced: 357 us -> 256 us
  matrix products: 78 us -> 0 us
  Pallas kernels: 0 us -> 74.2 us
  other arithmetic: 50.1 us -> 5.15 us
  waiting for transfers between devices: 49.6 us -> 12.3 us
  blocking collectives: 159 us -> 141 us
  between operations: 14.3 us -> 0.71 us
  starting transfers between devices: 3.3 us -> 15.4 us
  local copies, waits for them, and re-layouts: 2.96 us -> 7.87 us
    dot_general x14 -> x0, matrix products: 77 us -> none  [the longest x4 54.9 us: product(): lax.dot_general(left, right, ((contract[:1], contract[1:]), ((), ())), pr...]
    pallas_call x0 -> x5, Pallas kernels: none -> 74.2 us  [the longest x3 53.3 us: step(): pl.pallas_call(next_kernel, out_shape=(*partial, *more), in_specs=[VMEM,...]
    another operation x20 -> x0, other arithmetic: 48.3 us -> none  [the longest x12 26.1 us: inverse_factor(): lower = jnp.linalg.cholesky(gram)]
    all_gather x4 -> x0, waiting for transfers between devices: 43.6 us -> none  [total(): return from_parts(lax.all_gather(half, 'core', axis=0, tiled=False))]
    all_to_all x4, blocking collectives: 85 us -> 67.6 us  [total(): terms = lax.all_to_all(pair, CHIPS, 0, 0, tiled=True)]
    ppermute x4 -> x8, starting transfers between devices: 2.35 us -> 15.4 us  [the longest x4 12.5 us: total(): return (own, lax.ppermute(own, 'core', [(0, 1), (1, 0)]))]
    unnamed x14 -> x18, local copies, waits for them, and re-layouts: 1.11 us -> 7.65 us
    ppermute x4 -> x8, waiting for transfers between devices: 5.9 us -> 12.3 us  [the longest x4 6.25 us: total(): got = lax.ppermute(send, 'core', [(0, 1), (1, 0)])]
  transfers between devices with their start and end apart: 8 -> 8, of which waited for: 8 -> 8; matrix products, arithmetic and copies ran while one was open for 0% -> 1% of each run, Pallas kernels for 0% -> 0%
where the time goes in v2:
time: 257 us; the launch traced here: 256 us
  blocking collectives  141 us (55%)
  Pallas kernels  74.2 us (29%)
  starting transfers between devices  15.4 us (6%)
  waiting for transfers between devices  12.3 us (5%)
  local copies, waits for them, and re-layouts  7.87 us (3%)
  other arithmetic  5.15 us (2%)
    all_to_all x4, blocking collectives, total(): own = lax.all_to_all(copies, CHIPS, 0, 0, tiled=True)  73.3 us
    all_to_all x4, blocking collectives, total(): terms = lax.all_to_all(pair, CHIPS, 0, 0, tiled=True)  67.6 us
    pallas_call x3, Pallas kernels, step(): pl.pallas_call(next_kernel, out_shape=(*partial, *more), in_specs=[VMEM,...  53.3 us
    pallas_call x1, Pallas kernels, local(): pl.pallas_call(first_kernel, out_shape=partial, in_specs=[VMEM, ANY, ANY]...  14.4 us
    ppermute x4, starting transfers between devices, total(): return (own, lax.ppermute(own, 'core', [(0, 1), (1, 0)]))  12.5 us
    unnamed x18, local copies, waits for them, and re-layouts  7.65 us
    pallas_call x1, Pallas kernels, local(): pl.pallas_call(last_kernel, out_shape=(jax.ShapeDtypeStruct((rows, cols),...  6.47 us
    ppermute x4, waiting for transfers between devices, total(): got = lax.ppermute(send, 'core', [(0, 1), (1, 0)])  6.25 us
  transfers between devices with their start and end apart: 8, of which 8 were waited for; matrix products, arithmetic and copies ran while one was open for 1% of the time, Pallas kernels for 0%

profile of v2, /device:TPU:1, one launch (start us, length us, event | category | flops | bytes accessed | tf_op | source)
XLA Modules:
  0.0 256.5 jit_solution(14507159831736448397)
XLA Ops:
  0.6 2.5 copy.7.test_ref
  3.1 14.4 %first.1 = (f32[64,8,384]{2,1,0:T(8,128)}, bf16[64,8,384]{2,1,0:T(8,128)(2,1)}) custom-call(bf16[6144,64]{1,0:T(8,128)(2,1)} %copy.7.test_ref, bf16[960,6144]{1,0:T(8,128)(2,1)} %b_ref.7, bf16[960,6144]{1,0:T(8,128)(2,1)} %a_ref.7), custom_call_target="tpu_custom_call" | custom-call | tf_op jit(solution)/shard_map/first/pallas_call | solution.py:196
  17.6 1.5 collective-permute-start
  19.1 1.6 collective-permute-done
  20.6 1.2 add_convert_fusion.3
  21.8 22.0 %all_to_all.40 = bf16[64,8,384]{2,1,0:T(8,128)(2,1)S(1)} all-to-all(bf16[64,8,384]{2,1,0:T(8,128)(2,1)S(1)} %add_convert_fusion.3), channel_id=1, replica_groups=mesh['y'=4,'x'=4,'core'=2,'z'=4] {'y','x','z'}, dimensions={0} | all-to-all | bytes 786432 | tf_op jit(solution)/shard_map/all_to_all | solution.py:182
  43.8 0.1 convert_reduce_fusion.3
  43.9 0.1 broadcast_in_dim.8
  43.9 18.3 %all_to_all.41.own_ref = f32[64,8,384]{2,1,0:T(8,128)S(1)} all-to-all(f32[64,8,384]{2,1,0:T(8,128)S(1)} %broadcast_in_dim.8), channel_id=1, replica_groups=mesh['y'=4,'x'=4,'core'=2,'z'=4] {'y','x','z'}, dimensions={0} | all-to-all | bytes 1572864 | tf_op jit(solution)/shard_map/all_to_all | solution.py:185
  62.3 3.1 %collective-permute-start.1 = (f32[64,8,384]{2,1,0:T(8,128)S(1)}, f32[64,8,384]{2,1,0:T(8,128)S(1)}, u32[]{:S(2)}, u32[]{:S(2)}) collective-permute-start(f32[64,8,384]{2,1,0:T(8,128)S(1)} %all_to_all.41.own_ref), channel_id=1, source_target_pairs={{0,4},{4,0},{1,5},{5,1},{2,6},{6,2},{3,7},{7,3},{8,12},{12,8},{9,1... | collective-permute-start | bytes 2359304 | tf_op jit(solution)/shard_map/ppermute | solution.py:186
  65.4 1.9 collective-permute-done.1.other_ref
  67.3 0.9 copy-done.5
  68.2 17.7 %second.1 = (f32[64,8,384]{2,1,0:T(8,128)}, bf16[64,8,384]{2,1,0:T(8,128)(2,1)}) custom-call(f32[64,8,384]{2,1,0:T(8,128)} %copy-done.1, f32[64,8,384]{2,1,0:T(8,128)} %copy-done.5, bf16[960,6144]{1,0:T(8,128)(2,1)} %a_ref.7, bf16[960,6144]{1,0:T(8,128)(2,1)} %b_ref.7), custom_call_target="tpu_custom_call" | custom-call | tf_op jit(solution)/shard_map/second/pallas_call | solution.py:202
  85.9 0.5 collective-permute-start.2
  86.4 1.6 collective-permute-done.2
  87.9 1.2 add_convert_fusion.2
  89.2 15.2 %all_to_all.42 = bf16[64,8,384]{2,1,0:T(8,128)(2,1)S(1)} all-to-all(bf16[64,8,384]{2,1,0:T(8,128)(2,1)S(1)} %add_convert_fusion.2), channel_id=1, replica_groups=mesh['y'=4,'x'=4,'core'=2,'z'=4] {'y','x','z'}, dimensions={0} | all-to-all | bytes 786432 | tf_op jit(solution)/shard_map/all_to_all | solution.py:182
  104.4 0.1 convert_reduce_fusion.2
  104.4 0.1 broadcast_in_dim.9
  104.5 18.3 %all_to_all.43.own_ref = f32[64,8,384]{2,1,0:T(8,128)S(1)} all-to-all(f32[64,8,384]{2,1,0:T(8,128)S(1)} %broadcast_in_dim.9), channel_id=1, replica_groups=mesh['y'=4,'x'=4,'core'=2,'z'=4] {'y','x','z'}, dimensions={0} | all-to-all | bytes 1572864 | tf_op jit(solution)/shard_map/all_to_all | solution.py:185
  122.8 3.1 %collective-permute-start.3 = (f32[64,8,384]{2,1,0:T(8,128)S(1)}, f32[64,8,384]{2,1,0:T(8,128)S(1)}, u32[]{:S(2)}, u32[]{:S(2)}) collective-permute-start(f32[64,8,384]{2,1,0:T(8,128)S(1)} %all_to_all.43.own_ref), channel_id=1, source_target_pairs={{0,4},{4,0},{1,5},{5,1},{2,6},{6,2},{3,7},{7,3},{8,12},{12,8},{9,1... | collective-permute-start | bytes 2359304 | tf_op jit(solution)/shard_map/ppermute | solution.py:186
  126.0 1.9 collective-permute-done.3.other_ref
  127.9 0.9 copy-done.6
  128.8 17.7 %third.1 = (f32[64,8,384]{2,1,0:T(8,128)}, bf16[64,8,384]{2,1,0:T(8,128)(2,1)}) custom-call(f32[64,8,384]{2,1,0:T(8,128)} %copy-done.2, f32[64,8,384]{2,1,0:T(8,128)} %copy-done.6, bf16[960,6144]{1,0:T(8,128)(2,1)} %b_ref.7, bf16[960,6144]{1,0:T(8,128)(2,1)} %a_ref.7), custom_call_target="tpu_custom_call" | custom-call | tf_op jit(solution)/shard_map/third/pallas_call | solution.py:202
  146.5 0.5 collective-permute-start.4
  147.0 1.6 collective-permute-done.4
  148.5 1.2 add_convert_fusion.1
  149.7 15.2 %all_to_all.44 = bf16[64,8,384]{2,1,0:T(8,128)(2,1)S(1)} all-to-all(bf16[64,8,384]{2,1,0:T(8,128)(2,1)S(1)} %add_convert_fusion.1), channel_id=1, replica_groups=mesh['y'=4,'x'=4,'core'=2,'z'=4] {'y','x','z'}, dimensions={0} | all-to-all | bytes 786432 | tf_op jit(solution)/shard_map/all_to_all | solution.py:182
  164.9 0.1 convert_reduce_fusion.1
  165.0 0.1 broadcast_in_dim.10
  165.1 18.3 %all_to_all.45.own_ref = f32[64,8,384]{2,1,0:T(8,128)S(1)} all-to-all(f32[64,8,384]{2,1,0:T(8,128)S(1)} %broadcast_in_dim.10), channel_id=1, replica_groups=mesh['y'=4,'x'=4,'core'=2,'z'=4] {'y','x','z'}, dimensions={0} | all-to-all | bytes 1572864 | tf_op jit(solution)/shard_map/all_to_all | solution.py:185
  183.4 3.1 %collective-permute-start.5 = (f32[64,8,384]{2,1,0:T(8,128)S(1)}, f32[64,8,384]{2,1,0:T(8,128)S(1)}, u32[]{:S(2)}, u32[]{:S(2)}) collective-permute-start(f32[64,8,384]{2,1,0:T(8,128)S(1)} %all_to_all.45.own_ref), channel_id=1, source_target_pairs={{0,4},{4,0},{1,5},{5,1},{2,6},{6,2},{3,7},{7,3},{8,12},{12,8},{9,1... | collective-permute-start | bytes 2359304 | tf_op jit(solution)/shard_map/ppermute | solution.py:186
  186.5 1.9 collective-permute-done.5.other_ref
  188.5 0.9 copy-done.4
  189.3 17.8 %fourth.1 = (f32[64,8,384]{2,1,0:T(8,128)}, bf16[64,8,384]{2,1,0:T(8,128)(2,1)}, f32[192,64]{1,0:T(8,128)}) custom-call(f32[64,8,384]{2,1,0:T(8,128)} %copy-done, f32[64,8,384]{2,1,0:T(8,128)} %copy-done.4, bf16[960,6144]{1,0:T(8,128)(2,1)} %a_ref.7, bf16[960,6144]{1,0:T(8,128)(2,1)} %b_ref.7), custom_call_target="tpu_custom_call" | custom-call | tf_op jit(solution)/shard_map/fourth/pallas_call | solution.py:202
  207.1 0.5 collective-permute-start.6
  207.6 1.6 collective-permute-done.6
  209.2 1.2 add_convert_fusion
  210.4 15.2 %all_to_all.46 = bf16[64,8,384]{2,1,0:T(8,128)(2,1)S(1)} all-to-all(bf16[64,8,384]{2,1,0:T(8,128)(2,1)S(1)} %add_convert_fusion), channel_id=1, replica_groups=mesh['y'=4,'x'=4,'core'=2,'z'=4] {'y','x','z'}, dimensions={0} | all-to-all | bytes 786432 | tf_op jit(solution)/shard_map/all_to_all | solution.py:182
  225.6 0.1 convert_reduce_fusion
  225.7 0.1 broadcast_in_dim.11
  225.7 18.3 %all_to_all.47.own_ref = f32[64,8,384]{2,1,0:T(8,128)S(1)} all-to-all(f32[64,8,384]{2,1,0:T(8,128)S(1)} %broadcast_in_dim.11), channel_id=1, replica_groups=mesh['y'=4,'x'=4,'core'=2,'z'=4] {'y','x','z'}, dimensions={0} | all-to-all | bytes 1572864 | tf_op jit(solution)/shard_map/all_to_all | solution.py:185
  244.1 3.1 %collective-permute-start.7 = (f32[64,8,384]{2,1,0:T(8,128)S(1)}, f32[64,8,384]{2,1,0:T(8,128)S(1)}, u32[]{:S(2)}, u32[]{:S(2)}) collective-permute-start(f32[64,8,384]{2,1,0:T(8,128)S(1)} %all_to_all.47.own_ref), channel_id=1, source_target_pairs={{0,4},{4,0},{1,5},{5,1},{2,6},{6,2},{3,7},{7,3},{8,12},{12,8},{9,1... | collective-permute-start | bytes 2359304 | tf_op jit(solution)/shard_map/ppermute | solution.py:186
  247.2 1.6 copy.8
  248.8 0.3 collective-permute-done.7.other_ref
  249.1 0.0 copy-done.3
  249.1 0.9 copy-done.7
  250.0 6.5 %last.1 = (f32[192,1536]{1,0:T(8,128)}, f32[64,1536]{1,0:T(8,128)}) custom-call(f32[64,8,384]{2,1,0:T(8,128)} %copy-done.3, f32[64,8,384]{2,1,0:T(8,128)} %copy-done.7, f32[192,64]{1,0:T(8,128)} %get-tuple-element.26.left_ref, bf16[192,1536]{1,0:T(8,128)(2,1)} %weight_ref.1), custom_call_target="tpu_custom_call" | custom-call | tf_op jit(solution)/shard_map/last/pallas_call | solution.py:216
  (11 shorter events, 0.0 us)
Async XLA Ops:
  17.6 3.1 %collective-permute-start = (bf16[64,8,384]{2,1,0:T(8,128)(2,1)}, bf16[64,8,384]{2,1,0:T(8,128)(2,1)S(1)}, u32[]{:S(2)}, u32[]{:S(2)}) collective-permute-start(bf16[64,8,384]{2,1,0:T(8,128)(2,1)} %get-tuple-element.15), channel_id=1, source_target_pairs={{0,4},{4,0},{1,5},{5,1},{2,6},{6,2},{3,7},{7,3},{8,12},{12,8},{9,1... | collective-permute-start | bytes 1179656 | tf_op jit(solution)/shard_map/ppermute | solution.py:180
  62.3 5.0 %copy-start.1 = (f32[64,8,384]{2,1,0:T(8,128)}, f32[64,8,384]{2,1,0:T(8,128)S(1)}, u32[]{:S(2)}) copy-start(f32[64,8,384]{2,1,0:T(8,128)S(1)} %all_to_all.41.own_ref) | copy-start | bytes 2359300
  62.3 5.0 %collective-permute-start.1 = (f32[64,8,384]{2,1,0:T(8,128)S(1)}, f32[64,8,384]{2,1,0:T(8,128)S(1)}, u32[]{:S(2)}, u32[]{:S(2)}) collective-permute-start(f32[64,8,384]{2,1,0:T(8,128)S(1)} %all_to_all.41.own_ref), channel_id=1, source_target_pairs={{0,4},{4,0},{1,5},{5,1},{2,6},{6,2},{3,7},{7,3},{8,12},{12,8},{9,1... | collective-permute-start | bytes 2359304 | tf_op jit(solution)/shard_map/ppermute | solution.py:186
  67.3 0.9 copy-start.5
  85.9 2.0 collective-permute-start.2
  122.8 5.0 %copy-start.2 = (f32[64,8,384]{2,1,0:T(8,128)}, f32[64,8,384]{2,1,0:T(8,128)S(1)}, u32[]{:S(2)}) copy-start(f32[64,8,384]{2,1,0:T(8,128)S(1)} %all_to_all.43.own_ref) | copy-start | bytes 2359300
  122.8 5.0 %collective-permute-start.3 = (f32[64,8,384]{2,1,0:T(8,128)S(1)}, f32[64,8,384]{2,1,0:T(8,128)S(1)}, u32[]{:S(2)}, u32[]{:S(2)}) collective-permute-start(f32[64,8,384]{2,1,0:T(8,128)S(1)} %all_to_all.43.own_ref), channel_id=1, source_target_pairs={{0,4},{4,0},{1,5},{5,1},{2,6},{6,2},{3,7},{7,3},{8,12},{12,8},{9,1... | collective-permute-start | bytes 2359304 | tf_op jit(solution)/shard_map/ppermute | solution.py:186
  127.9 0.9 copy-start.6
  146.5 2.0 collective-permute-start.4
  183.4 5.0 %copy-start = (f32[64,8,384]{2,1,0:T(8,128)}, f32[64,8,384]{2,1,0:T(8,128)S(1)}, u32[]{:S(2)}) copy-start(f32[64,8,384]{2,1,0:T(8,128)S(1)} %all_to_all.45.own_ref) | copy-start | bytes 2359300
  183.4 5.0 %collective-permute-start.5 = (f32[64,8,384]{2,1,0:T(8,128)S(1)}, f32[64,8,384]{2,1,0:T(8,128)S(1)}, u32[]{:S(2)}, u32[]{:S(2)}) collective-permute-start(f32[64,8,384]{2,1,0:T(8,128)S(1)} %all_to_all.45.own_ref), channel_id=1, source_target_pairs={{0,4},{4,0},{1,5},{5,1},{2,6},{6,2},{3,7},{7,3},{8,12},{12,8},{9,1... | collective-permute-start | bytes 2359304 | tf_op jit(solution)/shard_map/ppermute | solution.py:186
  188.5 0.9 copy-start.4
  207.1 2.0 collective-permute-start.6
  244.1 5.0 %copy-start.3 = (f32[64,8,384]{2,1,0:T(8,128)}, f32[64,8,384]{2,1,0:T(8,128)S(1)}, u32[]{:S(2)}) copy-start(f32[64,8,384]{2,1,0:T(8,128)S(1)} %all_to_all.47.own_ref) | copy-start | bytes 2359300
  244.1 5.0 %collective-permute-start.7 = (f32[64,8,384]{2,1,0:T(8,128)S(1)}, f32[64,8,384]{2,1,0:T(8,128)S(1)}, u32[]{:S(2)}, u32[]{:S(2)}) collective-permute-start(f32[64,8,384]{2,1,0:T(8,128)S(1)} %all_to_all.47.own_ref), channel_id=1, source_target_pairs={{0,4},{4,0},{1,5},{5,1},{2,6},{6,2},{3,7},{7,3},{8,12},{12,8},{9,1... | collective-permute-start | bytes 2359304 | tf_op jit(solution)/shard_map/ppermute | solution.py:186
  249.1 0.9 copy-start.7

commit v3 on v2

--- a/solution.py
+++ b/solution.py
@@ -12,8 +12,8 @@
 BF16 = jnp.bfloat16
 RANK = 64
 VMEM = pl.BlockSpec(memory_space=pltpu.VMEM)
-ANY = pl.BlockSpec(memory_space=pl.ANY)
-PARAMS = pltpu.CompilerParams(vmem_limit_bytes=56 * 2**20)
+HBM = pl.BlockSpec(memory_space=pltpu.HBM)
+PARAMS = pltpu.CompilerParams(vmem_limit_bytes=16 * 2**20)
 GROUPS = 4
 LANES = 16
 
@@ -70,8 +70,8 @@
 
 
 def wide_block(first, own_ref, other_ref, lane):
-    own = [own_ref[g * LANES + lane] for g in range(GROUPS)]
-    other = [other_ref[g * LANES + lane] for g in range(GROUPS)]
+    own = [own_ref[g * LANES + lane].astype(F32) for g in range(GROUPS)]
+    other = [other_ref[g * LANES + lane].astype(F32) for g in range(GROUPS)]
     low = [jnp.where(first, a, b) for a, b in zip(own, other)]
     high = [jnp.where(first, b, a) for a, b in zip(own, other)]
     return jnp.concatenate(low + high, 0)
@@ -118,56 +118,55 @@
     ]
 
 
-def first_kernel(test_ref, a_ref, b_ref, keep_ref, send_ref, a_held, b_held, a_sems, b_sems):
+def first_kernel(
+    test_ref, a_ref, b_ref, keep_ref, send_ref, a_held, b_held, test_held, a_sems, b_sems, test_sem
+):
     first = lax.axis_index("core") == 0
+    test_copy = pltpu.make_async_copy(test_ref, test_held, test_sem)
     a_copies = row_copies(a_ref, a_held, a_sems)
     b_copies = col_copies(b_ref, b_held, b_sems)
-    for copy in a_copies + b_copies:
+    a_chunks = chunks(a_ref.shape[0], 256)
+    b_chunks = chunks(b_ref.shape[1], b_ref.shape[1] // 8)
+    for copy in [test_copy, *a_copies]:
         copy.start()
-    test = test_ref[...]
+    test_copy.wait()
+    test = test_held[...]
     applied = []
-    for copy, (s, n) in zip(a_copies, chunks(a_ref.shape[0], 256)):
+    for i, (copy, (s, n)) in enumerate(zip(a_copies, a_chunks)):
         copy.wait()
-        applied.append(dot(a_held[s : s + n, :], test, (1, 0)).astype(BF16))
-    applied = jnp.concatenate(applied, 0)
-    for i, (copy, (s, n)) in enumerate(zip(b_copies, chunks(b_ref.shape[1], b_ref.shape[1] // 8))):
-        copy.wait()
-        store_parts(first, dot(applied, b_held[:, s : s + n], (0, 0)), i, keep_ref, send_ref)
-
-
-def next_kernel(
-    own_ref, other_ref, a_ref, b_ref, keep_ref, send_ref, *rest
-):
-    left_ref = rest[0] if len(rest) == 7 else None
-    a_held, b_held, split_held, left_held, a_sems, b_sems = rest[-6:]
-    core = lax.axis_index("core")
-    first = core == 0
-    a_copies = row_copies(a_ref, a_held, a_sems)
-    b_copies = col_copies(b_ref, b_held, b_sems)
-    for copy in a_copies + b_copies:
-        copy.start()
-    gram = gram_of(first, own_ref, other_ref, split_held)
-    for copy in a_copies:
-        copy.wait()
-    inverse = inverse_factor(gram)
-    raw = dot(split_held[...], a_held[...], (1, 1))
-    applied = exact(inverse, raw[:RANK] + raw[RANK:]).astype(BF16)
-    for i, (copy, (s, n)) in enumerate(zip(b_copies, chunks(b_ref.shape[1], b_ref.shape[1] // 8))):
+        for later in b_copies[2 * i : 2 * i + 2]:
+            later.start()
+        applied.append(dot(test, a_held[s : s + n, :], (1, 1)).astype(BF16))
+    applied = jnp.concatenate(applied, 1)
+    for i, (copy, (s, n)) in enumerate(zip(b_copies, b_chunks)):
         copy.wait()
         store_parts(first, dot(applied, b_held[:, s : s + n], (1, 0)), i, keep_ref, send_ref)
-    if left_ref is not None:
+
+
+def next_kernel(own_ref, other_ref, a_ref, b_ref, keep_ref, send_ref, *rest):
+    *left_ref, split_held = rest
+    first = lax.axis_index("core") == 0
+    gram = gram_of(first, own_ref, other_ref, split_held)
+    inverse = inverse_factor(gram)
+    raw = dot(split_held[...], a_ref[...], (1, 1))
+    applied = exact(inverse, raw[:RANK] + raw[RANK:]).astype(BF16)
+    for i, (s, n) in enumerate(chunks(b_ref.shape[1], b_ref.shape[1] // 8)):
+        store_parts(first, dot(applied, b_ref[:, s : s + n], (1, 0)), i, keep_ref, send_ref)
+    if left_ref:
+        (left_ref,) = left_ref
         lane = lax.axis_index("y") * 4 + lax.axis_index("x")
-        rows = left_ref.shape[0]
-        left = exact(inverse, wide_block(first, own_ref, other_ref, lane)).T
-        left_held[...] = left * math.sqrt(a_ref.shape[1])
-        left_ref[...] = left_held[pl.ds(pl.multiple_of(core * rows, rows), rows), :]
-
-
-def last_kernel(own_ref, other_ref, left_ref, weight_ref, frozen_ref, right_ref):
+        rows = left_ref.shape[1]
+        left = exact(inverse, wide_block(first, own_ref, other_ref, lane))
+        left = jnp.where(first, left[:, :rows], left[:, rows:])
+        left_ref[...] = left * math.sqrt(a_ref.shape[1])
+
+
+def last_kernel(own_ref, other_ref, left_ref, weight_ref, frozen_ref, left_out, right_ref):
     first = lax.axis_index("core") == 0
     inverse = inverse_factor(gram_of(first, own_ref, other_ref))
     width = own_ref.shape[2]
-    left = left_ref[...]
+    left_out[...] = left_ref[...]
+    left = left_ref[...].T
     for q in range(4):
         block = wide_block(first, own_ref, other_ref, lax.axis_index("z") * 4 + q)
         right = exact(inverse, block) * math.sqrt(LANES * width)
@@ -176,11 +175,19 @@
         frozen_ref[:, at] = weight_ref[:, at].astype(F32) - exact(left, right) / math.sqrt(RANK)
 
 
-def total(keep, send):
+def in_hbm(array):
+    return pltpu.with_memory_space_constraint(array, pltpu.HBM)
+
+
+def in_vmem(array):
+    return pltpu.with_memory_space_constraint(array, pltpu.VMEM)
+
+
+def total(keep, send, dtype=F32):
     got = lax.ppermute(send, "core", [(0, 1), (1, 0)])
     pair = (keep + got.astype(F32)).astype(BF16)
     terms = lax.all_to_all(pair, CHIPS, 0, 0, tiled=True)
-    mine = jnp.sum(terms.astype(F32), axis=0)
+    mine = lax.optimization_barrier(jnp.sum(terms.astype(F32), axis=0)).astype(dtype)
     copies = jnp.broadcast_to(mine[None], terms.shape)
     own = lax.all_to_all(copies, CHIPS, 0, 0, tiled=True)
     return own, lax.ppermute(own, "core", [(0, 1), (1, 0)])
@@ -191,36 +198,40 @@
     rows, cols = weight.shape
     parts = (LANES * GROUPS, 8, n // LANES)
     partial = (jax.ShapeDtypeStruct(parts, F32), jax.ShapeDtypeStruct(parts, BF16))
-    held = [pltpu.VMEM((tokens, n), BF16)] * 2
-    sems = [pltpu.SemaphoreType.DMA((len(chunks(tokens, 256)),)), pltpu.SemaphoreType.DMA((8,))]
-    sketch = total(*pl.pallas_call(
-        first_kernel, out_shape=partial, in_specs=[VMEM, ANY, ANY], out_specs=(VMEM, VMEM),
-        scratch_shapes=[*held, *sems], compiler_params=PARAMS, name="first",
-    )(test_matrix, acts, out_grads))
+    held = pltpu.VMEM((tokens, n), BF16)
+    keep, send, acts, out_grads = pl.pallas_call(
+        first_kernel, out_shape=(*partial, held, held), in_specs=[HBM] * 3,
+        out_specs=(VMEM,) * 4,
+        scratch_shapes=[
+            pltpu.VMEM((RANK, n), BF16), pltpu.SemaphoreType.DMA((len(chunks(tokens, 256)),)),
+            pltpu.SemaphoreType.DMA((8,)), pltpu.SemaphoreType.DMA(()),
+        ],
+        compiler_params=PARAMS, name="first",
+    )(in_hbm(test_matrix.T), in_hbm(acts), in_hbm(out_grads))
 
     def step(name, wide, a, b, *more):
         return pl.pallas_call(
-            next_kernel, out_shape=(*partial, *more), in_specs=[VMEM, VMEM, ANY, ANY],
+            next_kernel, out_shape=(*partial, *more), in_specs=[VMEM] * 4,
             out_specs=(VMEM,) * (2 + len(more)),
-            scratch_shapes=[
-                *held, pltpu.VMEM((2 * RANK, n), BF16), pltpu.VMEM((n // LANES, RANK), F32), *sems,
-            ],
+            scratch_shapes=[pltpu.VMEM((2 * RANK, n), BF16)],
             compiler_params=PARAMS, name=name,
-        )(*wide, a, b)
-
-    cosketch = total(*step("second", sketch, out_grads, acts))
+        )(*wide, in_vmem(a), in_vmem(b))
+
+    sketch = total(keep, send)
+    cosketch = total(*step("second", sketch, out_grads, acts), BF16)
     power = total(*step("third", cosketch, acts, out_grads))
     *project, left = step(
-        "fourth", power, out_grads, acts, jax.ShapeDtypeStruct((rows, RANK), F32)
+        "fourth", power, out_grads, acts, pltpu.VMEM((RANK, rows), F32)
     )
-    frozen, right = pl.pallas_call(
+    frozen, left, right = pl.pallas_call(
         last_kernel,
         out_shape=(
-            jax.ShapeDtypeStruct((rows, cols), F32), jax.ShapeDtypeStruct((RANK, cols), F32),
+            jax.ShapeDtypeStruct((rows, cols), F32), jax.ShapeDtypeStruct((RANK, rows), F32),
+            jax.ShapeDtypeStruct((RANK, cols), F32),
         ),
-        in_specs=[VMEM] * 4, out_specs=(VMEM, VMEM), compiler_params=PARAMS, name="last",
+        in_specs=[VMEM] * 4, out_specs=(VMEM,) * 3, compiler_params=PARAMS, name="last",
     )(*total(*project), left, weight)
-    return (frozen, left, right)
+    return (frozen, left.T, right)
 
 
 def solution(mesh):

time: 257 us -> 207 us (0.81)
  Pallas kernels: 74.2 us -> 40 us
  local copies, waits for them, and re-layouts: 7.87 us -> 0.21 us
  other arithmetic: 5.15 us -> 0.63 us
  blocking collectives: 141 us -> 137 us
    pallas_call x4, Pallas kernels: 67.7 us -> 35.1 us  [the longest x3 20.8 us: step(): pl.pallas_call(next_kernel, out_shape=(*partial, *more), in_specs=[VMEM]...]
    unnamed x18 -> x2, local copies, waits for them, and re-layouts: 7.65 us -> 0.01 us
    convert_element_type x4, other arithmetic: 4.82 us -> 0.29 us  [total(): pair = (keep + got.astype(F32)).astype(BF16)]
    all_to_all x4, blocking collectives: 73.3 us -> 69.6 us  [total(): own = lax.all_to_all(copies, CHIPS, 0, 0, tiled=True)]
  transfers between devices with their start and end apart: 8 -> 8, of which waited for: 8 -> 8; matrix products, arithmetic and copies ran while one was open for 1% -> 0% of each run, Pallas kernels for 0% -> 0%
where the time goes in v3:
time: 207 us
  blocking collectives  137 us (66%)
  Pallas kernels  40 us (19%)
  starting transfers between devices  15.4 us (7%)
  waiting for transfers between devices  12.5 us (6%)
    all_to_all x4, blocking collectives, total(): own = lax.all_to_all(copies, CHIPS, 0, 0, tiled=True)  69.6 us
    all_to_all x4, blocking collectives, total(): terms = lax.all_to_all(pair, CHIPS, 0, 0, tiled=True)  67.7 us
    pallas_call x3, Pallas kernels, step(): pl.pallas_call(next_kernel, out_shape=(*partial, *more), in_specs=[VMEM]...  20.8 us
    pallas_call x1, Pallas kernels, local(): pl.pallas_call(first_kernel, out_shape=(*partial, held, held), in_specs=[...  14.3 us
    ppermute x4, starting transfers between devices, total(): return (own, lax.ppermute(own, 'core', [(0, 1), (1, 0)]))  12.6 us
    ppermute x4, waiting for transfers between devices, total(): return (own, lax.ppermute(own, 'core', [(0, 1), (1, 0)]))  7.09 us
    ppermute x4, waiting for transfers between devices, total(): got = lax.ppermute(send, 'core', [(0, 1), (1, 0)])  5.4 us
    pallas_call x1, Pallas kernels, local(): pl.pallas_call(last_kernel, out_shape=(jax.ShapeDtypeStruct((rows, cols),...  4.93 us
  transfers between devices with their start and end apart: 8, of which 8 were waited for; matrix products, arithmetic and copies ran while one was open for 0% of the time, Pallas kernels for 0%

profile of v3, /device:TPU:1, one launch (start us, length us, event | category | flops | bytes accessed | tf_op | source)
XLA Modules:
  0.0 206.8 jit_solution(15672356848588297401)
XLA Ops:
  0.6 14.3 %first.1 = (f32[64,8,384]{2,1,0:T(8,128)S(1)}, bf16[64,8,384]{2,1,0:T(8,128)(2,1)S(1)}, bf16[960,6144]{1,0:T(8,128)(2,1)S(1)}, bf16[960,6144]{1,0:T(8,128)(2,1)S(1)}) custom-call(bf16[64,6144]{1,0:T(8,128)(2,1)} %bitcast.2, bf16[960,6144]{1,0:T(8,128)(2,1)} %a_ref.1, bf16[960,6144]{1,0:T(8,128)(2,1)} %b_ref.1), custom_call_target="tpu_custom_call" | custom-call | tf_op jit(solution)/shard_map/first/pallas_call | solution.py:202
  14.9 1.5 collective-permute-start
  16.4 1.3 collective-permute-done
  17.8 0.1 add_convert_fusion.3
  17.9 22.0 %all_to_all.40 = bf16[64,8,384]{2,1,0:T(8,128)(2,1)S(1)} all-to-all(bf16[64,8,384]{2,1,0:T(8,128)(2,1)S(1)} %add_convert_fusion.3), channel_id=1, replica_groups=mesh['y'=4,'x'=4,'core'=2,'z'=4] {'y','x','z'}, dimensions={0} | all-to-all | bytes 786432 | tf_op jit(solution)/shard_map/all_to_all | solution.py:189
  39.8 0.1 convert_reduce_fusion.3
  39.9 0.1 broadcast_in_dim.8
  40.0 18.3 %all_to_all.41.own_ref = f32[64,8,384]{2,1,0:T(8,128)S(1)} all-to-all(f32[64,8,384]{2,1,0:T(8,128)S(1)} %broadcast_in_dim.8), channel_id=1, replica_groups=mesh['y'=4,'x'=4,'core'=2,'z'=4] {'y','x','z'}, dimensions={0} | all-to-all | bytes 1572864 | tf_op jit(solution)/shard_map/all_to_all | solution.py:192
  58.3 3.1 %collective-permute-start.1 = (f32[64,8,384]{2,1,0:T(8,128)S(1)}, f32[64,8,384]{2,1,0:T(8,128)S(1)}, u32[]{:S(2)}, u32[]{:S(2)}) collective-permute-start(f32[64,8,384]{2,1,0:T(8,128)S(1)} %all_to_all.41.own_ref), channel_id=1, source_target_pairs={{0,4},{4,0},{1,5},{5,1},{2,6},{6,2},{3,7},{7,3},{8,12},{12,8},{9,1... | collective-permute-start | bytes 2359304 | tf_op jit(solution)/shard_map/ppermute | solution.py:193
  61.4 1.9 collective-permute-done.1.other_ref
  63.3 7.0 %second.1 = (f32[64,8,384]{2,1,0:T(8,128)S(1)}, bf16[64,8,384]{2,1,0:T(8,128)(2,1)S(1)}) custom-call(f32[64,8,384]{2,1,0:T(8,128)S(1)} %all_to_all.41.own_ref, f32[64,8,384]{2,1,0:T(8,128)S(1)} %collective-permute-done.1.other_ref, bf16[960,6144]{1,0:T(8,128)(2,1)S(1)} %get-tuple-element.19.a_ref.b_ref, bf16[960,6144]{1,0:T(8,128)(2,1)S(1)} %get-tuple-element.20.b_ref.a_ref), custom_call_target="tpu_custom_call" | custom-call | tf_op jit(solution)/shard_map/second/pallas_call | solution.py:213
  70.4 0.5 collective-permute-start.2
  70.8 1.4 collective-permute-done.2
  72.2 0.1 add_convert_fusion.2
  72.2 15.2 %all_to_all.42 = bf16[64,8,384]{2,1,0:T(8,128)(2,1)S(1)} all-to-all(bf16[64,8,384]{2,1,0:T(8,128)(2,1)S(1)} %add_convert_fusion.2), channel_id=1, replica_groups=mesh['y'=4,'x'=4,'core'=2,'z'=4] {'y','x','z'}, dimensions={0} | all-to-all | bytes 786432 | tf_op jit(solution)/shard_map/all_to_all | solution.py:189
  87.4 0.1 convert_reduce_fusion.2
  87.6 14.6 %all_to_all.43.own_ref = bf16[64,8,384]{2,1,0:T(8,128)(2,1)S(1)} all-to-all(bf16[64,8,384]{2,1,0:T(8,128)(2,1)S(1)} %broadcast_in_dim.9), channel_id=1, replica_groups=mesh['y'=4,'x'=4,'core'=2,'z'=4] {'y','x','z'}, dimensions={0} | all-to-all | bytes 786432 | tf_op jit(solution)/shard_map/all_to_all | solution.py:192
  102.2 3.2 %collective-permute-start.3 = (bf16[64,8,384]{2,1,0:T(8,128)(2,1)S(1)}, bf16[64,8,384]{2,1,0:T(8,128)(2,1)S(1)}, u32[]{:S(2)}, u32[]{:S(2)}) collective-permute-start(bf16[64,8,384]{2,1,0:T(8,128)(2,1)S(1)} %all_to_all.43.own_ref), channel_id=1, source_target_pairs={{0,4},{4,0},{1,5},{5,1},{2,6},{6,2},{3,7},{7,3},{8,12},{12,8},{9,1... | collective-permute-start | bytes 1179656 | tf_op jit(solution)/shard_map/ppermute | solution.py:193
  105.4 1.3 collective-permute-done.3.other_ref
  106.7 7.0 %third.1 = (f32[64,8,384]{2,1,0:T(8,128)S(1)}, bf16[64,8,384]{2,1,0:T(8,128)(2,1)S(1)}) custom-call(bf16[64,8,384]{2,1,0:T(8,128)(2,1)S(1)} %all_to_all.43.own_ref, bf16[64,8,384]{2,1,0:T(8,128)(2,1)S(1)} %collective-permute-done.3.other_ref, bf16[960,6144]{1,0:T(8,128)(2,1)S(1)} %get-tuple-element.20.b_ref.a_ref, ...), custom_call_target="tpu_custom_call" | custom-call | tf_op jit(solution)/shard_map/third/pallas_call | solution.py:213
  113.7 0.5 collective-permute-start.4
  114.2 1.3 collective-permute-done.4
  115.5 0.1 add_convert_fusion.1
  115.6 15.3 %all_to_all.44 = bf16[64,8,384]{2,1,0:T(8,128)(2,1)S(1)} all-to-all(bf16[64,8,384]{2,1,0:T(8,128)(2,1)S(1)} %add_convert_fusion.1), channel_id=1, replica_groups=mesh['y'=4,'x'=4,'core'=2,'z'=4] {'y','x','z'}, dimensions={0} | all-to-all | bytes 786432 | tf_op jit(solution)/shard_map/all_to_all | solution.py:189
  130.9 0.1 convert_reduce_fusion.1
  131.0 0.1 broadcast_in_dim.10
  131.1 18.3 %all_to_all.45.own_ref = f32[64,8,384]{2,1,0:T(8,128)S(1)} all-to-all(f32[64,8,384]{2,1,0:T(8,128)S(1)} %broadcast_in_dim.10), channel_id=1, replica_groups=mesh['y'=4,'x'=4,'core'=2,'z'=4] {'y','x','z'}, dimensions={0} | all-to-all | bytes 1572864 | tf_op jit(solution)/shard_map/all_to_all | solution.py:192
  149.4 0.0 copy-start
  149.4 3.1 %collective-permute-start.5 = (f32[64,8,384]{2,1,0:T(8,128)S(1)}, f32[64,8,384]{2,1,0:T(8,128)S(1)}, u32[]{:S(2)}, u32[]{:S(2)}) collective-permute-start(f32[64,8,384]{2,1,0:T(8,128)S(1)} %all_to_all.45.own_ref), channel_id=1, source_target_pairs={{0,4},{4,0},{1,5},{5,1},{2,6},{6,2},{3,7},{7,3},{8,12},{12,8},{9,1... | collective-permute-start | bytes 2359304 | tf_op jit(solution)/shard_map/ppermute | solution.py:193
  152.6 1.9 collective-permute-done.5.other_ref
  154.5 6.8 %fourth.1 = (f32[64,8,384]{2,1,0:T(8,128)S(1)}, bf16[64,8,384]{2,1,0:T(8,128)(2,1)S(1)}, f32[64,192]{1,0:T(8,128)S(1)}) custom-call(f32[64,8,384]{2,1,0:T(8,128)S(1)} %all_to_all.45.own_ref, f32[64,8,384]{2,1,0:T(8,128)S(1)} %collective-permute-done.5.other_ref, bf16[960,6144]{1,0:T(8,128)(2,1)S(1)} %get-tuple-element.19.a_ref.b_ref, ...), custom_call_target="tpu_custom_call" | custom-call | tf_op jit(solution)/shard_map/fourth/pallas_call | solution.py:213
  161.2 0.5 collective-permute-start.6
  161.7 1.4 collective-permute-done.6
  163.1 0.1 add_convert_fusion
  163.1 15.2 %all_to_all.46 = bf16[64,8,384]{2,1,0:T(8,128)(2,1)S(1)} all-to-all(bf16[64,8,384]{2,1,0:T(8,128)(2,1)S(1)} %add_convert_fusion), channel_id=1, replica_groups=mesh['y'=4,'x'=4,'core'=2,'z'=4] {'y','x','z'}, dimensions={0} | all-to-all | bytes 786432 | tf_op jit(solution)/shard_map/all_to_all | solution.py:189
  178.3 0.1 convert_reduce_fusion
  178.4 0.1 broadcast_in_dim.11
  178.5 18.3 %all_to_all.47.own_ref = f32[64,8,384]{2,1,0:T(8,128)S(1)} all-to-all(f32[64,8,384]{2,1,0:T(8,128)S(1)} %broadcast_in_dim.11), channel_id=1, replica_groups=mesh['y'=4,'x'=4,'core'=2,'z'=4] {'y','x','z'}, dimensions={0} | all-to-all | bytes 1572864 | tf_op jit(solution)/shard_map/all_to_all | solution.py:192
  196.8 3.1 %collective-permute-start.7 = (f32[64,8,384]{2,1,0:T(8,128)S(1)}, f32[64,8,384]{2,1,0:T(8,128)S(1)}, u32[]{:S(2)}, u32[]{:S(2)}) collective-permute-start(f32[64,8,384]{2,1,0:T(8,128)S(1)} %all_to_all.47.own_ref), channel_id=1, source_target_pairs={{0,4},{4,0},{1,5},{5,1},{2,6},{6,2},{3,7},{7,3},{8,12},{12,8},{9,1... | collective-permute-start | bytes 2359304 | tf_op jit(solution)/shard_map/ppermute | solution.py:193
  199.9 1.9 collective-permute-done.7.other_ref
  201.8 0.0 copy-done
  201.8 4.9 %last.1 = (f32[192,1536]{1,0:T(8,128)}, f32[64,192]{1,0:T(8,128)}, f32[64,1536]{1,0:T(8,128)}) custom-call(f32[64,8,384]{2,1,0:T(8,128)S(1)} %all_to_all.47.own_ref, f32[64,8,384]{2,1,0:T(8,128)S(1)} %collective-permute-done.7.other_ref, f32[64,192]{1,0:T(8,128)S(1)} %get-tuple-element.27.left_ref, bf16[192,1536]{1,0:T(8,128)(2,1)S(1)} %copy-done), custom_call_target="tpu_custom_call" | custom-call | tf_op jit(solution)/shard_map/last/pallas_call | solution.py:226
  (1 shorter events, 0.0 us)
Async XLA Ops:
  14.9 2.9 %collective-permute-start = (bf16[64,8,384]{2,1,0:T(8,128)(2,1)S(1)}, bf16[64,8,384]{2,1,0:T(8,128)(2,1)S(1)}, u32[]{:S(2)}, u32[]{:S(2)}) collective-permute-start(bf16[64,8,384]{2,1,0:T(8,128)(2,1)S(1)} %get-tuple-element.18), channel_id=1, source_target_pairs={{0,4},{4,0},{1,5},{5,1},{2,6},{6,2},{3,7},{7,3},{8,12},{12,8},{9,1... | collective-permute-start | bytes 1179656 | tf_op jit(solution)/shard_map/ppermute | solution.py:187
  58.3 5.0 %collective-permute-start.1 = (f32[64,8,384]{2,1,0:T(8,128)S(1)}, f32[64,8,384]{2,1,0:T(8,128)S(1)}, u32[]{:S(2)}, u32[]{:S(2)}) collective-permute-start(f32[64,8,384]{2,1,0:T(8,128)S(1)} %all_to_all.41.own_ref), channel_id=1, source_target_pairs={{0,4},{4,0},{1,5},{5,1},{2,6},{6,2},{3,7},{7,3},{8,12},{12,8},{9,1... | collective-permute-start | bytes 2359304 | tf_op jit(solution)/shard_map/ppermute | solution.py:193
  70.4 1.8 collective-permute-start.2
  102.2 4.6 %collective-permute-start.3 = (bf16[64,8,384]{2,1,0:T(8,128)(2,1)S(1)}, bf16[64,8,384]{2,1,0:T(8,128)(2,1)S(1)}, u32[]{:S(2)}, u32[]{:S(2)}) collective-permute-start(bf16[64,8,384]{2,1,0:T(8,128)(2,1)S(1)} %all_to_all.43.own_ref), channel_id=1, source_target_pairs={{0,4},{4,0},{1,5},{5,1},{2,6},{6,2},{3,7},{7,3},{8,12},{12,8},{9,1... | collective-permute-start | bytes 1179656 | tf_op jit(solution)/shard_map/ppermute | solution.py:193
  113.7 1.8 collective-permute-start.4
  149.4 52.4 %copy-start = (bf16[192,1536]{1,0:T(8,128)(2,1)S(1)}, bf16[192,1536]{1,0:T(8,128)(2,1)}, u32[]{:S(2)}) copy-start(bf16[192,1536]{1,0:T(8,128)(2,1)} %weight_ref.1) | copy-start | bytes 1769476
  149.4 5.0 %collective-permute-start.5 = (f32[64,8,384]{2,1,0:T(8,128)S(1)}, f32[64,8,384]{2,1,0:T(8,128)S(1)}, u32[]{:S(2)}, u32[]{:S(2)}) collective-permute-start(f32[64,8,384]{2,1,0:T(8,128)S(1)} %all_to_all.45.own_ref), channel_id=1, source_target_pairs={{0,4},{4,0},{1,5},{5,1},{2,6},{6,2},{3,7},{7,3},{8,12},{12,8},{9,1... | collective-permute-start | bytes 2359304 | tf_op jit(solution)/shard_map/ppermute | solution.py:193
  161.2 1.8 collective-permute-start.6
  196.8 5.0 %collective-permute-start.7 = (f32[64,8,384]{2,1,0:T(8,128)S(1)}, f32[64,8,384]{2,1,0:T(8,128)S(1)}, u32[]{:S(2)}, u32[]{:S(2)}) collective-permute-start(f32[64,8,384]{2,1,0:T(8,128)S(1)} %all_to_all.47.own_ref), channel_id=1, source_target_pairs={{0,4},{4,0},{1,5},{5,1},{2,6},{6,2},{3,7},{7,3},{8,12},{12,8},{9,1... | collective-permute-start | bytes 2359304 | tf_op jit(solution)/shard_map/ppermute | solution.py:193

commit v4 on v3

v4 whole, which is shorter than its diff:
```python
import math

import jax
import jax.numpy as jnp
from jax import lax
from jax.experimental import pallas as pl
from jax.experimental.pallas import tpu as pltpu
from jax.sharding import Mesh, PartitionSpec as P

CHIPS = ("y", "x", "z")
F32 = jnp.float32
BF16 = jnp.bfloat16
RANK = 64
VMEM = pl.BlockSpec(memory_space=pltpu.VMEM)
HBM = pl.BlockSpec(memory_space=pltpu.HBM)
PARAMS = pltpu.CompilerParams(vmem_limit_bytes=16 * 2**20)
AHEAD = 3
GROUPS = 8
LANES = 8


def dot(left, right, contract):
    dims = (((contract[0],), (contract[1],)), ((), ()))
    return lax.dot_general(left, right, dims, preferred_element_type=F32)


def split(value):
    high = value.astype(BF16)
    return high, (value - high.astype(F32)).astype(BF16)


def exact(left, right):
    left_high, left_low = split(left)
    right_high, right_low = split(right)
    return dot(
        jnp.concatenate([left_high, left_high, left_low], 1),
        jnp.concatenate([right_high, right_low, right_high], 0),
        (1, 0),
    )


def inverse_factor(gram):
    shape = (RANK, RANK)
    eye = lax.broadcasted_iota(jnp.int32, shape, 0) == lax.broadcasted_iota(jnp.int32, shape, 1)
    both = jnp.concatenate([gram, eye.astype(F32)], 1)
    work = [both[8 * i : 8 * i + 8] for i in range(8)]
    tile = (8, 2 * RANK)
    sub = lax.broadcasted_iota(jnp.int32, tile, 0)
    done = []
    for p in range(8):
        cols = {
            i: [jnp.broadcast_to(work[i][:, k : k + 1], tile) for k in range(8 * p, 8 * p + 8)]
            for i in range(p, 8)
        }
        pivots = jnp.zeros(tile, F32)
        for j in range(8):
            pivot = jnp.broadcast_to(cols[p][j][j : j + 1], tile)
            inverse = 1.0 / pivot
            pivots = jnp.where(sub == j, pivot, pivots)
            row = jnp.broadcast_to(work[p][j : j + 1], tile)
            ahead = {q: jnp.broadcast_to(cols[p][q][j : j + 1], tile) for q in range(j + 1, 8)}
            for i in range(p, 8):
                scale = cols[i][j] * inverse
                if i == p:
                    scale = jnp.where(sub > j, scale, 0.0)
                work[i] = work[i] - scale * row
                for q in range(j + 1, 8):
                    cols[i][q] = cols[i][q] - scale * ahead[q]
        done.append(work[p] * lax.rsqrt(pivots))
    return jnp.concatenate(done, 0)[:, RANK:]


def wide_block(first, own_ref, other_ref, half, lane):
    swap = first if half == 0 else jnp.logical_not(first)
    own = jnp.concatenate([own_ref[g * LANES + lane].astype(F32) for g in range(GROUPS)], 0)
    other = jnp.concatenate([other_ref[g * LANES + lane].astype(F32) for g in range(GROUPS)], 0)
    return jnp.where(swap, own, other)


def gram_of(first, own_ref, other_ref, split_ref=None):
    width = own_ref.shape[2]
    gram = jnp.zeros((2 * RANK, 2 * RANK), F32)
    for half in range(2):
        for lane in range(LANES):
            block = wide_block(first, own_ref, other_ref, half, lane)
            terms = jnp.concatenate(split(block), 0)
            if split_ref is not None:
                start = (half * LANES + lane) * width
                split_ref[:, start : start + width] = terms
            gram = gram + dot(terms, terms, (1, 1))
    cross = gram[:RANK, RANK:] + gram[RANK:, :RANK]
    return gram[:RANK, :RANK] + (gram[RANK:, RANK:] + cross)


def half_columns(ref, half, index):
    size = ref.shape[1] // 8
    return pl.ds(pl.multiple_of(half * (4 * size) + index * size, size), size)


def store_parts(part, index, ref):
    width = ref.shape[2]
    for h in range(2):
        for g in range(GROUPS):
            value = part[8 * g : 8 * g + 8, h * width : (h + 1) * width]
            ref[g * LANES + 2 * index + h] = value.astype(ref.dtype)


def chunks(total, size):
    return [(s, min(size, total - s)) for s in range(0, total, size)]


def first_kernel(
    test_ref, a_ref, b_ref, send_ref, applied_ref, a_held, b_held, test_held, a_sems, b_sems, test_sem
):
    core = lax.axis_index("core")
    places = [half_columns(b_ref, half, i) for half in (1 - core, core) for i in range(4)]
    rows = chunks(a_ref.shape[0], 128)
    test_copy = pltpu.make_async_copy(test_ref, test_held, test_sem)
    copies = [
        pltpu.make_async_copy(a_ref.at[pl.ds(s, n), :], a_held.at[pl.ds(s, n), :], a_sems.at[i])
        for i, (s, n) in enumerate(rows)
    ] + [
        pltpu.make_async_copy(b_ref.at[:, at], b_held.at[:, at], b_sems.at[i])
        for i, at in enumerate(places)
    ]
    test_copy.start()
    for copy in copies[:AHEAD]:
        copy.start()
    test_copy.wait()

    def arrive(i):
        copies[i].wait()
        if i + AHEAD < len(copies):
            copies[i + AHEAD].start()

    test = test_held[...]
    applied = []
    for i in range(0, len(rows), 2):
        start = rows[i][0]
        stop = sum(rows[min(i + 1, len(rows) - 1)])
        for j in range(i, min(i + 2, len(rows))):
            arrive(j)
        applied.append(dot(test, a_held[start:stop, :], (1, 1)).astype(BF16))
    applied = jnp.concatenate(applied, 1)
    applied_ref[...] = applied
    for i, at in enumerate(places):
        arrive(len(rows) + i)
        if i < 4:
            store_parts(dot(applied, b_held[:, at], (1, 0)), i, send_ref)


def next_kernel(own_ref, other_ref, a_ref, b_ref, send_ref, applied_ref, inverse_ref, split_held):
    core = lax.axis_index("core")
    gram = gram_of(core == 0, own_ref, other_ref, split_held)
    inverse = inverse_factor(gram)
    inverse_ref[...] = inverse
    raw = dot(split_held[...], a_ref[...], (1, 1))
    applied = exact(inverse, raw[:RANK] + raw[RANK:]).astype(BF16)
    applied_ref[...] = applied
    for i in range(4):
        part = dot(applied, b_ref[:, half_columns(b_ref, 1 - core, i)], (1, 0))
        store_parts(part, i, send_ref)


def keep_kernel(applied_ref, b_ref, keep_ref):
    core = lax.axis_index("core")
    for i in range(4):
        part = dot(applied_ref[...], b_ref[:, half_columns(b_ref, core, i)], (1, 0))
        store_parts(part, i, keep_ref)


def left_kernel(own_ref, other_ref, inverse_ref, left_ref):
    core = lax.axis_index("core")
    block = 4 * lax.axis_index("y") + lax.axis_index("x")
    half, lane = block // LANES, lax.rem(block, LANES)
    wide = jnp.where(
        half == 0,
        wide_block(core == 0, own_ref, other_ref, 0, lane),
        wide_block(core == 0, own_ref, other_ref, 1, lane),
    )
    left = exact(inverse_ref[...], wide)
    rows = left_ref.shape[1]
    left = jnp.where(core == 0, left[:, :rows], left[:, rows:])
    left_ref[...] = left * math.sqrt(2 * LANES * own_ref.shape[2])


def last_kernel(own_ref, other_ref, left_ref, weight_ref, frozen_ref, left_out, right_ref):
    first = lax.axis_index("core") == 0
    inverse = inverse_factor(gram_of(first, own_ref, other_ref))
    width = own_ref.shape[2]
    left_out[...] = left_ref[...]
    left = left_ref[...].T
    half = lax.axis_index("z") // 2
    for q in range(4):
        lane = lax.rem(lax.axis_index("z"), 2) * 4 + q
        block = jnp.where(
            half == 0,
            wide_block(first, own_ref, other_ref, 0, lane),
            wide_block(first, own_ref, other_ref, 1, lane),
        )
        right = exact(inverse, block) * math.sqrt(2 * LANES * width)
        at = slice(q * width, (q + 1) * width)
        right_ref[:, at] = right
        frozen_ref[:, at] = weight_ref[:, at].astype(F32) - exact(left, right) / math.sqrt(RANK)


def in_hbm(array):
    return pltpu.with_memory_space_constraint(array, pltpu.HBM)


def in_vmem(array):
    return pltpu.with_memory_space_constraint(array, pltpu.VMEM)


def total(send, applied, b, dtype=F32):
    keep = pl.pallas_call(
        keep_kernel, out_shape=jax.ShapeDtypeStruct(send.shape, F32), in_specs=[VMEM] * 2,
        out_specs=VMEM, compiler_params=PARAMS, name="keep",
    )(applied, in_vmem(b))
    got = lax.ppermute(send, "core", [(0, 1), (1, 0)])
    pair = (keep + got.astype(F32)).astype(BF16)
    terms = lax.all_to_all(pair, CHIPS, 0, 0, tiled=True)
    mine = lax.optimization_barrier(jnp.sum(terms.astype(F32), axis=0)).astype(dtype)
    copies = jnp.broadcast_to(mine[None], terms.shape)
    own = lax.all_to_all(copies, CHIPS, 0, 0, tiled=True)
    return own, lax.ppermute(own, "core", [(0, 1), (1, 0)])


def local(acts, out_grads, test_matrix, weight):
    tokens, n = acts.shape
    rows, cols = weight.shape
    partial = (
        jax.ShapeDtypeStruct((LANES * GROUPS, 8, n // (2 * LANES)), BF16),
        jax.ShapeDtypeStruct((RANK, tokens), BF16),
    )
    held = pltpu.VMEM((tokens, n), BF16)
    *made, acts, out_grads = pl.pallas_call(
        first_kernel, out_shape=(*partial, held, held), in_specs=[HBM] * 3,
        out_specs=(VMEM,) * 4,
        scratch_shapes=[
            pltpu.VMEM((RANK, n), BF16), pltpu.SemaphoreType.DMA((len(chunks(tokens, 128)),)),
            pltpu.SemaphoreType.DMA((8,)), pltpu.SemaphoreType.DMA(()),
        ],
        compiler_params=PARAMS, name="first",
    )(in_hbm(test_matrix.T), in_hbm(acts), in_hbm(out_grads))

    def step(wide, a, b):
        return pl.pallas_call(
            next_kernel, out_shape=(*partial, jax.ShapeDtypeStruct((RANK, RANK), F32)),
            in_specs=[VMEM] * 4, out_specs=(VMEM,) * 3,
            scratch_shapes=[pltpu.VMEM((2 * RANK, n), BF16)], compiler_params=PARAMS, name="step",
        )(*wide, in_vmem(a), in_vmem(b))

    sketch = total(*made, out_grads)
    *made, _ = step(sketch, out_grads, acts)
    cosketch = total(*made, acts, BF16)
    *made, _ = step(cosketch, acts, out_grads)
    power = total(*made, out_grads)
    *made, inverse = step(power, out_grads, acts)
    left = pl.pallas_call(
        left_kernel, out_shape=pltpu.VMEM((RANK, rows), F32), in_specs=[VMEM] * 3, out_specs=VMEM,
        compiler_params=PARAMS, name="left",
    )(*power, inverse)
    frozen, left, right = pl.pallas_call(
        last_kernel,
        out_shape=(
            jax.ShapeDtypeStruct((rows, cols), F32), jax.ShapeDtypeStruct((RANK, rows), F32),
            jax.ShapeDtypeStruct((RANK, cols), F32),
        ),
        in_specs=[VMEM] * 4, out_specs=(VMEM,) * 3, compiler_params=PARAMS, name="last",
    )(*total(*made, acts), left, weight)
    return (frozen, left.T, right)


def solution(mesh):
    mesh = Mesh(mesh.devices.reshape(4, 4, 2, 4), ("y", "x", "core", "z"))
    row = ("y", "x", "core")
    tokens = P((*row, "z"), None)
    return jax.shard_map(
        local, mesh=mesh, in_specs=(tokens, tokens, P(), P(row, "z")),
        out_specs=(P(row, "z"), P(row, None), P(None, "z")), check_vma=False,
    )
```

time: 207 us -> 203 us (0.981)
  waiting for transfers between devices: 12.5 us -> 7.65 us
    ppermute x4, waiting for transfers between devices: 5.4 us -> 0.83 us  [total(): got = lax.ppermute(send, 'core', [(0, 1), (1, 0)])]
    pallas_call x3 -> x8, Pallas kernels: 20.8 us -> 22.8 us  [the longest x3 18 us: step(): pl.pallas_call(next_kernel, out_shape=(*partial, jax.ShapeDtypeStruct((RA...]
  transfers between devices with their start and end apart: 8 -> 8, of which waited for: 8 -> 8; matrix products, arithmetic and copies ran while one was open for 0% -> 0% of each run, Pallas kernels for 0% -> 2%
where the time goes in v4:
time: 203 us
  blocking collectives  137 us (67%)
  Pallas kernels  40.5 us (20%)
  starting transfers between devices  15.6 us (8%)
  waiting for transfers between devices  7.65 us (4%)
    all_to_all x4, blocking collectives, total(): own = lax.all_to_all(copies, CHIPS, 0, 0, tiled=True)  69.6 us
    all_to_all x4, blocking collectives, total(): terms = lax.all_to_all(pair, CHIPS, 0, 0, tiled=True)  67.7 us
    pallas_call x3, Pallas kernels, step(): pl.pallas_call(next_kernel, out_shape=(*partial, jax.ShapeDtypeStruct((RA...  18 us
    pallas_call x1, Pallas kernels, local(): pl.pallas_call(first_kernel, out_shape=(*partial, held, held), in_specs=[...  12.7 us
    ppermute x4, starting transfers between devices, total(): return (own, lax.ppermute(own, 'core', [(0, 1), (1, 0)]))  12.6 us
    ppermute x4, waiting for transfers between devices, total(): return (own, lax.ppermute(own, 'core', [(0, 1), (1, 0)]))  6.81 us
    pallas_call x1, Pallas kernels, local(): pl.pallas_call(last_kernel, out_shape=(jax.ShapeDtypeStruct((rows, cols),...  4.92 us
    pallas_call x4, Pallas kernels, total(): pl.pallas_call(keep_kernel, out_shape=jax.ShapeDtypeStruct(send.shape, F3...  4.54 us
  transfers between devices with their start and end apart: 8, of which 8 were waited for; matrix products, arithmetic and copies ran while one was open for 0% of the time, Pallas kernels for 2%

profile of v4, /device:TPU:1, one launch (start us, length us, event | category | flops | bytes accessed | tf_op | source)
XLA Modules:
  0.0 202.6 jit_solution(10983639773834929958)
XLA Ops:
  0.6 12.7 %first.1 = (bf16[64,8,384]{2,1,0:T(8,128)(2,1)S(1)}, bf16[64,960]{1,0:T(8,128)(2,1)S(1)}, bf16[960,6144]{1,0:T(8,128)(2,1)S(1)}, bf16[960,6144]{1,0:T(8,128)(2,1)S(1)}) custom-call(bf16[64,6144]{1,0:T(8,128)(2,1)} %bitcast.2, bf16[960,6144]{1,0:T(8,128)(2,1)} %a_ref.1, bf16[960,6144]{1,0:T(8,128)(2,1)} %b_ref.1), custom_call_target="tpu_custom_call" | custom-call | tf_op jit(solution)/shard_map/first/pallas_call | solution.py:237
  13.3 1.5 collective-permute-start
  14.8 1.1 keep.4
  16.0 0.2 collective-permute-done
  16.2 0.1 add_convert_fusion.3
  16.3 22.0 %all_to_all.40 = bf16[64,8,384]{2,1,0:T(8,128)(2,1)S(1)} all-to-all(bf16[64,8,384]{2,1,0:T(8,128)(2,1)S(1)} %add_convert_fusion.3), channel_id=1, replica_groups=mesh['y'=4,'x'=4,'core'=2,'z'=4] {'y','x','z'}, dimensions={0} | all-to-all | bytes 786432 | tf_op jit(solution)/shard_map/all_to_all | solution.py:222
  38.2 0.1 convert_reduce_fusion.3
  38.3 0.1 broadcast_in_dim.8
  38.4 18.3 %all_to_all.41.own_ref = f32[64,8,384]{2,1,0:T(8,128)S(1)} all-to-all(f32[64,8,384]{2,1,0:T(8,128)S(1)} %broadcast_in_dim.8), channel_id=1, replica_groups=mesh['y'=4,'x'=4,'core'=2,'z'=4] {'y','x','z'}, dimensions={0} | all-to-all | bytes 1572864 | tf_op jit(solution)/shard_map/all_to_all | solution.py:225
  56.7 3.1 %collective-permute-start.1 = (f32[64,8,384]{2,1,0:T(8,128)S(1)}, f32[64,8,384]{2,1,0:T(8,128)S(1)}, u32[]{:S(2)}, u32[]{:S(2)}) collective-permute-start(f32[64,8,384]{2,1,0:T(8,128)S(1)} %all_to_all.41.own_ref), channel_id=1, source_target_pairs={{0,4},{4,0},{1,5},{5,1},{2,6},{6,2},{3,7},{7,3},{8,12},{12,8},{9,1... | collective-permute-start | bytes 2359304 | tf_op jit(solution)/shard_map/ppermute | solution.py:226
  59.8 1.9 collective-permute-done.1.other_ref
  61.7 6.0 %step.3 = (bf16[64,8,384]{2,1,0:T(8,128)(2,1)S(1)}, bf16[64,960]{1,0:T(8,128)(2,1)S(1)}, f32[64,64]{1,0:T(8,128)}) custom-call(f32[64,8,384]{2,1,0:T(8,128)S(1)} %all_to_all.41.own_ref, f32[64,8,384]{2,1,0:T(8,128)S(1)} %collective-permute-done.1.other_ref, bf16[960,6144]{1,0:T(8,128)(2,1)S(1)} %get-tuple-element.18.b_ref.a_ref, ...), custom_call_target="tpu_custom_call" | custom-call | tf_op jit(solution)/shard_map/step/pallas_call | solution.py:248
  67.7 0.6 collective-permute-start.2
  68.4 1.1 keep.5
  69.5 0.2 collective-permute-done.2
  69.7 0.1 add_convert_fusion.2
  69.8 15.2 %all_to_all.42 = bf16[64,8,384]{2,1,0:T(8,128)(2,1)S(1)} all-to-all(bf16[64,8,384]{2,1,0:T(8,128)(2,1)S(1)} %add_convert_fusion.2), channel_id=1, replica_groups=mesh['y'=4,'x'=4,'core'=2,'z'=4] {'y','x','z'}, dimensions={0} | all-to-all | bytes 786432 | tf_op jit(solution)/shard_map/all_to_all | solution.py:222
  85.0 0.1 convert_reduce_fusion.2
  85.1 14.6 %all_to_all.43.own_ref = bf16[64,8,384]{2,1,0:T(8,128)(2,1)S(1)} all-to-all(bf16[64,8,384]{2,1,0:T(8,128)(2,1)S(1)} %broadcast_in_dim.9), channel_id=1, replica_groups=mesh['y'=4,'x'=4,'core'=2,'z'=4] {'y','x','z'}, dimensions={0} | all-to-all | bytes 786432 | tf_op jit(solution)/shard_map/all_to_all | solution.py:225
  99.7 3.2 %collective-permute-start.3 = (bf16[64,8,384]{2,1,0:T(8,128)(2,1)S(1)}, bf16[64,8,384]{2,1,0:T(8,128)(2,1)S(1)}, u32[]{:S(2)}, u32[]{:S(2)}) collective-permute-start(bf16[64,8,384]{2,1,0:T(8,128)(2,1)S(1)} %all_to_all.43.own_ref), channel_id=1, source_target_pairs={{0,4},{4,0},{1,5},{5,1},{2,6},{6,2},{3,7},{7,3},{8,12},{12,8},{9,1... | collective-permute-start | bytes 1179656 | tf_op jit(solution)/shard_map/ppermute | solution.py:226
  102.9 1.3 collective-permute-done.3.other_ref
  104.3 6.0 %step.4 = (bf16[64,8,384]{2,1,0:T(8,128)(2,1)S(1)}, bf16[64,960]{1,0:T(8,128)(2,1)S(1)}, f32[64,64]{1,0:T(8,128)}) custom-call(bf16[64,8,384]{2,1,0:T(8,128)(2,1)S(1)} %all_to_all.43.own_ref, bf16[64,8,384]{2,1,0:T(8,128)(2,1)S(1)} %collective-permute-done.3.other_ref, bf16[960,6144]{1,0:T(8,128)(2,1)S(1)} %get-tuple-element.20.b_ref.a_ref, ...), custom_call_target="tpu_custom_call" | custom-call | tf_op jit(solution)/shard_map/step/pallas_call | solution.py:248
  110.3 0.5 collective-permute-start.4
  110.8 1.1 keep.6
  111.9 0.2 collective-permute-done.4
  112.1 0.1 add_convert_fusion.1
  112.2 15.3 %all_to_all.44 = bf16[64,8,384]{2,1,0:T(8,128)(2,1)S(1)} all-to-all(bf16[64,8,384]{2,1,0:T(8,128)(2,1)S(1)} %add_convert_fusion.1), channel_id=1, replica_groups=mesh['y'=4,'x'=4,'core'=2,'z'=4] {'y','x','z'}, dimensions={0} | all-to-all | bytes 786432 | tf_op jit(solution)/shard_map/all_to_all | solution.py:222
  127.5 0.1 convert_reduce_fusion.1
  127.6 0.1 broadcast_in_dim.10
  127.7 18.3 %all_to_all.45.own_ref = f32[64,8,384]{2,1,0:T(8,128)S(1)} all-to-all(f32[64,8,384]{2,1,0:T(8,128)S(1)} %broadcast_in_dim.10), channel_id=1, replica_groups=mesh['y'=4,'x'=4,'core'=2,'z'=4] {'y','x','z'}, dimensions={0} | all-to-all | bytes 1572864 | tf_op jit(solution)/shard_map/all_to_all | solution.py:225
  146.0 3.1 %collective-permute-start.5 = (f32[64,8,384]{2,1,0:T(8,128)S(1)}, f32[64,8,384]{2,1,0:T(8,128)S(1)}, u32[]{:S(2)}, u32[]{:S(2)}) collective-permute-start(f32[64,8,384]{2,1,0:T(8,128)S(1)} %all_to_all.45.own_ref), channel_id=1, source_target_pairs={{0,4},{4,0},{1,5},{5,1},{2,6},{6,2},{3,7},{7,3},{8,12},{12,8},{9,1... | collective-permute-start | bytes 2359304 | tf_op jit(solution)/shard_map/ppermute | solution.py:226
  149.1 1.9 collective-permute-done.5.other_ref
  151.1 6.0 %step.5 = (bf16[64,8,384]{2,1,0:T(8,128)(2,1)S(1)}, bf16[64,960]{1,0:T(8,128)(2,1)S(1)}, f32[64,64]{1,0:T(8,128)S(1)}) custom-call(f32[64,8,384]{2,1,0:T(8,128)S(1)} %all_to_all.45.own_ref, f32[64,8,384]{2,1,0:T(8,128)S(1)} %collective-permute-done.5.other_ref, bf16[960,6144]{1,0:T(8,128)(2,1)S(1)} %get-tuple-element.18.b_ref.a_ref, ...), custom_call_target="tpu_custom_call" | custom-call | tf_op jit(solution)/shard_map/step/pallas_call | solution.py:248
  157.1 0.0 copy-start
  157.1 0.5 collective-permute-start.6
  157.5 1.1 keep.7
  158.7 0.2 collective-permute-done.6
  158.9 0.1 add_convert_fusion
  159.0 15.2 %all_to_all.46 = bf16[64,8,384]{2,1,0:T(8,128)(2,1)S(1)} all-to-all(bf16[64,8,384]{2,1,0:T(8,128)(2,1)S(1)} %add_convert_fusion), channel_id=1, replica_groups=mesh['y'=4,'x'=4,'core'=2,'z'=4] {'y','x','z'}, dimensions={0} | all-to-all | bytes 786432 | tf_op jit(solution)/shard_map/all_to_all | solution.py:222
  174.2 0.1 convert_reduce_fusion
  174.3 0.1 broadcast_in_dim.11
  174.3 18.3 %all_to_all.47.own_ref = f32[64,8,384]{2,1,0:T(8,128)S(1)} all-to-all(f32[64,8,384]{2,1,0:T(8,128)S(1)} %broadcast_in_dim.11), channel_id=1, replica_groups=mesh['y'=4,'x'=4,'core'=2,'z'=4] {'y','x','z'}, dimensions={0} | all-to-all | bytes 1572864 | tf_op jit(solution)/shard_map/all_to_all | solution.py:225
  192.6 3.1 %collective-permute-start.7 = (f32[64,8,384]{2,1,0:T(8,128)S(1)}, f32[64,8,384]{2,1,0:T(8,128)S(1)}, u32[]{:S(2)}, u32[]{:S(2)}) collective-permute-start(f32[64,8,384]{2,1,0:T(8,128)S(1)} %all_to_all.47.own_ref), channel_id=1, source_target_pairs={{0,4},{4,0},{1,5},{5,1},{2,6},{6,2},{3,7},{7,3},{8,12},{12,8},{9,1... | collective-permute-start | bytes 2359304 | tf_op jit(solution)/shard_map/ppermute | solution.py:226
  195.8 0.3 left.1.left_ref
  196.0 1.6 collective-permute-done.7.other_ref
  197.7 0.0 copy-done
  197.7 4.9 %last.1 = (f32[192,1536]{1,0:T(8,128)}, f32[64,192]{1,0:T(8,128)}, f32[64,1536]{1,0:T(8,128)}) custom-call(f32[64,8,384]{2,1,0:T(8,128)S(1)} %all_to_all.47.own_ref, f32[64,8,384]{2,1,0:T(8,128)S(1)} %collective-permute-done.7.other_ref, f32[64,192]{1,0:T(8,128)S(1)} %left.1.left_ref, bf16[192,1536]{1,0:T(8,128)(2,1)S(1)} %copy-done), custom_call_target="tpu_custom_call" | custom-call | tf_op jit(solution)/shard_map/last/pallas_call | solution.py:264
  (1 shorter events, 0.0 us)
Async XLA Ops:
  13.3 2.9 %collective-permute-start = (bf16[64,8,384]{2,1,0:T(8,128)(2,1)S(1)}, bf16[64,8,384]{2,1,0:T(8,128)(2,1)S(1)}, u32[]{:S(2)}, u32[]{:S(2)}) collective-permute-start(bf16[64,8,384]{2,1,0:T(8,128)(2,1)S(1)} %get-tuple-element.19), channel_id=1, source_target_pairs={{0,4},{4,0},{1,5},{5,1},{2,6},{6,2},{3,7},{7,3},{8,12},{12,8},{9,1... | collective-permute-start | bytes 1179656 | tf_op jit(solution)/shard_map/ppermute | solution.py:220
  56.7 5.0 %collective-permute-start.1 = (f32[64,8,384]{2,1,0:T(8,128)S(1)}, f32[64,8,384]{2,1,0:T(8,128)S(1)}, u32[]{:S(2)}, u32[]{:S(2)}) collective-permute-start(f32[64,8,384]{2,1,0:T(8,128)S(1)} %all_to_all.41.own_ref), channel_id=1, source_target_pairs={{0,4},{4,0},{1,5},{5,1},{2,6},{6,2},{3,7},{7,3},{8,12},{12,8},{9,1... | collective-permute-start | bytes 2359304 | tf_op jit(solution)/shard_map/ppermute | solution.py:226
  67.7 2.0 collective-permute-start.2
  99.7 4.6 %collective-permute-start.3 = (bf16[64,8,384]{2,1,0:T(8,128)(2,1)S(1)}, bf16[64,8,384]{2,1,0:T(8,128)(2,1)S(1)}, u32[]{:S(2)}, u32[]{:S(2)}) collective-permute-start(bf16[64,8,384]{2,1,0:T(8,128)(2,1)S(1)} %all_to_all.43.own_ref), channel_id=1, source_target_pairs={{0,4},{4,0},{1,5},{5,1},{2,6},{6,2},{3,7},{7,3},{8,12},{12,8},{9,1... | collective-permute-start | bytes 1179656 | tf_op jit(solution)/shard_map/ppermute | solution.py:226
  110.3 1.8 collective-permute-start.4
  146.0 5.0 %collective-permute-start.5 = (f32[64,8,384]{2,1,0:T(8,128)S(1)}, f32[64,8,384]{2,1,0:T(8,128)S(1)}, u32[]{:S(2)}, u32[]{:S(2)}) collective-permute-start(f32[64,8,384]{2,1,0:T(8,128)S(1)} %all_to_all.45.own_ref), channel_id=1, source_target_pairs={{0,4},{4,0},{1,5},{5,1},{2,6},{6,2},{3,7},{7,3},{8,12},{12,8},{9,1... | collective-permute-start | bytes 2359304 | tf_op jit(solution)/shard_map/ppermute | solution.py:226
  157.1 40.6 %copy-start = (bf16[192,1536]{1,0:T(8,128)(2,1)S(1)}, bf16[192,1536]{1,0:T(8,128)(2,1)}, u32[]{:S(2)}) copy-start(bf16[192,1536]{1,0:T(8,128)(2,1)} %weight_ref.1) | copy-start | bytes 1769476
  157.1 1.8 collective-permute-start.6
  192.6 5.0 %collective-permute-start.7 = (f32[64,8,384]{2,1,0:T(8,128)S(1)}, f32[64,8,384]{2,1,0:T(8,128)S(1)}, u32[]{:S(2)}, u32[]{:S(2)}) collective-permute-start(f32[64,8,384]{2,1,0:T(8,128)S(1)} %all_to_all.47.own_ref), channel_id=1, source_target_pairs={{0,4},{4,0},{1,5},{5,1},{2,6},{6,2},{3,7},{7,3},{8,12},{12,8},{9,1... | collective-permute-start | bytes 2359304 | tf_op jit(solution)/shard_map/ppermute | solution.py:226

commit v5 on v4

--- a/solution.py
+++ b/solution.py
@@ -14,7 +14,6 @@
 VMEM = pl.BlockSpec(memory_space=pltpu.VMEM)
 HBM = pl.BlockSpec(memory_space=pltpu.HBM)
 PARAMS = pltpu.CompilerParams(vmem_limit_bytes=16 * 2**20)
-AHEAD = 3
 GROUPS = 8
 LANES = 8
 
@@ -77,19 +76,27 @@
     return jnp.where(swap, own, other)
 
 
-def gram_of(first, own_ref, other_ref, split_ref=None):
-    width = own_ref.shape[2]
+def half_gram(ref, split_ref=None):
+    width = ref.shape[2]
     gram = jnp.zeros((2 * RANK, 2 * RANK), F32)
-    for half in range(2):
-        for lane in range(LANES):
-            block = wide_block(first, own_ref, other_ref, half, lane)
-            terms = jnp.concatenate(split(block), 0)
-            if split_ref is not None:
-                start = (half * LANES + lane) * width
-                split_ref[:, start : start + width] = terms
-            gram = gram + dot(terms, terms, (1, 1))
+    for lane in range(LANES):
+        block = jnp.concatenate([ref[g * LANES + lane].astype(F32) for g in range(GROUPS)], 0)
+        terms = jnp.concatenate(split(block), 0)
+        if split_ref is not None:
+            split_ref[:, lane * width : (lane + 1) * width] = terms
+        gram = gram + dot(terms, terms, (1, 1))
+    return gram
+
+
+def whole_gram(gram):
     cross = gram[:RANK, RANK:] + gram[RANK:, :RANK]
     return gram[:RANK, :RANK] + (gram[RANK:, RANK:] + cross)
+
+
+def half_product(terms, ref, half):
+    size = ref.shape[1] // 2
+    raw = dot(terms, ref[:, pl.ds(pl.multiple_of(half * size, size), size)], (1, 1))
+    return raw[:RANK] + raw[RANK:]
 
 
 def half_columns(ref, half, index):
@@ -114,51 +121,56 @@
 ):
     core = lax.axis_index("core")
     places = [half_columns(b_ref, half, i) for half in (1 - core, core) for i in range(4)]
-    rows = chunks(a_ref.shape[0], 128)
+    rows = chunks(a_ref.shape[0], 256)
     test_copy = pltpu.make_async_copy(test_ref, test_held, test_sem)
-    copies = [
+    a_copies = [
         pltpu.make_async_copy(a_ref.at[pl.ds(s, n), :], a_held.at[pl.ds(s, n), :], a_sems.at[i])
         for i, (s, n) in enumerate(rows)
-    ] + [
+    ]
+    b_copies = [
         pltpu.make_async_copy(b_ref.at[:, at], b_held.at[:, at], b_sems.at[i])
         for i, at in enumerate(places)
     ]
-    test_copy.start()
-    for copy in copies[:AHEAD]:
+    for copy in [test_copy, *a_copies]:
         copy.start()
     test_copy.wait()
-
-    def arrive(i):
-        copies[i].wait()
-        if i + AHEAD < len(copies):
-            copies[i + AHEAD].start()
-
     test = test_held[...]
     applied = []
-    for i in range(0, len(rows), 2):
-        start = rows[i][0]
-        stop = sum(rows[min(i + 1, len(rows) - 1)])
-        for j in range(i, min(i + 2, len(rows))):
-            arrive(j)
-        applied.append(dot(test, a_held[start:stop, :], (1, 1)).astype(BF16))
+    for i, (copy, (s, n)) in enumerate(zip(a_copies, rows)):
+        copy.wait()
+        for later in b_copies[4 * i : 4 * i + 4]:
+            later.start()
+        applied.append(dot(test, a_held[s : s + n, :], (1, 1)).astype(BF16))
     applied = jnp.concatenate(applied, 1)
     applied_ref[...] = applied
-    for i, at in enumerate(places):
-        arrive(len(rows) + i)
-        if i < 4:
-            store_parts(dot(applied, b_held[:, at], (1, 0)), i, send_ref)
-
-
-def next_kernel(own_ref, other_ref, a_ref, b_ref, send_ref, applied_ref, inverse_ref, split_held):
-    core = lax.axis_index("core")
-    gram = gram_of(core == 0, own_ref, other_ref, split_held)
-    inverse = inverse_factor(gram)
+    for copy in b_copies[:4]:
+        copy.wait()
+    for i in range(4):
+        store_parts(dot(applied, b_held[:, places[i]], (1, 0)), i, send_ref)
+    for copy in b_copies[4:]:
+        copy.wait()
+
+
+def own_kernel(own_ref, a_ref, gram_ref, raw_ref, split_held):
+    gram_ref[...] = half_gram(own_ref, split_held)
+    raw_ref[...] = half_product(split_held[...], a_ref, lax.axis_index("core"))
+
+
+def own_gram_kernel(own_ref, gram_ref):
+    gram_ref[...] = half_gram(own_ref)
+
+
+def next_kernel(
+    other_ref, gram_ref, raw_ref, a_ref, b_ref, send_ref, applied_ref, inverse_ref, split_held
+):
+    other = 1 - lax.axis_index("core")
+    inverse = inverse_factor(whole_gram(gram_ref[...] + half_gram(other_ref, split_held)))
     inverse_ref[...] = inverse
-    raw = dot(split_held[...], a_ref[...], (1, 1))
-    applied = exact(inverse, raw[:RANK] + raw[RANK:]).astype(BF16)
+    raw = raw_ref[...] + half_product(split_held[...], a_ref, other)
+    applied = exact(inverse, raw).astype(BF16)
     applied_ref[...] = applied
     for i in range(4):
-        part = dot(applied, b_ref[:, half_columns(b_ref, 1 - core, i)], (1, 0))
+        part = dot(applied, b_ref[:, half_columns(b_ref, other, i)], (1, 0))
         store_parts(part, i, send_ref)
 
 
@@ -184,9 +196,11 @@
     left_ref[...] = left * math.sqrt(2 * LANES * own_ref.shape[2])
 
 
-def last_kernel(own_ref, other_ref, left_ref, weight_ref, frozen_ref, left_out, right_ref):
+def last_kernel(
+    own_ref, other_ref, gram_ref, left_ref, weight_ref, frozen_ref, left_out, right_ref
+):
     first = lax.axis_index("core") == 0
-    inverse = inverse_factor(gram_of(first, own_ref, other_ref))
+    inverse = inverse_factor(whole_gram(gram_ref[...] + half_gram(other_ref)))
     width = own_ref.shape[2]
     left_out[...] = left_ref[...]
     left = left_ref[...].T
@@ -238,18 +252,27 @@
         first_kernel, out_shape=(*partial, held, held), in_specs=[HBM] * 3,
         out_specs=(VMEM,) * 4,
         scratch_shapes=[
-            pltpu.VMEM((RANK, n), BF16), pltpu.SemaphoreType.DMA((len(chunks(tokens, 128)),)),
+            pltpu.VMEM((RANK, n), BF16), pltpu.SemaphoreType.DMA((len(chunks(tokens, 256)),)),
             pltpu.SemaphoreType.DMA((8,)), pltpu.SemaphoreType.DMA(()),
         ],
         compiler_params=PARAMS, name="first",
     )(in_hbm(test_matrix.T), in_hbm(acts), in_hbm(out_grads))
 
+    gram = jax.ShapeDtypeStruct((2 * RANK, 2 * RANK), F32)
+
     def step(wide, a, b):
+        own, other = wide
+        raw = jax.ShapeDtypeStruct((RANK, tokens), F32)
+        terms = pltpu.VMEM((2 * RANK, n // 2), BF16)
+        sums = pl.pallas_call(
+            own_kernel, out_shape=(gram, raw), in_specs=[VMEM] * 2, out_specs=(VMEM,) * 2,
+            scratch_shapes=[terms], compiler_params=PARAMS, name="own",
+        )(own, in_vmem(a))
         return pl.pallas_call(
             next_kernel, out_shape=(*partial, jax.ShapeDtypeStruct((RANK, RANK), F32)),
-            in_specs=[VMEM] * 4, out_specs=(VMEM,) * 3,
-            scratch_shapes=[pltpu.VMEM((2 * RANK, n), BF16)], compiler_params=PARAMS, name="step",
-        )(*wide, in_vmem(a), in_vmem(b))
+            in_specs=[VMEM] * 5, out_specs=(VMEM,) * 3, scratch_shapes=[terms],
+            compiler_params=PARAMS, name="step",
+        )(other, *sums, in_vmem(a), in_vmem(b))
 
     sketch = total(*made, out_grads)
     *made, _ = step(sketch, out_grads, acts)
@@ -261,14 +284,19 @@
         left_kernel, out_shape=pltpu.VMEM((RANK, rows), F32), in_specs=[VMEM] * 3, out_specs=VMEM,
         compiler_params=PARAMS, name="left",
     )(*power, inverse)
+    own, other = total(*made, acts)
+    own_gram = pl.pallas_call(
+        own_gram_kernel, out_shape=gram, in_specs=[VMEM], out_specs=VMEM, compiler_params=PARAMS,
+        name="own_gram",
+    )(own)
     frozen, left, right = pl.pallas_call(
         last_kernel,
         out_shape=(
             jax.ShapeDtypeStruct((rows, cols), F32), jax.ShapeDtypeStruct((RANK, rows), F32),
             jax.ShapeDtypeStruct((RANK, cols), F32),
         ),
-        in_specs=[VMEM] * 4, out_specs=(VMEM,) * 3, compiler_params=PARAMS, name="last",
-    )(*total(*made, acts), left, weight)
+        in_specs=[VMEM] * 5, out_specs=(VMEM,) * 3, compiler_params=PARAMS, name="last",
+    )(own, other, own_gram, left, weight)
     return (frozen, left.T, right)
 
 

time: 203 us -> 199 us (0.980)
  waiting for transfers between devices: 7.65 us -> 3.02 us
    pallas_call x0 -> x4, Pallas kernels: none -> 7.32 us  [the longest x3 6.85 us: step(): pl.pallas_call(own_kernel, out_shape=(gram, raw), in_specs=[VMEM] * 2, ou...]
    ppermute x4, waiting for transfers between devices: 6.81 us -> 1.18 us  [total(): return (own, lax.ppermute(own, 'core', [(0, 1), (1, 0)]))]
    pallas_call x3, Pallas kernels: 18 us -> 12.4 us  [step(): pl.pallas_call(next_kernel, out_shape=(*partial, jax.ShapeDtypeStruct((RA...]
  transfers between devices with their start and end apart: 8 -> 8, of which waited for: 8 -> 5; matrix products, arithmetic and copies ran while one was open for 0% -> 0% of each run, Pallas kernels for 2% -> 6%
where the time goes in v5:
time: 199 us; the launch traced here: 198 us
  blocking collectives  138 us (69%)
  Pallas kernels  41.3 us (21%)
  starting transfers between devices  14.2 us (7%)
  waiting for transfers between devices  3.02 us (2%)
    all_to_all x4, blocking collectives, total(): own = lax.all_to_all(copies, CHIPS, 0, 0, tiled=True)  69.8 us
    all_to_all x4, blocking collectives, total(): terms = lax.all_to_all(pair, CHIPS, 0, 0, tiled=True)  68.4 us
    pallas_call x3, Pallas kernels, step(): pl.pallas_call(next_kernel, out_shape=(*partial, jax.ShapeDtypeStruct((RA...  12.4 us
    ppermute x4, starting transfers between devices, total(): return (own, lax.ppermute(own, 'core', [(0, 1), (1, 0)]))  12.2 us
    pallas_call x1, Pallas kernels, local(): pl.pallas_call(first_kernel, out_shape=(*partial, held, held), in_specs=[...  12 us
    pallas_call x3, Pallas kernels, step(): pl.pallas_call(own_kernel, out_shape=(gram, raw), in_specs=[VMEM] * 2, ou...  6.85 us
    pallas_call x4, Pallas kernels, total(): pl.pallas_call(keep_kernel, out_shape=jax.ShapeDtypeStruct(send.shape, F3...  4.61 us
    pallas_call x1, Pallas kernels, local(): pl.pallas_call(last_kernel, out_shape=(jax.ShapeDtypeStruct((rows, cols),...  4.6 us
  transfers between devices with their start and end apart: 8, of which 5 were waited for; matrix products, arithmetic and copies ran while one was open for 0% of the time, Pallas kernels for 6%

profile of v5, /device:TPU:1, one launch (start us, length us, event | category | flops | bytes accessed | tf_op | source)
XLA Modules:
  0.0 198.2 jit_solution(10313929666934320193)
XLA Ops:
  0.6 12.0 %first.1 = (bf16[64,8,384]{2,1,0:T(8,128)(2,1)S(1)}, bf16[64,960]{1,0:T(8,128)(2,1)S(1)}, bf16[960,6144]{1,0:T(8,128)(2,1)S(1)}, bf16[960,6144]{1,0:T(8,128)(2,1)S(1)}) custom-call(bf16[64,6144]{1,0:T(8,128)(2,1)} %bitcast.2, bf16[960,6144]{1,0:T(8,128)(2,1)} %a_ref.1, bf16[960,6144]{1,0:T(8,128)(2,1)} %b_ref.1), custom_call_target="tpu_custom_call" | custom-call | tf_op jit(solution)/shard_map/first/pallas_call | solution.py:251
  12.7 1.5 collective-permute-start
  14.2 1.1 keep.4
  15.3 0.2 collective-permute-done
  15.5 0.1 add_convert_fusion.3
  15.6 22.0 %all_to_all.40 = bf16[64,8,384]{2,1,0:T(8,128)(2,1)S(1)} all-to-all(bf16[64,8,384]{2,1,0:T(8,128)(2,1)S(1)} %add_convert_fusion.3), channel_id=1, replica_groups=mesh['y'=4,'x'=4,'core'=2,'z'=4] {'y','x','z'}, dimensions={0} | all-to-all | bytes 786432 | tf_op jit(solution)/shard_map/all_to_all | solution.py:236
  37.6 0.1 convert_reduce_fusion.3
  37.7 0.1 broadcast_in_dim.8
  37.7 18.3 %all_to_all.41.own_ref = f32[64,8,384]{2,1,0:T(8,128)S(1)} all-to-all(f32[64,8,384]{2,1,0:T(8,128)S(1)} %broadcast_in_dim.8), channel_id=1, replica_groups=mesh['y'=4,'x'=4,'core'=2,'z'=4] {'y','x','z'}, dimensions={0} | all-to-all | bytes 1572864 | tf_op jit(solution)/shard_map/all_to_all | solution.py:239
  56.0 3.1 %collective-permute-start.1 = (f32[64,8,384]{2,1,0:T(8,128)S(1)}, f32[64,8,384]{2,1,0:T(8,128)S(1)}, u32[]{:S(2)}, u32[]{:S(2)}) collective-permute-start(f32[64,8,384]{2,1,0:T(8,128)S(1)} %all_to_all.41.own_ref), channel_id=1, source_target_pairs={{0,4},{4,0},{1,5},{5,1},{2,6},{6,2},{3,7},{7,3},{8,12},{12,8},{9,1... | collective-permute-start | bytes 2359304 | tf_op jit(solution)/shard_map/ppermute | solution.py:240
  59.2 2.3 %own.3 = (f32[128,128]{1,0:T(8,128)S(1)}, f32[64,960]{1,0:T(8,128)S(1)}) custom-call(f32[64,8,384]{2,1,0:T(8,128)S(1)} %all_to_all.41.own_ref, bf16[960,6144]{1,0:T(8,128)(2,1)S(1)} %get-tuple-element.24.b_ref.a_ref), custom_call_target="tpu_custom_call" | custom-call | tf_op jit(solution)/shard_map/own/pallas_call | solution.py:267
  61.5 0.0 collective-permute-done.1.other_ref
  61.5 4.1 %step.3 = (bf16[64,8,384]{2,1,0:T(8,128)(2,1)S(1)}, bf16[64,960]{1,0:T(8,128)(2,1)S(1)}, f32[64,64]{1,0:T(8,128)}) custom-call(f32[64,8,384]{2,1,0:T(8,128)S(1)} %collective-permute-done.1.other_ref, f32[128,128]{1,0:T(8,128)S(1)} %get-tuple-element.26.gram_ref, f32[64,960]{1,0:T(8,128)S(1)} %get-tuple-element.27.raw_ref, ...), custom_call_target="tpu_custom_call" | custom-call | tf_op jit(solution)/shard_map/step/pallas_call | solution.py:271
  65.6 0.3 collective-permute-start.2
  65.9 1.2 keep.5
  67.1 0.5 collective-permute-done.2
  67.6 0.1 add_convert_fusion.2
  67.7 15.4 %all_to_all.42 = bf16[64,8,384]{2,1,0:T(8,128)(2,1)S(1)} all-to-all(bf16[64,8,384]{2,1,0:T(8,128)(2,1)S(1)} %add_convert_fusion.2), channel_id=1, replica_groups=mesh['y'=4,'x'=4,'core'=2,'z'=4] {'y','x','z'}, dimensions={0} | all-to-all | bytes 786432 | tf_op jit(solution)/shard_map/all_to_all | solution.py:236
  83.1 0.1 convert_reduce_fusion.2
  83.2 14.7 %all_to_all.43.own_ref = bf16[64,8,384]{2,1,0:T(8,128)(2,1)S(1)} all-to-all(bf16[64,8,384]{2,1,0:T(8,128)(2,1)S(1)} %broadcast_in_dim.9), channel_id=1, replica_groups=mesh['y'=4,'x'=4,'core'=2,'z'=4] {'y','x','z'}, dimensions={0} | all-to-all | bytes 786432 | tf_op jit(solution)/shard_map/all_to_all | solution.py:239
  97.9 2.9 %collective-permute-start.3 = (bf16[64,8,384]{2,1,0:T(8,128)(2,1)S(1)}, bf16[64,8,384]{2,1,0:T(8,128)(2,1)S(1)}, u32[]{:S(2)}, u32[]{:S(2)}) collective-permute-start(bf16[64,8,384]{2,1,0:T(8,128)(2,1)S(1)} %all_to_all.43.own_ref), channel_id=1, source_target_pairs={{0,4},{4,0},{1,5},{5,1},{2,6},{6,2},{3,7},{7,3},{8,12},{12,8},{9,1... | collective-permute-start | bytes 1179656 | tf_op jit(solution)/shard_map/ppermute | solution.py:240
  100.8 2.3 %own.4 = (f32[128,128]{1,0:T(8,128)S(1)}, f32[64,960]{1,0:T(8,128)S(1)}) custom-call(bf16[64,8,384]{2,1,0:T(8,128)(2,1)S(1)} %all_to_all.43.own_ref, bf16[960,6144]{1,0:T(8,128)(2,1)S(1)} %get-tuple-element.28.b_ref.a_ref), custom_call_target="tpu_custom_call" | custom-call | tf_op jit(solution)/shard_map/own/pallas_call | solution.py:267
  103.1 0.0 collective-permute-done.3.other_ref
  103.1 4.1 %step.4 = (bf16[64,8,384]{2,1,0:T(8,128)(2,1)S(1)}, bf16[64,960]{1,0:T(8,128)(2,1)S(1)}, f32[64,64]{1,0:T(8,128)}) custom-call(bf16[64,8,384]{2,1,0:T(8,128)(2,1)S(1)} %collective-permute-done.3.other_ref, f32[128,128]{1,0:T(8,128)S(1)} %get-tuple-element.31.gram_ref, f32[64,960]{1,0:T(8,128)S(1)} %get-tuple-element.32.raw_ref, ...), custom_call_target="tpu_custom_call" | custom-call | tf_op jit(solution)/shard_map/step/pallas_call | solution.py:271
  107.3 0.1 collective-permute-start.4
  107.3 1.1 keep.6
  108.5 0.6 collective-permute-done.4
  109.1 0.1 add_convert_fusion.1
  109.1 15.6 %all_to_all.44 = bf16[64,8,384]{2,1,0:T(8,128)(2,1)S(1)} all-to-all(bf16[64,8,384]{2,1,0:T(8,128)(2,1)S(1)} %add_convert_fusion.1), channel_id=1, replica_groups=mesh['y'=4,'x'=4,'core'=2,'z'=4] {'y','x','z'}, dimensions={0} | all-to-all | bytes 786432 | tf_op jit(solution)/shard_map/all_to_all | solution.py:236
  124.7 0.1 convert_reduce_fusion.1
  124.8 0.1 broadcast_in_dim.10
  124.8 18.4 %all_to_all.45.own_ref = f32[64,8,384]{2,1,0:T(8,128)S(1)} all-to-all(f32[64,8,384]{2,1,0:T(8,128)S(1)} %broadcast_in_dim.10), channel_id=1, replica_groups=mesh['y'=4,'x'=4,'core'=2,'z'=4] {'y','x','z'}, dimensions={0} | all-to-all | bytes 1572864 | tf_op jit(solution)/shard_map/all_to_all | solution.py:239
  143.2 3.1 %collective-permute-start.5 = (f32[64,8,384]{2,1,0:T(8,128)S(1)}, f32[64,8,384]{2,1,0:T(8,128)S(1)}, u32[]{:S(2)}, u32[]{:S(2)}) collective-permute-start(f32[64,8,384]{2,1,0:T(8,128)S(1)} %all_to_all.45.own_ref), channel_id=1, source_target_pairs={{0,4},{4,0},{1,5},{5,1},{2,6},{6,2},{3,7},{7,3},{8,12},{12,8},{9,1... | collective-permute-start | bytes 2359304 | tf_op jit(solution)/shard_map/ppermute | solution.py:240
  146.3 2.3 %own.5 = (f32[128,128]{1,0:T(8,128)S(1)}, f32[64,960]{1,0:T(8,128)S(1)}) custom-call(f32[64,8,384]{2,1,0:T(8,128)S(1)} %all_to_all.45.own_ref, bf16[960,6144]{1,0:T(8,128)(2,1)S(1)} %get-tuple-element.24.b_ref.a_ref), custom_call_target="tpu_custom_call" | custom-call | tf_op jit(solution)/shard_map/own/pallas_call | solution.py:267
  148.6 4.1 %step.5 = (bf16[64,8,384]{2,1,0:T(8,128)(2,1)S(1)}, bf16[64,960]{1,0:T(8,128)(2,1)S(1)}, f32[64,64]{1,0:T(8,128)S(1)}) custom-call(f32[64,8,384]{2,1,0:T(8,128)S(1)} %collective-permute-done.5.other_ref, f32[128,128]{1,0:T(8,128)S(1)} %get-tuple-element.35.gram_ref, f32[64,960]{1,0:T(8,128)S(1)} %get-tuple-element.36.raw_ref, ...), custom_call_target="tpu_custom_call" | custom-call | tf_op jit(solution)/shard_map/step/pallas_call | solution.py:271
  152.8 0.1 collective-permute-start.6
  152.9 1.1 keep.7
  154.0 0.6 collective-permute-done.6
  154.6 0.1 add_convert_fusion
  154.7 15.4 %all_to_all.46 = bf16[64,8,384]{2,1,0:T(8,128)(2,1)S(1)} all-to-all(bf16[64,8,384]{2,1,0:T(8,128)(2,1)S(1)} %add_convert_fusion), channel_id=1, replica_groups=mesh['y'=4,'x'=4,'core'=2,'z'=4] {'y','x','z'}, dimensions={0} | all-to-all | bytes 786432 | tf_op jit(solution)/shard_map/all_to_all | solution.py:236
  170.1 0.1 convert_reduce_fusion
  170.2 0.1 broadcast_in_dim.11
  170.2 18.4 %all_to_all.47.own_ref = f32[64,8,384]{2,1,0:T(8,128)S(1)} all-to-all(f32[64,8,384]{2,1,0:T(8,128)S(1)} %broadcast_in_dim.11), channel_id=1, replica_groups=mesh['y'=4,'x'=4,'core'=2,'z'=4] {'y','x','z'}, dimensions={0} | all-to-all | bytes 1572864 | tf_op jit(solution)/shard_map/all_to_all | solution.py:239
  188.6 3.1 %collective-permute-start.7 = (f32[64,8,384]{2,1,0:T(8,128)S(1)}, f32[64,8,384]{2,1,0:T(8,128)S(1)}, u32[]{:S(2)}, u32[]{:S(2)}) collective-permute-start(f32[64,8,384]{2,1,0:T(8,128)S(1)} %all_to_all.47.own_ref), channel_id=1, source_target_pairs={{0,4},{4,0},{1,5},{5,1},{2,6},{6,2},{3,7},{7,3},{8,12},{12,8},{9,1... | collective-permute-start | bytes 2359304 | tf_op jit(solution)/shard_map/ppermute | solution.py:240
  191.7 0.3 left.1.left_ref
  192.0 0.5 own_gram.1.gram_ref
  192.5 1.2 collective-permute-done.7.other_ref
  193.6 4.6 %last.1 = (f32[192,1536]{1,0:T(8,128)}, f32[64,192]{1,0:T(8,128)}, f32[64,1536]{1,0:T(8,128)}) custom-call(f32[64,8,384]{2,1,0:T(8,128)S(1)} %all_to_all.47.own_ref, f32[64,8,384]{2,1,0:T(8,128)S(1)} %collective-permute-done.7.other_ref, f32[128,128]{1,0:T(8,128)S(1)} %own_gram.1.gram_ref, f32[64,192]{1,0:T(8,128)S(1)} %left.1.left_ref, ...), custom_call_target="tpu_custom_call" | custom-call | tf_op jit(solution)/shard_map/last/pallas_call | solution.py:292
  (4 shorter events, 0.0 us)
Async XLA Ops:
  12.7 2.9 %collective-permute-start = (bf16[64,8,384]{2,1,0:T(8,128)(2,1)S(1)}, bf16[64,8,384]{2,1,0:T(8,128)(2,1)S(1)}, u32[]{:S(2)}, u32[]{:S(2)}) collective-permute-start(bf16[64,8,384]{2,1,0:T(8,128)(2,1)S(1)} %get-tuple-element.25), channel_id=1, source_target_pairs={{0,4},{4,0},{1,5},{5,1},{2,6},{6,2},{3,7},{7,3},{8,12},{12,8},{9,1... | collective-permute-start | bytes 1179656 | tf_op jit(solution)/shard_map/ppermute | solution.py:234
  56.0 5.4 %collective-permute-start.1 = (f32[64,8,384]{2,1,0:T(8,128)S(1)}, f32[64,8,384]{2,1,0:T(8,128)S(1)}, u32[]{:S(2)}, u32[]{:S(2)}) collective-permute-start(f32[64,8,384]{2,1,0:T(8,128)S(1)} %all_to_all.41.own_ref), channel_id=1, source_target_pairs={{0,4},{4,0},{1,5},{5,1},{2,6},{6,2},{3,7},{7,3},{8,12},{12,8},{9,1... | collective-permute-start | bytes 2359304 | tf_op jit(solution)/shard_map/ppermute | solution.py:240
  65.6 2.0 %collective-permute-start.2 = (bf16[64,8,384]{2,1,0:T(8,128)(2,1)S(1)}, bf16[64,8,384]{2,1,0:T(8,128)(2,1)S(1)}, u32[]{:S(2)}, u32[]{:S(2)}) collective-permute-start(bf16[64,8,384]{2,1,0:T(8,128)(2,1)S(1)} %get-tuple-element.30), channel_id=1, source_target_pairs={{0,4},{4,0},{1,5},{5,1},{2,6},{6,2},{3,7},{7,3},{8,12},{12,8},{9,1... | collective-permute-start | bytes 1179656 | tf_op jit(solution)/shard_map/ppermute | solution.py:234
  97.9 5.2 %collective-permute-start.3 = (bf16[64,8,384]{2,1,0:T(8,128)(2,1)S(1)}, bf16[64,8,384]{2,1,0:T(8,128)(2,1)S(1)}, u32[]{:S(2)}, u32[]{:S(2)}) collective-permute-start(bf16[64,8,384]{2,1,0:T(8,128)(2,1)S(1)} %all_to_all.43.own_ref), channel_id=1, source_target_pairs={{0,4},{4,0},{1,5},{5,1},{2,6},{6,2},{3,7},{7,3},{8,12},{12,8},{9,1... | collective-permute-start | bytes 1179656 | tf_op jit(solution)/shard_map/ppermute | solution.py:240
  107.3 1.8 collective-permute-start.4
  143.2 5.4 %collective-permute-start.5 = (f32[64,8,384]{2,1,0:T(8,128)S(1)}, f32[64,8,384]{2,1,0:T(8,128)S(1)}, u32[]{:S(2)}, u32[]{:S(2)}) collective-permute-start(f32[64,8,384]{2,1,0:T(8,128)S(1)} %all_to_all.45.own_ref), channel_id=1, source_target_pairs={{0,4},{4,0},{1,5},{5,1},{2,6},{6,2},{3,7},{7,3},{8,12},{12,8},{9,1... | collective-permute-start | bytes 2359304 | tf_op jit(solution)/shard_map/ppermute | solution.py:240
  152.8 40.9 %copy-start = (bf16[192,1536]{1,0:T(8,128)(2,1)S(1)}, bf16[192,1536]{1,0:T(8,128)(2,1)}, u32[]{:S(2)}) copy-start(bf16[192,1536]{1,0:T(8,128)(2,1)} %weight_ref.1) | copy-start | bytes 1769476
  152.8 1.8 collective-permute-start.6
  188.6 5.0 %collective-permute-start.7 = (f32[64,8,384]{2,1,0:T(8,128)S(1)}, f32[64,8,384]{2,1,0:T(8,128)S(1)}, u32[]{:S(2)}, u32[]{:S(2)}) collective-permute-start(f32[64,8,384]{2,1,0:T(8,128)S(1)} %all_to_all.47.own_ref), channel_id=1, source_target_pairs={{0,4},{4,0},{1,5},{5,1},{2,6},{6,2},{3,7},{7,3},{8,12},{12,8},{9,1... | collective-permute-start | bytes 2359304 | tf_op jit(solution)/shard_map/ppermute | solution.py:240

commit v6 on v5

--- a/solution.py
+++ b/solution.py
@@ -7,7 +7,7 @@
 from jax.experimental.pallas import tpu as pltpu
 from jax.sharding import Mesh, PartitionSpec as P
 
-CHIPS = ("y", "x", "z")
+CHIPS = ("yh", "z", "yl", "x")
 F32 = jnp.float32
 BF16 = jnp.bfloat16
 RANK = 64
@@ -16,6 +16,8 @@
 PARAMS = pltpu.CompilerParams(vmem_limit_bytes=16 * 2**20)
 GROUPS = 8
 LANES = 8
+TILES = 3
+TILE = 128
 
 
 def dot(left, right, contract):
@@ -69,21 +71,27 @@
     return jnp.concatenate(done, 0)[:, RANK:]
 
 
-def wide_block(first, own_ref, other_ref, half, lane):
-    swap = first if half == 0 else jnp.logical_not(first)
-    own = jnp.concatenate([own_ref[g * LANES + lane].astype(F32) for g in range(GROUPS)], 0)
-    other = jnp.concatenate([other_ref[g * LANES + lane].astype(F32) for g in range(GROUPS)], 0)
-    return jnp.where(swap, own, other)
+def lane_of(block, tile):
+    return (block - tile + LANES) % LANES
+
+
+def block_of(ref, block, low=False):
+    def tile(g, j):
+        at = g * LANES + lane_of(block, j)
+        value = ref[at, j].astype(F32)
+        return value + ref[at, TILES].astype(F32) if low else value
+
+    rows = [jnp.concatenate([tile(g, j) for j in range(TILES)], 1) for g in range(GROUPS)]
+    return jnp.concatenate(rows, 0)
 
 
 def half_gram(ref, split_ref=None):
-    width = ref.shape[2]
+    width = TILES * TILE
     gram = jnp.zeros((2 * RANK, 2 * RANK), F32)
-    for lane in range(LANES):
-        block = jnp.concatenate([ref[g * LANES + lane].astype(F32) for g in range(GROUPS)], 0)
-        terms = jnp.concatenate(split(block), 0)
+    for block in range(LANES):
+        terms = jnp.concatenate(split(block_of(ref, block)), 0)
         if split_ref is not None:
-            split_ref[:, lane * width : (lane + 1) * width] = terms
+            split_ref[:, block * width : (block + 1) * width] = terms
         gram = gram + dot(terms, terms, (1, 1))
     return gram
 
@@ -105,11 +113,12 @@
 
 
 def store_parts(part, index, ref):
-    width = ref.shape[2]
     for h in range(2):
         for g in range(GROUPS):
-            value = part[8 * g : 8 * g + 8, h * width : (h + 1) * width]
-            ref[g * LANES + 2 * index + h] = value.astype(ref.dtype)
+            for j in range(TILES):
+                start = (h * TILES + j) * TILE
+                value = part[8 * g : 8 * g + 8, start : start + TILE]
+                ref[g * LANES + lane_of(2 * index + h, j), j] = value.astype(ref.dtype)
 
 
 def chunks(total, size):
@@ -183,41 +192,54 @@
 
 def left_kernel(own_ref, other_ref, inverse_ref, left_ref):
     core = lax.axis_index("core")
-    block = 4 * lax.axis_index("y") + lax.axis_index("x")
-    half, lane = block // LANES, lax.rem(block, LANES)
+    block = 4 * lax.axis_index("yl") + lax.axis_index("x")
     wide = jnp.where(
-        half == 0,
-        wide_block(core == 0, own_ref, other_ref, 0, lane),
-        wide_block(core == 0, own_ref, other_ref, 1, lane),
+        core == lax.axis_index("yh"),
+        block_of(own_ref, block, low=True),
+        block_of(other_ref, block, low=True),
     )
     left = exact(inverse_ref[...], wide)
     rows = left_ref.shape[1]
     left = jnp.where(core == 0, left[:, :rows], left[:, rows:])
-    left_ref[...] = left * math.sqrt(2 * LANES * own_ref.shape[2])
+    left_ref[...] = left * math.sqrt(2 * LANES * TILES * TILE)
 
 
 def last_kernel(
     own_ref, other_ref, gram_ref, left_ref, weight_ref, frozen_ref, left_out, right_ref
 ):
-    first = lax.axis_index("core") == 0
+    core, z = lax.axis_index("core"), lax.axis_index("z")
     inverse = inverse_factor(whole_gram(gram_ref[...] + half_gram(other_ref)))
-    width = own_ref.shape[2]
+    width = TILES * TILE
     left_out[...] = left_ref[...]
     left = left_ref[...].T
-    half = lax.axis_index("z") // 2
     for q in range(4):
-        lane = lax.rem(lax.axis_index("z"), 2) * 4 + q
-        block = jnp.where(
-            half == 0,
-            wide_block(first, own_ref, other_ref, 0, lane),
-            wide_block(first, own_ref, other_ref, 1, lane),
-        )
-        right = exact(inverse, block) * math.sqrt(2 * LANES * width)
+        block = z % 2 * 4 + q
+        wide = jnp.where(core == z // 2, block_of(own_ref, block), block_of(other_ref, block))
+        right = exact(inverse, wide) * math.sqrt(2 * LANES * width)
         at = slice(q * width, (q + 1) * width)
         right_ref[:, at] = right
         frozen_ref[:, at] = weight_ref[:, at].astype(F32) - exact(left, right) / math.sqrt(RANK)
 
 
+def spread_kernel(terms_ref, copies_ref):
+    lane = 4 * lax.axis_index("yl") + lax.axis_index("x")
+    pairs = []
+    for j in range(TILES):
+        value = terms_ref[0, j].astype(F32)
+        for i in range(1, GROUPS * LANES):
+            value = value + terms_ref[i, j].astype(F32)
+        pairs.append(split(value))
+    for block in range(LANES):
+        tile = (block - lane + LANES) % LANES
+        low = pairs[0][1].astype(F32)
+        for j in range(1, TILES):
+            low = jnp.where(tile == j, pairs[j][1].astype(F32), low)
+        for g in range(GROUPS):
+            for j in range(TILES):
+                copies_ref[g * LANES + block, j] = pairs[j][0]
+            copies_ref[g * LANES + block, TILES] = low.astype(BF16)
+
+
 def in_hbm(array):
     return pltpu.with_memory_space_constraint(array, pltpu.HBM)
 
@@ -226,7 +248,7 @@
     return pltpu.with_memory_space_constraint(array, pltpu.VMEM)
 
 
-def total(send, applied, b, dtype=F32):
+def total(send, applied, b, dtype=F32, low=False):
     keep = pl.pallas_call(
         keep_kernel, out_shape=jax.ShapeDtypeStruct(send.shape, F32), in_specs=[VMEM] * 2,
         out_specs=VMEM, compiler_params=PARAMS, name="keep",
@@ -234,8 +256,15 @@
     got = lax.ppermute(send, "core", [(0, 1), (1, 0)])
     pair = (keep + got.astype(F32)).astype(BF16)
     terms = lax.all_to_all(pair, CHIPS, 0, 0, tiled=True)
-    mine = lax.optimization_barrier(jnp.sum(terms.astype(F32), axis=0)).astype(dtype)
-    copies = jnp.broadcast_to(mine[None], terms.shape)
+    if low:
+        copies = pl.pallas_call(
+            spread_kernel,
+            out_shape=jax.ShapeDtypeStruct((GROUPS * LANES, TILES + 1, 8, TILE), BF16),
+            in_specs=[VMEM], out_specs=VMEM, compiler_params=PARAMS, name="spread",
+        )(terms)
+    else:
+        mine = lax.optimization_barrier(jnp.sum(terms.astype(F32), axis=0)).astype(dtype)
+        copies = jnp.broadcast_to(mine[None], terms.shape)
     own = lax.all_to_all(copies, CHIPS, 0, 0, tiled=True)
     return own, lax.ppermute(own, "core", [(0, 1), (1, 0)])
 
@@ -244,7 +273,7 @@
     tokens, n = acts.shape
     rows, cols = weight.shape
     partial = (
-        jax.ShapeDtypeStruct((LANES * GROUPS, 8, n // (2 * LANES)), BF16),
+        jax.ShapeDtypeStruct((GROUPS * LANES, TILES, 8, TILE), BF16),
         jax.ShapeDtypeStruct((RANK, tokens), BF16),
     )
     held = pltpu.VMEM((tokens, n), BF16)
@@ -278,7 +307,7 @@
     *made, _ = step(sketch, out_grads, acts)
     cosketch = total(*made, acts, BF16)
     *made, _ = step(cosketch, acts, out_grads)
-    power = total(*made, out_grads)
+    power = total(*made, out_grads, low=True)
     *made, inverse = step(power, out_grads, acts)
     left = pl.pallas_call(
         left_kernel, out_shape=pltpu.VMEM((RANK, rows), F32), in_specs=[VMEM] * 3, out_specs=VMEM,
@@ -301,8 +330,8 @@
 
 
 def solution(mesh):
-    mesh = Mesh(mesh.devices.reshape(4, 4, 2, 4), ("y", "x", "core", "z"))
-    row = ("y", "x", "core")
+    mesh = Mesh(mesh.devices.reshape(2, 2, 4, 2, 4), ("yh", "yl", "x", "core", "z"))
+    row = ("yh", "yl", "x", "core")
     tokens = P((*row, "z"), None)
     return jax.shard_map(
         local, mesh=mesh, in_specs=(tokens, tokens, P(), P(row, "z")),

time: 199 us -> 194 us (0.975)
  blocking collectives: 138 us -> 134 us
    all_to_all x4, blocking collectives: 69.8 us -> 66.1 us  [total(): own = lax.all_to_all(copies, CHIPS, 0, 0, tiled=True)]
where the time goes in v6:
time: 194 us
  blocking collectives  134 us (69%)
  Pallas kernels  41.3 us (21%)
  starting transfers between devices  13.8 us (7%)
  waiting for transfers between devices  3.04 us (2%)
    all_to_all x4, blocking collectives, total(): terms = lax.all_to_all(pair, CHIPS, 0, 0, tiled=True)  68.1 us
    all_to_all x4, blocking collectives, total(): own = lax.all_to_all(copies, CHIPS, 0, 0, tiled=True)  66.1 us
    pallas_call x3, Pallas kernels, step(): pl.pallas_call(next_kernel, out_shape=(*partial, jax.ShapeDtypeStruct((RA...  12.4 us
    pallas_call x1, Pallas kernels, local(): pl.pallas_call(first_kernel, out_shape=(*partial, held, held), in_specs=[...  12 us
    ppermute x4, starting transfers between devices, total(): return (own, lax.ppermute(own, 'core', [(0, 1), (1, 0)]))  11.9 us
    pallas_call x3, Pallas kernels, step(): pl.pallas_call(own_kernel, out_shape=(gram, raw), in_specs=[VMEM] * 2, ou...  6.85 us
    pallas_call x1, Pallas kernels, local(): pl.pallas_call(last_kernel, out_shape=(jax.ShapeDtypeStruct((rows, cols),...  4.61 us
    pallas_call x4, Pallas kernels, total(): pl.pallas_call(keep_kernel, out_shape=jax.ShapeDtypeStruct(send.shape, F3...  4.59 us
  transfers between devices with their start and end apart: 8, of which 5 were waited for; matrix products, arithmetic and copies ran while one was open for 0% of the time, Pallas kernels for 6%

profile of v6, /device:TPU:1, one launch (start us, length us, event | category | flops | bytes accessed | tf_op | source)
XLA Modules:
  0.0 194.0 jit_solution(17109289383989883166)
XLA Ops:
  0.6 12.0 %first.1 = (bf16[64,3,8,128]{3,2,1,0:T(8,128)(2,1)S(1)}, bf16[64,960]{1,0:T(8,128)(2,1)S(1)}, bf16[960,6144]{1,0:T(8,128)(2,1)S(1)}, bf16[960,6144]{1,0:T(8,128)(2,1)S(1)}) custom-call(bf16[64,6144]{1,0:T(8,128)(2,1)} %bitcast.2, bf16[960,6144]{1,0:T(8,128)(2,1)} %a_ref.1, bf16[960,6144]{1,0:T(8,128)(2,1)} %b_ref.1), custom_call_target="tpu_custom_call" | custom-call | tf_op jit(solution)/shard_map/first/pallas_call | solution.py:280
  12.7 1.5 collective-permute-start
  14.2 1.1 keep.4
  15.3 0.2 collective-permute-done
  15.5 0.1 add_convert_fusion.3
  15.6 22.3 %all_to_all.40 = bf16[64,3,8,128]{3,2,1,0:T(8,128)(2,1)S(1)} all-to-all(bf16[64,3,8,128]{3,2,1,0:T(8,128)(2,1)S(1)} %add_convert_fusion.3), channel_id=1, replica_groups=mesh['yh'=2,'yl'=2,'x'=4,'core'=2,'z'=4] {'yh','z','yl','x'}, dimensions={0} | all-to-all | bytes 786432 | tf_op jit(solution)/shard_map/all_to_all | solution.py:258
  37.9 0.1 convert_reduce_fusion.2
  38.0 0.1 broadcast_in_dim.6
  38.0 17.9 %all_to_all.41.own_ref = f32[64,3,8,128]{3,2,1,0:T(8,128)S(1)} all-to-all(f32[64,3,8,128]{3,2,1,0:T(8,128)S(1)} %broadcast_in_dim.6), channel_id=1, replica_groups=mesh['yh'=2,'yl'=2,'x'=4,'core'=2,'z'=4] {'yh','z','yl','x'}, dimensions={0} | all-to-all | bytes 1572864 | tf_op jit(solution)/shard_map/all_to_all | solution.py:268
  56.0 3.1 %collective-permute-start.1 = (f32[64,3,8,128]{3,2,1,0:T(8,128)S(1)}, f32[64,3,8,128]{3,2,1,0:T(8,128)S(1)}, u32[]{:S(2)}, u32[]{:S(2)}) collective-permute-start(f32[64,3,8,128]{3,2,1,0:T(8,128)S(1)} %all_to_all.41.own_ref), channel_id=1, source_target_pairs={{0,4},{4,0},{1,5},{5,1},{2,6},{6,2},{3,7},{7,3},{8,12},{12,8},{9,1... | collective-permute-start | bytes 2359304 | tf_op jit(solution)/shard_map/ppermute | solution.py:269
  59.1 2.3 %own.3 = (f32[128,128]{1,0:T(8,128)S(1)}, f32[64,960]{1,0:T(8,128)S(1)}) custom-call(f32[64,3,8,128]{3,2,1,0:T(8,128)S(1)} %all_to_all.41.own_ref, bf16[960,6144]{1,0:T(8,128)(2,1)S(1)} %get-tuple-element.24.b_ref.a_ref), custom_call_target="tpu_custom_call" | custom-call | tf_op jit(solution)/shard_map/own/pallas_call | solution.py:296
  61.4 4.1 %step.3 = (bf16[64,3,8,128]{3,2,1,0:T(8,128)(2,1)S(1)}, bf16[64,960]{1,0:T(8,128)(2,1)S(1)}, f32[64,64]{1,0:T(8,128)}) custom-call(f32[64,3,8,128]{3,2,1,0:T(8,128)S(1)} %collective-permute-done.1.other_ref, f32[128,128]{1,0:T(8,128)S(1)} %get-tuple-element.26.gram_ref, f32[64,960]{1,0:T(8,128)S(1)} %get-tuple-element.27.raw_ref, ...), custom_call_target="tpu_custom_call" | custom-call | tf_op jit(solution)/shard_map/step/pallas_call | solution.py:300
  65.6 0.3 collective-permute-start.2
  65.8 1.2 keep.5
  67.0 0.5 collective-permute-done.2
  67.6 0.1 add_convert_fusion.2
  67.6 15.2 %all_to_all.42 = bf16[64,3,8,128]{3,2,1,0:T(8,128)(2,1)S(1)} all-to-all(bf16[64,3,8,128]{3,2,1,0:T(8,128)(2,1)S(1)} %add_convert_fusion.2), channel_id=1, replica_groups=mesh['yh'=2,'yl'=2,'x'=4,'core'=2,'z'=4] {'yh','z','yl','x'}, dimensions={0} | all-to-all | bytes 786432 | tf_op jit(solution)/shard_map/all_to_all | solution.py:258
  82.9 0.1 convert_reduce_fusion.1
  83.0 0.1 broadcast_in_dim.7
  83.0 14.3 %all_to_all.43.own_ref = bf16[64,3,8,128]{3,2,1,0:T(8,128)(2,1)S(1)} all-to-all(bf16[64,3,8,128]{3,2,1,0:T(8,128)(2,1)S(1)} %broadcast_in_dim.7), channel_id=1, replica_groups=mesh['yh'=2,'yl'=2,'x'=4,'core'=2,'z'=4] {'yh','z','yl','x'}, dimensions={0} | all-to-all | bytes 786432 | tf_op jit(solution)/shard_map/all_to_all | solution.py:268
  97.4 2.9 %collective-permute-start.3 = (bf16[64,3,8,128]{3,2,1,0:T(8,128)(2,1)S(1)}, bf16[64,3,8,128]{3,2,1,0:T(8,128)(2,1)S(1)}, u32[]{:S(2)}, u32[]{:S(2)}) collective-permute-start(bf16[64,3,8,128]{3,2,1,0:T(8,128)(2,1)S(1)} %all_to_all.43.own_ref), channel_id=1, source_target_pairs={{0,4},{4,0},{1,5},{5,1},{2,6},{6,2},{3,7},{7,3},{8,12},{12,8},{9,1... | collective-permute-start | bytes 1179656 | tf_op jit(solution)/shard_map/ppermute | solution.py:269
  100.2 2.3 %own.4 = (f32[128,128]{1,0:T(8,128)S(1)}, f32[64,960]{1,0:T(8,128)S(1)}) custom-call(bf16[64,3,8,128]{3,2,1,0:T(8,128)(2,1)S(1)} %all_to_all.43.own_ref, bf16[960,6144]{1,0:T(8,128)(2,1)S(1)} %get-tuple-element.28.b_ref.a_ref), custom_call_target="tpu_custom_call" | custom-call | tf_op jit(solution)/shard_map/own/pallas_call | solution.py:296
  102.5 0.0 collective-permute-done.3.other_ref
  102.5 4.1 %step.4 = (bf16[64,3,8,128]{3,2,1,0:T(8,128)(2,1)S(1)}, bf16[64,960]{1,0:T(8,128)(2,1)S(1)}, f32[64,64]{1,0:T(8,128)}) custom-call(bf16[64,3,8,128]{3,2,1,0:T(8,128)(2,1)S(1)} %collective-permute-done.3.other_ref, f32[128,128]{1,0:T(8,128)S(1)} %get-tuple-element.31.gram_ref, f32[64,960]{1,0:T(8,128)S(1)} %get-tuple-element.32.raw_ref, ...), custom_call_target="tpu_custom_call" | custom-call | tf_op jit(solution)/shard_map/step/pallas_call | solution.py:300
  106.7 0.1 collective-permute-start.4
  106.8 1.1 keep.6
  107.9 0.6 collective-permute-done.4
  108.5 0.1 add_convert_fusion.1
  108.5 15.4 %all_to_all.44.terms_ref = bf16[64,3,8,128]{3,2,1,0:T(8,128)(2,1)S(1)} all-to-all(bf16[64,3,8,128]{3,2,1,0:T(8,128)(2,1)S(1)} %add_convert_fusion.1), channel_id=1, replica_groups=mesh['yh'=2,'yl'=2,'x'=4,'core'=2,'z'=4] {'yh','z','yl','x'}, dimensions={0} | all-to-all | bytes 786432 | tf_op jit(solution)/shard_map/all_to_all | solution.py:258
  123.9 0.1 spread.1
  124.0 15.5 %all_to_all.45.own_ref = bf16[64,4,8,128]{3,2,1,0:T(8,128)(2,1)S(1)} all-to-all(bf16[64,4,8,128]{3,2,1,0:T(8,128)(2,1)S(1)} %spread.1), channel_id=1, replica_groups=mesh['yh'=2,'yl'=2,'x'=4,'core'=2,'z'=4] {'yh','z','yl','x'}, dimensions={0} | all-to-all | bytes 1048576 | tf_op jit(solution)/shard_map/all_to_all | solution.py:268
  139.5 3.0 %collective-permute-start.5 = (bf16[64,4,8,128]{3,2,1,0:T(8,128)(2,1)S(1)}, bf16[64,4,8,128]{3,2,1,0:T(8,128)(2,1)S(1)}, u32[]{:S(2)}, u32[]{:S(2)}) collective-permute-start(bf16[64,4,8,128]{3,2,1,0:T(8,128)(2,1)S(1)} %all_to_all.45.own_ref), channel_id=1, source_target_pairs={{0,4},{4,0},{1,5},{5,1},{2,6},{6,2},{3,7},{7,3},{8,12},{12,8},{9,1... | collective-permute-start | bytes 1572872 | tf_op jit(solution)/shard_map/ppermute | solution.py:269
  142.5 2.3 %own.5 = (f32[128,128]{1,0:T(8,128)S(1)}, f32[64,960]{1,0:T(8,128)S(1)}) custom-call(bf16[64,4,8,128]{3,2,1,0:T(8,128)(2,1)S(1)} %all_to_all.45.own_ref, bf16[960,6144]{1,0:T(8,128)(2,1)S(1)} %get-tuple-element.24.b_ref.a_ref), custom_call_target="tpu_custom_call" | custom-call | tf_op jit(solution)/shard_map/own/pallas_call | solution.py:296
  144.8 4.1 %step.5 = (bf16[64,3,8,128]{3,2,1,0:T(8,128)(2,1)S(1)}, bf16[64,960]{1,0:T(8,128)(2,1)S(1)}, f32[64,64]{1,0:T(8,128)S(1)}) custom-call(bf16[64,4,8,128]{3,2,1,0:T(8,128)(2,1)S(1)} %collective-permute-done.5.other_ref, f32[128,128]{1,0:T(8,128)S(1)} %get-tuple-element.35.gram_ref, f32[64,960]{1,0:T(8,128)S(1)} %get-tuple-element.36.raw_ref, ...), custom_call_target="tpu_custom_call" | custom-call | tf_op jit(solution)/shard_map/step/pallas_call | solution.py:300
  148.9 0.0 copy-start
  149.0 0.1 collective-permute-start.6
  149.1 1.1 keep.7
  150.2 0.6 collective-permute-done.6
  150.8 0.1 add_convert_fusion
  150.8 15.2 %all_to_all.46 = bf16[64,3,8,128]{3,2,1,0:T(8,128)(2,1)S(1)} all-to-all(bf16[64,3,8,128]{3,2,1,0:T(8,128)(2,1)S(1)} %add_convert_fusion), channel_id=1, replica_groups=mesh['yh'=2,'yl'=2,'x'=4,'core'=2,'z'=4] {'yh','z','yl','x'}, dimensions={0} | all-to-all | bytes 786432 | tf_op jit(solution)/shard_map/all_to_all | solution.py:258
  166.1 0.1 convert_reduce_fusion
  166.1 0.1 broadcast_in_dim.8
  166.2 18.4 %all_to_all.47.own_ref = f32[64,3,8,128]{3,2,1,0:T(8,128)S(1)} all-to-all(f32[64,3,8,128]{3,2,1,0:T(8,128)S(1)} %broadcast_in_dim.8), channel_id=1, replica_groups=mesh['yh'=2,'yl'=2,'x'=4,'core'=2,'z'=4] {'yh','z','yl','x'}, dimensions={0} | all-to-all | bytes 1572864 | tf_op jit(solution)/shard_map/all_to_all | solution.py:268
  184.6 2.9 %collective-permute-start.7 = (f32[64,3,8,128]{3,2,1,0:T(8,128)S(1)}, f32[64,3,8,128]{3,2,1,0:T(8,128)S(1)}, u32[]{:S(2)}, u32[]{:S(2)}) collective-permute-start(f32[64,3,8,128]{3,2,1,0:T(8,128)S(1)} %all_to_all.47.own_ref), channel_id=1, source_target_pairs={{0,4},{4,0},{1,5},{5,1},{2,6},{6,2},{3,7},{7,3},{8,12},{12,8},{9,1... | collective-permute-start | bytes 2359304 | tf_op jit(solution)/shard_map/ppermute | solution.py:269
  187.5 0.3 left.1.left_ref
  187.7 0.5 own_gram.1.gram_ref
  188.2 1.2 collective-permute-done.7.other_ref
  189.4 4.6 %last.1 = (f32[192,1536]{1,0:T(8,128)}, f32[64,192]{1,0:T(8,128)}, f32[64,1536]{1,0:T(8,128)}) custom-call(f32[64,3,8,128]{3,2,1,0:T(8,128)S(1)} %all_to_all.47.own_ref, f32[64,3,8,128]{3,2,1,0:T(8,128)S(1)} %collective-permute-done.7.other_ref, f32[128,128]{1,0:T(8,128)S(1)} %own_gram.1.gram_ref, f32[64,192]{1,0:T(8,128)S(1)} %left.1.left_ref, ...), custom_call_target="tpu_custom_call" | custom-call | tf_op jit(solution)/shard_map/last/pallas_call | solution.py:321
  (3 shorter events, 0.0 us)
Async XLA Ops:
  12.7 2.9 %collective-permute-start = (bf16[64,3,8,128]{3,2,1,0:T(8,128)(2,1)S(1)}, bf16[64,3,8,128]{3,2,1,0:T(8,128)(2,1)S(1)}, u32[]{:S(2)}, u32[]{:S(2)}) collective-permute-start(bf16[64,3,8,128]{3,2,1,0:T(8,128)(2,1)S(1)} %get-tuple-element.25), channel_id=1, source_target_pairs={{0,4},{4,0},{1,5},{5,1},{2,6},{6,2},{3,7},{7,3},{8,12},{12,8},{9,1... | collective-permute-start | bytes 1179656 | tf_op jit(solution)/shard_map/ppermute | solution.py:256
  56.0 5.4 %collective-permute-start.1 = (f32[64,3,8,128]{3,2,1,0:T(8,128)S(1)}, f32[64,3,8,128]{3,2,1,0:T(8,128)S(1)}, u32[]{:S(2)}, u32[]{:S(2)}) collective-permute-start(f32[64,3,8,128]{3,2,1,0:T(8,128)S(1)} %all_to_all.41.own_ref), channel_id=1, source_target_pairs={{0,4},{4,0},{1,5},{5,1},{2,6},{6,2},{3,7},{7,3},{8,12},{12,8},{9,1... | collective-permute-start | bytes 2359304 | tf_op jit(solution)/shard_map/ppermute | solution.py:269
  65.6 2.0 %collective-permute-start.2 = (bf16[64,3,8,128]{3,2,1,0:T(8,128)(2,1)S(1)}, bf16[64,3,8,128]{3,2,1,0:T(8,128)(2,1)S(1)}, u32[]{:S(2)}, u32[]{:S(2)}) collective-permute-start(bf16[64,3,8,128]{3,2,1,0:T(8,128)(2,1)S(1)} %get-tuple-element.30), channel_id=1, source_target_pairs={{0,4},{4,0},{1,5},{5,1},{2,6},{6,2},{3,7},{7,3},{8,12},{12,8},{9,1... | collective-permute-start | bytes 1179656 | tf_op jit(solution)/shard_map/ppermute | solution.py:256
  97.4 5.1 %collective-permute-start.3 = (bf16[64,3,8,128]{3,2,1,0:T(8,128)(2,1)S(1)}, bf16[64,3,8,128]{3,2,1,0:T(8,128)(2,1)S(1)}, u32[]{:S(2)}, u32[]{:S(2)}) collective-permute-start(bf16[64,3,8,128]{3,2,1,0:T(8,128)(2,1)S(1)} %all_to_all.43.own_ref), channel_id=1, source_target_pairs={{0,4},{4,0},{1,5},{5,1},{2,6},{6,2},{3,7},{7,3},{8,12},{12,8},{9,1... | collective-permute-start | bytes 1179656 | tf_op jit(solution)/shard_map/ppermute | solution.py:269
  106.7 1.8 collective-permute-start.4
  139.5 5.3 %collective-permute-start.5 = (bf16[64,4,8,128]{3,2,1,0:T(8,128)(2,1)S(1)}, bf16[64,4,8,128]{3,2,1,0:T(8,128)(2,1)S(1)}, u32[]{:S(2)}, u32[]{:S(2)}) collective-permute-start(bf16[64,4,8,128]{3,2,1,0:T(8,128)(2,1)S(1)} %all_to_all.45.own_ref), channel_id=1, source_target_pairs={{0,4},{4,0},{1,5},{5,1},{2,6},{6,2},{3,7},{7,3},{8,12},{12,8},{9,1... | collective-permute-start | bytes 1572872 | tf_op jit(solution)/shard_map/ppermute | solution.py:269
  148.9 40.4 %copy-start = (bf16[192,1536]{1,0:T(8,128)(2,1)S(1)}, bf16[192,1536]{1,0:T(8,128)(2,1)}, u32[]{:S(2)}) copy-start(bf16[192,1536]{1,0:T(8,128)(2,1)} %weight_ref.1) | copy-start | bytes 1769476
  149.0 1.8 collective-permute-start.6
  184.6 4.8 %collective-permute-start.7 = (f32[64,3,8,128]{3,2,1,0:T(8,128)S(1)}, f32[64,3,8,128]{3,2,1,0:T(8,128)S(1)}, u32[]{:S(2)}, u32[]{:S(2)}) collective-permute-start(f32[64,3,8,128]{3,2,1,0:T(8,128)S(1)} %all_to_all.47.own_ref), channel_id=1, source_target_pairs={{0,4},{4,0},{1,5},{5,1},{2,6},{6,2},{3,7},{7,3},{8,12},{12,8},{9,1... | collective-permute-start | bytes 2359304 | tf_op jit(solution)/shard_map/ppermute | solution.py:269

commit v7 on v6

--- a/solution.py
+++ b/solution.py
@@ -1,3 +1,4 @@
+import functools
 import math
 
 import jax
@@ -7,7 +8,7 @@
 from jax.experimental.pallas import tpu as pltpu
 from jax.sharding import Mesh, PartitionSpec as P
 
-CHIPS = ("yh", "z", "yl", "x")
+CHIPS = ("xl", "z", "y", "xh")
 F32 = jnp.float32
 BF16 = jnp.bfloat16
 RANK = 64
@@ -72,7 +73,7 @@
 
 
 def lane_of(block, tile):
-    return (block - tile + LANES) % LANES
+    return (block - 2 * tile + LANES) % LANES
 
 
 def block_of(ref, block, low=False):
@@ -101,15 +102,18 @@
     return gram[:RANK, :RANK] + (gram[RANK:, RANK:] + cross)
 
 
+def columns(half, block):
+    width = TILES * TILE
+    return pl.ds(pl.multiple_of((2 * block + half) * width, width), width)
+
+
+def blocks_of(ref, half, which):
+    return jnp.concatenate([ref[:, columns(half, block)] for block in which], 1)
+
+
 def half_product(terms, ref, half):
-    size = ref.shape[1] // 2
-    raw = dot(terms, ref[:, pl.ds(pl.multiple_of(half * size, size), size)], (1, 1))
+    raw = dot(terms, blocks_of(ref, half, range(LANES)), (1, 1))
     return raw[:RANK] + raw[RANK:]
-
-
-def half_columns(ref, half, index):
-    size = ref.shape[1] // 8
-    return pl.ds(pl.multiple_of(half * (4 * size) + index * size, size), size)
 
 
 def store_parts(part, index, ref):
@@ -121,6 +125,11 @@
                 ref[g * LANES + lane_of(2 * index + h, j), j] = value.astype(ref.dtype)
 
 
+def half_parts(applied, b_ref, half, ref):
+    for i in range(LANES // 2):
+        store_parts(dot(applied, blocks_of(b_ref, half, (2 * i, 2 * i + 1)), (1, 0)), i, ref)
+
+
 def chunks(total, size):
     return [(s, min(size, total - s)) for s in range(0, total, size)]
 
@@ -129,7 +138,7 @@
     test_ref, a_ref, b_ref, send_ref, applied_ref, a_held, b_held, test_held, a_sems, b_sems, test_sem
 ):
     core = lax.axis_index("core")
-    places = [half_columns(b_ref, half, i) for half in (1 - core, core) for i in range(4)]
+    places = [columns(half, block) for half in (1 - core, core) for block in range(LANES)]
     rows = chunks(a_ref.shape[0], 256)
     test_copy = pltpu.make_async_copy(test_ref, test_held, test_sem)
     a_copies = [
@@ -147,16 +156,15 @@
     applied = []
     for i, (copy, (s, n)) in enumerate(zip(a_copies, rows)):
         copy.wait()
-        for later in b_copies[4 * i : 4 * i + 4]:
+        for later in b_copies[LANES * i : LANES * (i + 1)]:
             later.start()
         applied.append(dot(test, a_held[s : s + n, :], (1, 1)).astype(BF16))
     applied = jnp.concatenate(applied, 1)
     applied_ref[...] = applied
-    for copy in b_copies[:4]:
+    for copy in b_copies[:LANES]:
         copy.wait()
-    for i in range(4):
-        store_parts(dot(applied, b_held[:, places[i]], (1, 0)), i, send_ref)
-    for copy in b_copies[4:]:
+    half_parts(applied, b_held, 1 - core, send_ref)
+    for copy in b_copies[LANES:]:
         copy.wait()
 
 
@@ -178,23 +186,18 @@
     raw = raw_ref[...] + half_product(split_held[...], a_ref, other)
     applied = exact(inverse, raw).astype(BF16)
     applied_ref[...] = applied
-    for i in range(4):
-        part = dot(applied, b_ref[:, half_columns(b_ref, other, i)], (1, 0))
-        store_parts(part, i, send_ref)
+    half_parts(applied, b_ref, other, send_ref)
 
 
 def keep_kernel(applied_ref, b_ref, keep_ref):
-    core = lax.axis_index("core")
-    for i in range(4):
-        part = dot(applied_ref[...], b_ref[:, half_columns(b_ref, core, i)], (1, 0))
-        store_parts(part, i, keep_ref)
+    half_parts(applied_ref[...], b_ref, lax.axis_index("core"), keep_ref)
 
 
 def left_kernel(own_ref, other_ref, inverse_ref, left_ref):
     core = lax.axis_index("core")
-    block = 4 * lax.axis_index("yl") + lax.axis_index("x")
+    block = 2 * lax.axis_index("y") + lax.axis_index("xh")
     wide = jnp.where(
-        core == lax.axis_index("yh"),
+        core == lax.axis_index("xl"),
         block_of(own_ref, block, low=True),
         block_of(other_ref, block, low=True),
     )
@@ -213,16 +216,20 @@
     left_out[...] = left_ref[...]
     left = left_ref[...].T
     for q in range(4):
-        block = z % 2 * 4 + q
-        wide = jnp.where(core == z // 2, block_of(own_ref, block), block_of(other_ref, block))
+        block = 2 * z + q // 2
+        wide = jnp.where(
+            core == q % 2,
+            block_of(own_ref, block, low=True),
+            block_of(other_ref, block, low=True),
+        )
         right = exact(inverse, wide) * math.sqrt(2 * LANES * width)
         at = slice(q * width, (q + 1) * width)
         right_ref[:, at] = right
         frozen_ref[:, at] = weight_ref[:, at].astype(F32) - exact(left, right) / math.sqrt(RANK)
 
 
-def spread_kernel(terms_ref, copies_ref):
-    lane = 4 * lax.axis_index("yl") + lax.axis_index("x")
+def spread_kernel(terms_ref, copies_ref, *, rows):
+    lane = 2 * lax.axis_index("y") + lax.axis_index("xh")
     pairs = []
     for j in range(TILES):
         value = terms_ref[0, j].astype(F32)
@@ -230,13 +237,18 @@
             value = value + terms_ref[i, j].astype(F32)
         pairs.append(split(value))
     for block in range(LANES):
-        tile = (block - lane + LANES) % LANES
-        low = pairs[0][1].astype(F32)
-        for j in range(1, TILES):
-            low = jnp.where(tile == j, pairs[j][1].astype(F32), low)
         for g in range(GROUPS):
-            for j in range(TILES):
+            if rows:
+                tile = (block - lane + LANES) % LANES
+                step = 2
+            else:
+                tile = (g % 4 - lane // 2 + 4) % 4
+                step = 1
+            low = pairs[0][1].astype(F32)
+            for j in range(1, TILES):
+                low = jnp.where(tile == step * j, pairs[j][1].astype(F32), low)
                 copies_ref[g * LANES + block, j] = pairs[j][0]
+            copies_ref[g * LANES + block, 0] = pairs[0][0]
             copies_ref[g * LANES + block, TILES] = low.astype(BF16)
 
 
@@ -248,7 +260,7 @@
     return pltpu.with_memory_space_constraint(array, pltpu.VMEM)
 
 
-def total(send, applied, b, dtype=F32, low=False):
+def total(send, applied, b, dtype=F32, low=None):
     keep = pl.pallas_call(
         keep_kernel, out_shape=jax.ShapeDtypeStruct(send.shape, F32), in_specs=[VMEM] * 2,
         out_specs=VMEM, compiler_params=PARAMS, name="keep",
@@ -258,7 +270,7 @@
     terms = lax.all_to_all(pair, CHIPS, 0, 0, tiled=True)
     if low:
         copies = pl.pallas_call(
-            spread_kernel,
+            functools.partial(spread_kernel, rows=low == "rows"),
             out_shape=jax.ShapeDtypeStruct((GROUPS * LANES, TILES + 1, 8, TILE), BF16),
             in_specs=[VMEM], out_specs=VMEM, compiler_params=PARAMS, name="spread",
         )(terms)
@@ -282,7 +294,7 @@
         out_specs=(VMEM,) * 4,
         scratch_shapes=[
             pltpu.VMEM((RANK, n), BF16), pltpu.SemaphoreType.DMA((len(chunks(tokens, 256)),)),
-            pltpu.SemaphoreType.DMA((8,)), pltpu.SemaphoreType.DMA(()),
+            pltpu.SemaphoreType.DMA((2 * LANES,)), pltpu.SemaphoreType.DMA(()),
         ],
         compiler_params=PARAMS, name="first",
     )(in_hbm(test_matrix.T), in_hbm(acts), in_hbm(out_grads))
@@ -307,13 +319,13 @@
     *made, _ = step(sketch, out_grads, acts)
     cosketch = total(*made, acts, BF16)
     *made, _ = step(cosketch, acts, out_grads)
-    power = total(*made, out_grads, low=True)
+    power = total(*made, out_grads, low="rows")
     *made, inverse = step(power, out_grads, acts)
     left = pl.pallas_call(
         left_kernel, out_shape=pltpu.VMEM((RANK, rows), F32), in_specs=[VMEM] * 3, out_specs=VMEM,
         compiler_params=PARAMS, name="left",
     )(*power, inverse)
-    own, other = total(*made, acts)
+    own, other = total(*made, acts, low="columns")
     own_gram = pl.pallas_call(
         own_gram_kernel, out_shape=gram, in_specs=[VMEM], out_specs=VMEM, compiler_params=PARAMS,
         name="own_gram",
@@ -330,8 +342,8 @@
 
 
 def solution(mesh):
-    mesh = Mesh(mesh.devices.reshape(2, 2, 4, 2, 4), ("yh", "yl", "x", "core", "z"))
-    row = ("yh", "yl", "x", "core")
+    mesh = Mesh(mesh.devices.reshape(4, 2, 2, 2, 4), ("y", "xh", "xl", "core", "z"))
+    row = ("y", "xh", "xl", "core")
     tokens = P((*row, "z"), None)
     return jax.shard_map(
         local, mesh=mesh, in_specs=(tokens, tokens, P(), P(row, "z")),

time: 194 us -> 192 us (0.990)
  blocking collectives: 134 us -> 131 us
    all_to_all x4, blocking collectives: 66.1 us -> 63.3 us  [total(): own = lax.all_to_all(copies, CHIPS, 0, 0, tiled=True)]
  transfers between devices with their start and end apart: 8 -> 8, of which waited for: 5 -> 5; matrix products, arithmetic and copies ran while one was open for 0% -> 0% of each run, Pallas kernels for 6% -> 7%
where the time goes in v7:
time: 192 us
  blocking collectives  131 us (68%)
  Pallas kernels  42.8 us (22%)
  starting transfers between devices  14.2 us (7%)
  waiting for transfers between devices  2.25 us (1%)
    all_to_all x4, blocking collectives, total(): terms = lax.all_to_all(pair, CHIPS, 0, 0, tiled=True)  67.9 us
    all_to_all x4, blocking collectives, total(): own = lax.all_to_all(copies, CHIPS, 0, 0, tiled=True)  63.3 us
    pallas_call x3, Pallas kernels, step(): pl.pallas_call(next_kernel, out_shape=(*partial, jax.ShapeDtypeStruct((RA...  13 us
    ppermute x4, starting transfers between devices, total(): return (own, lax.ppermute(own, 'core', [(0, 1), (1, 0)]))  12.5 us
    pallas_call x1, Pallas kernels, local(): pl.pallas_call(first_kernel, out_shape=(*partial, held, held), in_specs=[...  12.2 us
    pallas_call x3, Pallas kernels, step(): pl.pallas_call(own_kernel, out_shape=(gram, raw), in_specs=[VMEM] * 2, ou...  7.17 us
    pallas_call x4, Pallas kernels, total(): pl.pallas_call(keep_kernel, out_shape=jax.ShapeDtypeStruct(send.shape, F3...  4.95 us
    pallas_call x1, Pallas kernels, local(): pl.pallas_call(last_kernel, out_shape=(jax.ShapeDtypeStruct((rows, cols),...  4.6 us
  transfers between devices with their start and end apart: 8, of which 5 were waited for; matrix products, arithmetic and copies ran while one was open for 0% of the time, Pallas kernels for 7%

profile of v7, /device:TPU:1, one launch (start us, length us, event | category | flops | bytes accessed | tf_op | source)
XLA Modules:
  0.0 192.0 jit_solution(12113660602884106586)
XLA Ops:
  0.6 12.2 %first.1 = (bf16[64,3,8,128]{3,2,1,0:T(8,128)(2,1)S(1)}, bf16[64,960]{1,0:T(8,128)(2,1)S(1)}, bf16[960,6144]{1,0:T(8,128)(2,1)S(1)}, bf16[960,6144]{1,0:T(8,128)(2,1)S(1)}) custom-call(bf16[64,6144]{1,0:T(8,128)(2,1)} %bitcast.2, bf16[960,6144]{1,0:T(8,128)(2,1)} %a_ref.1, bf16[960,6144]{1,0:T(8,128)(2,1)} %b_ref.1), custom_call_target="tpu_custom_call" | custom-call | tf_op jit(solution)/shard_map/first/pallas_call | solution.py:292
  12.8 1.5 collective-permute-start
  14.3 1.2 keep.4
  15.6 0.1 collective-permute-done
  15.7 0.1 add_convert_fusion.3
  15.8 21.9 %all_to_all.40 = bf16[64,3,8,128]{3,2,1,0:T(8,128)(2,1)S(1)} all-to-all(bf16[64,3,8,128]{3,2,1,0:T(8,128)(2,1)S(1)} %add_convert_fusion.3), channel_id=1, replica_groups=mesh['y'=4,'xh'=2,'xl'=2,'core'=2,'z'=4] {'xl','z','y','xh'}, dimensions={0} | all-to-all | bytes 786432 | tf_op jit(solution)/shard_map/all_to_all | solution.py:270
  37.6 0.1 convert_reduce_fusion.1
  37.7 0.1 broadcast_in_dim.4
  37.8 18.3 %all_to_all.41.own_ref = f32[64,3,8,128]{3,2,1,0:T(8,128)S(1)} all-to-all(f32[64,3,8,128]{3,2,1,0:T(8,128)S(1)} %broadcast_in_dim.4), channel_id=1, replica_groups=mesh['y'=4,'xh'=2,'xl'=2,'core'=2,'z'=4] {'xl','z','y','xh'}, dimensions={0} | all-to-all | bytes 1572864 | tf_op jit(solution)/shard_map/all_to_all | solution.py:280
  56.1 3.1 %collective-permute-start.1 = (f32[64,3,8,128]{3,2,1,0:T(8,128)S(1)}, f32[64,3,8,128]{3,2,1,0:T(8,128)S(1)}, u32[]{:S(2)}, u32[]{:S(2)}) collective-permute-start(f32[64,3,8,128]{3,2,1,0:T(8,128)S(1)} %all_to_all.41.own_ref), channel_id=1, source_target_pairs={{0,4},{4,0},{1,5},{5,1},{2,6},{6,2},{3,7},{7,3},{8,12},{12,8},{9,1... | collective-permute-start | bytes 2359304 | tf_op jit(solution)/shard_map/ppermute | solution.py:281
  59.1 2.4 %own.3 = (f32[128,128]{1,0:T(8,128)S(1)}, f32[64,960]{1,0:T(8,128)S(1)}) custom-call(f32[64,3,8,128]{3,2,1,0:T(8,128)S(1)} %all_to_all.41.own_ref, bf16[960,6144]{1,0:T(8,128)(2,1)S(1)} %get-tuple-element.24.b_ref.a_ref), custom_call_target="tpu_custom_call" | custom-call | tf_op jit(solution)/shard_map/own/pallas_call | solution.py:308
  61.5 0.0 collective-permute-done.1.other_ref
  61.5 4.3 %step.3 = (bf16[64,3,8,128]{3,2,1,0:T(8,128)(2,1)S(1)}, bf16[64,960]{1,0:T(8,128)(2,1)S(1)}, f32[64,64]{1,0:T(8,128)}) custom-call(f32[64,3,8,128]{3,2,1,0:T(8,128)S(1)} %collective-permute-done.1.other_ref, f32[128,128]{1,0:T(8,128)S(1)} %get-tuple-element.26.gram_ref, f32[64,960]{1,0:T(8,128)S(1)} %get-tuple-element.27.raw_ref, ...), custom_call_target="tpu_custom_call" | custom-call | tf_op jit(solution)/shard_map/step/pallas_call | solution.py:312
  65.9 0.1 collective-permute-start.2
  65.9 1.2 keep.5
  67.2 0.5 collective-permute-done.2
  67.6 0.1 add_convert_fusion.2
  67.7 15.3 %all_to_all.42 = bf16[64,3,8,128]{3,2,1,0:T(8,128)(2,1)S(1)} all-to-all(bf16[64,3,8,128]{3,2,1,0:T(8,128)(2,1)S(1)} %add_convert_fusion.2), channel_id=1, replica_groups=mesh['y'=4,'xh'=2,'xl'=2,'core'=2,'z'=4] {'xl','z','y','xh'}, dimensions={0} | all-to-all | bytes 786432 | tf_op jit(solution)/shard_map/all_to_all | solution.py:270
  83.0 0.1 convert_reduce_fusion
  83.1 0.1 broadcast_in_dim.5
  83.1 14.4 %all_to_all.43.own_ref = bf16[64,3,8,128]{3,2,1,0:T(8,128)(2,1)S(1)} all-to-all(bf16[64,3,8,128]{3,2,1,0:T(8,128)(2,1)S(1)} %broadcast_in_dim.5), channel_id=1, replica_groups=mesh['y'=4,'xh'=2,'xl'=2,'core'=2,'z'=4] {'xl','z','y','xh'}, dimensions={0} | all-to-all | bytes 786432 | tf_op jit(solution)/shard_map/all_to_all | solution.py:280
  97.5 3.0 %collective-permute-start.3 = (bf16[64,3,8,128]{3,2,1,0:T(8,128)(2,1)S(1)}, bf16[64,3,8,128]{3,2,1,0:T(8,128)(2,1)S(1)}, u32[]{:S(2)}, u32[]{:S(2)}) collective-permute-start(bf16[64,3,8,128]{3,2,1,0:T(8,128)(2,1)S(1)} %all_to_all.43.own_ref), channel_id=1, source_target_pairs={{0,4},{4,0},{1,5},{5,1},{2,6},{6,2},{3,7},{7,3},{8,12},{12,8},{9,1... | collective-permute-start | bytes 1179656 | tf_op jit(solution)/shard_map/ppermute | solution.py:281
  100.6 2.4 %own.4 = (f32[128,128]{1,0:T(8,128)S(1)}, f32[64,960]{1,0:T(8,128)S(1)}) custom-call(bf16[64,3,8,128]{3,2,1,0:T(8,128)(2,1)S(1)} %all_to_all.43.own_ref, bf16[960,6144]{1,0:T(8,128)(2,1)S(1)} %get-tuple-element.28.b_ref.a_ref), custom_call_target="tpu_custom_call" | custom-call | tf_op jit(solution)/shard_map/own/pallas_call | solution.py:308
  103.0 4.3 %step.4 = (bf16[64,3,8,128]{3,2,1,0:T(8,128)(2,1)S(1)}, bf16[64,960]{1,0:T(8,128)(2,1)S(1)}, f32[64,64]{1,0:T(8,128)}) custom-call(bf16[64,3,8,128]{3,2,1,0:T(8,128)(2,1)S(1)} %collective-permute-done.3.other_ref, f32[128,128]{1,0:T(8,128)S(1)} %get-tuple-element.31.gram_ref, f32[64,960]{1,0:T(8,128)S(1)} %get-tuple-element.32.raw_ref, ...), custom_call_target="tpu_custom_call" | custom-call | tf_op jit(solution)/shard_map/step/pallas_call | solution.py:312
  107.3 0.1 collective-permute-start.4
  107.4 1.2 keep.6
  108.6 0.4 collective-permute-done.4
  109.1 0.1 add_convert_fusion.1
  109.2 15.4 %all_to_all.44.terms_ref = bf16[64,3,8,128]{3,2,1,0:T(8,128)(2,1)S(1)} all-to-all(bf16[64,3,8,128]{3,2,1,0:T(8,128)(2,1)S(1)} %add_convert_fusion.1), channel_id=1, replica_groups=mesh['y'=4,'xh'=2,'xl'=2,'core'=2,'z'=4] {'xl','z','y','xh'}, dimensions={0} | all-to-all | bytes 786432 | tf_op jit(solution)/shard_map/all_to_all | solution.py:270
  124.6 0.1 spread.2
  124.7 15.3 %all_to_all.45.own_ref = bf16[64,4,8,128]{3,2,1,0:T(8,128)(2,1)S(1)} all-to-all(bf16[64,4,8,128]{3,2,1,0:T(8,128)(2,1)S(1)} %spread.2), channel_id=1, replica_groups=mesh['y'=4,'xh'=2,'xl'=2,'core'=2,'z'=4] {'xl','z','y','xh'}, dimensions={0} | all-to-all | bytes 1048576 | tf_op jit(solution)/shard_map/all_to_all | solution.py:280
  140.0 3.2 %collective-permute-start.5 = (bf16[64,4,8,128]{3,2,1,0:T(8,128)(2,1)S(1)}, bf16[64,4,8,128]{3,2,1,0:T(8,128)(2,1)S(1)}, u32[]{:S(2)}, u32[]{:S(2)}) collective-permute-start(bf16[64,4,8,128]{3,2,1,0:T(8,128)(2,1)S(1)} %all_to_all.45.own_ref), channel_id=1, source_target_pairs={{0,4},{4,0},{1,5},{5,1},{2,6},{6,2},{3,7},{7,3},{8,12},{12,8},{9,1... | collective-permute-start | bytes 1572872 | tf_op jit(solution)/shard_map/ppermute | solution.py:281
  143.2 2.4 %own.5 = (f32[128,128]{1,0:T(8,128)S(1)}, f32[64,960]{1,0:T(8,128)S(1)}) custom-call(bf16[64,4,8,128]{3,2,1,0:T(8,128)(2,1)S(1)} %all_to_all.45.own_ref, bf16[960,6144]{1,0:T(8,128)(2,1)S(1)} %get-tuple-element.24.b_ref.a_ref), custom_call_target="tpu_custom_call" | custom-call | tf_op jit(solution)/shard_map/own/pallas_call | solution.py:308
  145.6 0.0 collective-permute-done.5.other_ref
  145.6 4.3 %step.5 = (bf16[64,3,8,128]{3,2,1,0:T(8,128)(2,1)S(1)}, bf16[64,960]{1,0:T(8,128)(2,1)S(1)}, f32[64,64]{1,0:T(8,128)S(1)}) custom-call(bf16[64,4,8,128]{3,2,1,0:T(8,128)(2,1)S(1)} %collective-permute-done.5.other_ref, f32[128,128]{1,0:T(8,128)S(1)} %get-tuple-element.35.gram_ref, f32[64,960]{1,0:T(8,128)S(1)} %get-tuple-element.36.raw_ref, ...), custom_call_target="tpu_custom_call" | custom-call | tf_op jit(solution)/shard_map/step/pallas_call | solution.py:312
  149.9 0.0 copy-start
  150.0 0.1 collective-permute-start.6
  150.0 1.2 keep.7
  151.3 0.5 collective-permute-done.6
  151.8 0.1 add_convert_fusion
  151.8 15.4 %all_to_all.46.terms_ref = bf16[64,3,8,128]{3,2,1,0:T(8,128)(2,1)S(1)} all-to-all(bf16[64,3,8,128]{3,2,1,0:T(8,128)(2,1)S(1)} %add_convert_fusion), channel_id=1, replica_groups=mesh['y'=4,'xh'=2,'xl'=2,'core'=2,'z'=4] {'xl','z','y','xh'}, dimensions={0} | all-to-all | bytes 786432 | tf_op jit(solution)/shard_map/all_to_all | solution.py:270
  167.2 0.1 spread.3
  167.3 15.3 %all_to_all.47.own_ref = bf16[64,4,8,128]{3,2,1,0:T(8,128)(2,1)S(1)} all-to-all(bf16[64,4,8,128]{3,2,1,0:T(8,128)(2,1)S(1)} %spread.3), channel_id=1, replica_groups=mesh['y'=4,'xh'=2,'xl'=2,'core'=2,'z'=4] {'xl','z','y','xh'}, dimensions={0} | all-to-all | bytes 1048576 | tf_op jit(solution)/shard_map/all_to_all | solution.py:280
  182.6 3.2 %collective-permute-start.7 = (bf16[64,4,8,128]{3,2,1,0:T(8,128)(2,1)S(1)}, bf16[64,4,8,128]{3,2,1,0:T(8,128)(2,1)S(1)}, u32[]{:S(2)}, u32[]{:S(2)}) collective-permute-start(bf16[64,4,8,128]{3,2,1,0:T(8,128)(2,1)S(1)} %all_to_all.47.own_ref), channel_id=1, source_target_pairs={{0,4},{4,0},{1,5},{5,1},{2,6},{6,2},{3,7},{7,3},{8,12},{12,8},{9,1... | collective-permute-start | bytes 1572872 | tf_op jit(solution)/shard_map/ppermute | solution.py:281
  185.8 0.3 left.1.left_ref
  186.1 0.5 own_gram.1.gram_ref
  186.6 0.8 collective-permute-done.7.other_ref
  187.4 4.6 %last.1 = (f32[192,1536]{1,0:T(8,128)}, f32[64,192]{1,0:T(8,128)}, f32[64,1536]{1,0:T(8,128)}) custom-call(bf16[64,4,8,128]{3,2,1,0:T(8,128)(2,1)S(1)} %all_to_all.47.own_ref, bf16[64,4,8,128]{3,2,1,0:T(8,128)(2,1)S(1)} %collective-permute-done.7.other_ref, f32[128,128]{1,0:T(8,128)S(1)} %own_gram.1.gram_ref, f32[64,192]{1,0:T(8,128)S(1)} %left.1.left_ref, ...), custom_call_target="tpu_custom_call" | custom-call | tf_op jit(solution)/shard_map/last/pallas_call | solution.py:333
  (2 shorter events, 0.0 us)
Async XLA Ops:
  12.8 2.9 %collective-permute-start = (bf16[64,3,8,128]{3,2,1,0:T(8,128)(2,1)S(1)}, bf16[64,3,8,128]{3,2,1,0:T(8,128)(2,1)S(1)}, u32[]{:S(2)}, u32[]{:S(2)}) collective-permute-start(bf16[64,3,8,128]{3,2,1,0:T(8,128)(2,1)S(1)} %get-tuple-element.25), channel_id=1, source_target_pairs={{0,4},{4,0},{1,5},{5,1},{2,6},{6,2},{3,7},{7,3},{8,12},{12,8},{9,1... | collective-permute-start | bytes 1179656 | tf_op jit(solution)/shard_map/ppermute | solution.py:268
  56.1 5.4 %collective-permute-start.1 = (f32[64,3,8,128]{3,2,1,0:T(8,128)S(1)}, f32[64,3,8,128]{3,2,1,0:T(8,128)S(1)}, u32[]{:S(2)}, u32[]{:S(2)}) collective-permute-start(f32[64,3,8,128]{3,2,1,0:T(8,128)S(1)} %all_to_all.41.own_ref), channel_id=1, source_target_pairs={{0,4},{4,0},{1,5},{5,1},{2,6},{6,2},{3,7},{7,3},{8,12},{12,8},{9,1... | collective-permute-start | bytes 2359304 | tf_op jit(solution)/shard_map/ppermute | solution.py:281
  65.9 1.8 collective-permute-start.2
  97.5 5.4 %collective-permute-start.3 = (bf16[64,3,8,128]{3,2,1,0:T(8,128)(2,1)S(1)}, bf16[64,3,8,128]{3,2,1,0:T(8,128)(2,1)S(1)}, u32[]{:S(2)}, u32[]{:S(2)}) collective-permute-start(bf16[64,3,8,128]{3,2,1,0:T(8,128)(2,1)S(1)} %all_to_all.43.own_ref), channel_id=1, source_target_pairs={{0,4},{4,0},{1,5},{5,1},{2,6},{6,2},{3,7},{7,3},{8,12},{12,8},{9,1... | collective-permute-start | bytes 1179656 | tf_op jit(solution)/shard_map/ppermute | solution.py:281
  107.3 1.8 collective-permute-start.4
  140.0 5.6 %collective-permute-start.5 = (bf16[64,4,8,128]{3,2,1,0:T(8,128)(2,1)S(1)}, bf16[64,4,8,128]{3,2,1,0:T(8,128)(2,1)S(1)}, u32[]{:S(2)}, u32[]{:S(2)}) collective-permute-start(bf16[64,4,8,128]{3,2,1,0:T(8,128)(2,1)S(1)} %all_to_all.45.own_ref), channel_id=1, source_target_pairs={{0,4},{4,0},{1,5},{5,1},{2,6},{6,2},{3,7},{7,3},{8,12},{12,8},{9,1... | collective-permute-start | bytes 1572872 | tf_op jit(solution)/shard_map/ppermute | solution.py:281
  149.9 37.4 %copy-start = (bf16[192,1536]{1,0:T(8,128)(2,1)S(1)}, bf16[192,1536]{1,0:T(8,128)(2,1)}, u32[]{:S(2)}) copy-start(bf16[192,1536]{1,0:T(8,128)(2,1)} %weight_ref.1) | copy-start | bytes 1769476
  150.0 1.8 collective-permute-start.6
  182.6 4.7 %collective-permute-start.7 = (bf16[64,4,8,128]{3,2,1,0:T(8,128)(2,1)S(1)}, bf16[64,4,8,128]{3,2,1,0:T(8,128)(2,1)S(1)}, u32[]{:S(2)}, u32[]{:S(2)}) collective-permute-start(bf16[64,4,8,128]{3,2,1,0:T(8,128)(2,1)S(1)} %all_to_all.47.own_ref), channel_id=1, source_target_pairs={{0,4},{4,0},{1,5},{5,1},{2,6},{6,2},{3,7},{7,3},{8,12},{12,8},{9,1... | collective-permute-start | bytes 1572872 | tf_op jit(solution)/shard_map/ppermute | solution.py:281

commit v8 on v7

--- a/solution.py
+++ b/solution.py
@@ -86,11 +86,17 @@
     return jnp.concatenate(rows, 0)
 
 
+def terms_of(dtype):
+    return RANK if dtype == BF16 else 2 * RANK
+
+
 def half_gram(ref, split_ref=None):
     width = TILES * TILE
-    gram = jnp.zeros((2 * RANK, 2 * RANK), F32)
+    size = terms_of(ref.dtype)
+    gram = jnp.zeros((size, size), F32)
     for block in range(LANES):
-        terms = jnp.concatenate(split(block_of(ref, block)), 0)
+        terms = block_of(ref, block)
+        terms = terms.astype(BF16) if size == RANK else jnp.concatenate(split(terms), 0)
         if split_ref is not None:
             split_ref[:, block * width : (block + 1) * width] = terms
         gram = gram + dot(terms, terms, (1, 1))
@@ -98,6 +104,8 @@
 
 
 def whole_gram(gram):
+    if gram.shape[0] == RANK:
+        return gram
     cross = gram[:RANK, RANK:] + gram[RANK:, :RANK]
     return gram[:RANK, :RANK] + (gram[RANK:, RANK:] + cross)
 
@@ -113,7 +121,7 @@
 
 def half_product(terms, ref, half):
     raw = dot(terms, blocks_of(ref, half, range(LANES)), (1, 1))
-    return raw[:RANK] + raw[RANK:]
+    return raw if raw.shape[0] == RANK else raw[:RANK] + raw[RANK:]
 
 
 def store_parts(part, index, ref):
@@ -299,14 +307,16 @@
         compiler_params=PARAMS, name="first",
     )(in_hbm(test_matrix.T), in_hbm(acts), in_hbm(out_grads))
 
-    gram = jax.ShapeDtypeStruct((2 * RANK, 2 * RANK), F32)
+
+    def gram_like(half):
+        return jax.ShapeDtypeStruct((terms_of(half.dtype),) * 2, F32)
 
     def step(wide, a, b):
         own, other = wide
         raw = jax.ShapeDtypeStruct((RANK, tokens), F32)
-        terms = pltpu.VMEM((2 * RANK, n // 2), BF16)
+        terms = pltpu.VMEM((terms_of(own.dtype), n // 2), BF16)
         sums = pl.pallas_call(
-            own_kernel, out_shape=(gram, raw), in_specs=[VMEM] * 2, out_specs=(VMEM,) * 2,
+            own_kernel, out_shape=(gram_like(own), raw), in_specs=[VMEM] * 2, out_specs=(VMEM,) * 2,
             scratch_shapes=[terms], compiler_params=PARAMS, name="own",
         )(own, in_vmem(a))
         return pl.pallas_call(
@@ -327,7 +337,7 @@
     )(*power, inverse)
     own, other = total(*made, acts, low="columns")
     own_gram = pl.pallas_call(
-        own_gram_kernel, out_shape=gram, in_specs=[VMEM], out_specs=VMEM, compiler_params=PARAMS,
+        own_gram_kernel, out_shape=gram_like(own), in_specs=[VMEM], out_specs=VMEM, compiler_params=PARAMS,
         name="own_gram",
     )(own)
     frozen, left, right = pl.pallas_call(

time: 192 us -> 190 us (0.990)
  Pallas kernels: 42.8 us -> 40.2 us
  transfers between devices with their start and end apart: 8 -> 8, of which waited for: 5 -> 5; matrix products, arithmetic and copies ran while one was open for 0% -> 0% of each run, Pallas kernels for 7% -> 6%
where the time goes in v8:
time: 190 us
  blocking collectives  131 us (69%)
  Pallas kernels  40.2 us (21%)
  starting transfers between devices  14.2 us (7%)
  waiting for transfers between devices  2.47 us (1%)
    all_to_all x4, blocking collectives, total(): terms = lax.all_to_all(pair, CHIPS, 0, 0, tiled=True)  67.9 us
    all_to_all x4, blocking collectives, total(): own = lax.all_to_all(copies, CHIPS, 0, 0, tiled=True)  63.3 us
    ppermute x4, starting transfers between devices, total(): return (own, lax.ppermute(own, 'core', [(0, 1), (1, 0)]))  12.5 us
    pallas_call x1, Pallas kernels, local(): pl.pallas_call(first_kernel, out_shape=(*partial, held, held), in_specs=[...  12.2 us
    pallas_call x3, Pallas kernels, step(): pl.pallas_call(next_kernel, out_shape=(*partial, jax.ShapeDtypeStruct((RA...  11.7 us
    pallas_call x3, Pallas kernels, step(): pl.pallas_call(own_kernel, out_shape=(gram_like(own), raw), in_specs=[VME...  6.5 us
    pallas_call x4, Pallas kernels, total(): pl.pallas_call(keep_kernel, out_shape=jax.ShapeDtypeStruct(send.shape, F3...  4.96 us
    pallas_call x1, Pallas kernels, local(): pl.pallas_call(last_kernel, out_shape=(jax.ShapeDtypeStruct((rows, cols),...  4.14 us
  transfers between devices with their start and end apart: 8, of which 5 were waited for; matrix products, arithmetic and copies ran while one was open for 0% of the time, Pallas kernels for 6%

profile of v8, /device:TPU:1, one launch (start us, length us, event | category | flops | bytes accessed | tf_op | source)
XLA Modules:
  0.0 189.5 jit_solution(14173974020558052680)
XLA Ops:
  0.6 12.2 %first.1 = (bf16[64,3,8,128]{3,2,1,0:T(8,128)(2,1)S(1)}, bf16[64,960]{1,0:T(8,128)(2,1)S(1)}, bf16[960,6144]{1,0:T(8,128)(2,1)S(1)}, bf16[960,6144]{1,0:T(8,128)(2,1)S(1)}) custom-call(bf16[64,6144]{1,0:T(8,128)(2,1)} %bitcast.2, bf16[960,6144]{1,0:T(8,128)(2,1)} %a_ref.1, bf16[960,6144]{1,0:T(8,128)(2,1)} %b_ref.1), custom_call_target="tpu_custom_call" | custom-call | tf_op jit(solution)/shard_map/first/pallas_call | solution.py:300
  12.8 1.5 collective-permute-start
  14.3 1.2 keep.4
  15.6 0.1 collective-permute-done
  15.7 0.1 add_convert_fusion.3
  15.8 21.9 %all_to_all.40 = bf16[64,3,8,128]{3,2,1,0:T(8,128)(2,1)S(1)} all-to-all(bf16[64,3,8,128]{3,2,1,0:T(8,128)(2,1)S(1)} %add_convert_fusion.3), channel_id=1, replica_groups=mesh['y'=4,'xh'=2,'xl'=2,'core'=2,'z'=4] {'xl','z','y','xh'}, dimensions={0} | all-to-all | bytes 786432 | tf_op jit(solution)/shard_map/all_to_all | solution.py:278
  37.6 0.1 convert_reduce_fusion.1
  37.7 0.1 broadcast_in_dim.4
  37.8 18.3 %all_to_all.41.own_ref = f32[64,3,8,128]{3,2,1,0:T(8,128)S(1)} all-to-all(f32[64,3,8,128]{3,2,1,0:T(8,128)S(1)} %broadcast_in_dim.4), channel_id=1, replica_groups=mesh['y'=4,'xh'=2,'xl'=2,'core'=2,'z'=4] {'xl','z','y','xh'}, dimensions={0} | all-to-all | bytes 1572864 | tf_op jit(solution)/shard_map/all_to_all | solution.py:288
  56.1 3.1 %collective-permute-start.1 = (f32[64,3,8,128]{3,2,1,0:T(8,128)S(1)}, f32[64,3,8,128]{3,2,1,0:T(8,128)S(1)}, u32[]{:S(2)}, u32[]{:S(2)}) collective-permute-start(f32[64,3,8,128]{3,2,1,0:T(8,128)S(1)} %all_to_all.41.own_ref), channel_id=1, source_target_pairs={{0,4},{4,0},{1,5},{5,1},{2,6},{6,2},{3,7},{7,3},{8,12},{12,8},{9,1... | collective-permute-start | bytes 2359304 | tf_op jit(solution)/shard_map/ppermute | solution.py:289
  59.1 2.4 %own.3 = (f32[128,128]{1,0:T(8,128)S(1)}, f32[64,960]{1,0:T(8,128)S(1)}) custom-call(f32[64,3,8,128]{3,2,1,0:T(8,128)S(1)} %all_to_all.41.own_ref, bf16[960,6144]{1,0:T(8,128)(2,1)S(1)} %get-tuple-element.24.b_ref.a_ref), custom_call_target="tpu_custom_call" | custom-call | tf_op jit(solution)/shard_map/own/pallas_call | solution.py:318
  61.5 4.3 %step.3 = (bf16[64,3,8,128]{3,2,1,0:T(8,128)(2,1)S(1)}, bf16[64,960]{1,0:T(8,128)(2,1)S(1)}, f32[64,64]{1,0:T(8,128)}) custom-call(f32[64,3,8,128]{3,2,1,0:T(8,128)S(1)} %collective-permute-done.1.other_ref, f32[128,128]{1,0:T(8,128)S(1)} %get-tuple-element.26.gram_ref, f32[64,960]{1,0:T(8,128)S(1)} %get-tuple-element.27.raw_ref, ...), custom_call_target="tpu_custom_call" | custom-call | tf_op jit(solution)/shard_map/step/pallas_call | solution.py:322
  65.9 0.1 collective-permute-start.2
  65.9 1.2 keep.5
  67.2 0.5 collective-permute-done.2
  67.6 0.1 add_convert_fusion.2
  67.7 15.3 %all_to_all.42 = bf16[64,3,8,128]{3,2,1,0:T(8,128)(2,1)S(1)} all-to-all(bf16[64,3,8,128]{3,2,1,0:T(8,128)(2,1)S(1)} %add_convert_fusion.2), channel_id=1, replica_groups=mesh['y'=4,'xh'=2,'xl'=2,'core'=2,'z'=4] {'xl','z','y','xh'}, dimensions={0} | all-to-all | bytes 786432 | tf_op jit(solution)/shard_map/all_to_all | solution.py:278
  83.0 0.1 convert_reduce_fusion
  83.1 0.1 broadcast_in_dim.5
  83.1 14.4 %all_to_all.43.own_ref = bf16[64,3,8,128]{3,2,1,0:T(8,128)(2,1)S(1)} all-to-all(bf16[64,3,8,128]{3,2,1,0:T(8,128)(2,1)S(1)} %broadcast_in_dim.5), channel_id=1, replica_groups=mesh['y'=4,'xh'=2,'xl'=2,'core'=2,'z'=4] {'xl','z','y','xh'}, dimensions={0} | all-to-all | bytes 786432 | tf_op jit(solution)/shard_map/all_to_all | solution.py:288
  97.5 3.0 %collective-permute-start.3 = (bf16[64,3,8,128]{3,2,1,0:T(8,128)(2,1)S(1)}, bf16[64,3,8,128]{3,2,1,0:T(8,128)(2,1)S(1)}, u32[]{:S(2)}, u32[]{:S(2)}) collective-permute-start(bf16[64,3,8,128]{3,2,1,0:T(8,128)(2,1)S(1)} %all_to_all.43.own_ref), channel_id=1, source_target_pairs={{0,4},{4,0},{1,5},{5,1},{2,6},{6,2},{3,7},{7,3},{8,12},{12,8},{9,1... | collective-permute-start | bytes 1179656 | tf_op jit(solution)/shard_map/ppermute | solution.py:289
  100.6 2.1 %own.4 = (f32[64,64]{1,0:T(8,128)S(1)}, f32[64,960]{1,0:T(8,128)S(1)}) custom-call(bf16[64,3,8,128]{3,2,1,0:T(8,128)(2,1)S(1)} %all_to_all.43.own_ref, bf16[960,6144]{1,0:T(8,128)(2,1)S(1)} %get-tuple-element.28.b_ref.a_ref), custom_call_target="tpu_custom_call" | custom-call | tf_op jit(solution)/shard_map/own/pallas_call | solution.py:318
  102.6 0.0 collective-permute-done.3.other_ref
  102.6 3.7 %step.4 = (bf16[64,3,8,128]{3,2,1,0:T(8,128)(2,1)S(1)}, bf16[64,960]{1,0:T(8,128)(2,1)S(1)}, f32[64,64]{1,0:T(8,128)}) custom-call(bf16[64,3,8,128]{3,2,1,0:T(8,128)(2,1)S(1)} %collective-permute-done.3.other_ref, f32[64,64]{1,0:T(8,128)S(1)} %get-tuple-element.31.gram_ref, f32[64,960]{1,0:T(8,128)S(1)} %get-tuple-element.32.raw_ref, ...), custom_call_target="tpu_custom_call" | custom-call | tf_op jit(solution)/shard_map/step/pallas_call | solution.py:322
  106.3 0.0 collective-permute-start.4
  106.4 1.2 keep.6
  107.6 0.5 collective-permute-done.4
  108.1 0.1 add_convert_fusion.1
  108.2 15.4 %all_to_all.44.terms_ref = bf16[64,3,8,128]{3,2,1,0:T(8,128)(2,1)S(1)} all-to-all(bf16[64,3,8,128]{3,2,1,0:T(8,128)(2,1)S(1)} %add_convert_fusion.1), channel_id=1, replica_groups=mesh['y'=4,'xh'=2,'xl'=2,'core'=2,'z'=4] {'xl','z','y','xh'}, dimensions={0} | all-to-all | bytes 786432 | tf_op jit(solution)/shard_map/all_to_all | solution.py:278
  123.6 0.1 spread.2
  123.7 15.3 %all_to_all.45.own_ref = bf16[64,4,8,128]{3,2,1,0:T(8,128)(2,1)S(1)} all-to-all(bf16[64,4,8,128]{3,2,1,0:T(8,128)(2,1)S(1)} %spread.2), channel_id=1, replica_groups=mesh['y'=4,'xh'=2,'xl'=2,'core'=2,'z'=4] {'xl','z','y','xh'}, dimensions={0} | all-to-all | bytes 1048576 | tf_op jit(solution)/shard_map/all_to_all | solution.py:288
  139.0 3.2 %collective-permute-start.5 = (bf16[64,4,8,128]{3,2,1,0:T(8,128)(2,1)S(1)}, bf16[64,4,8,128]{3,2,1,0:T(8,128)(2,1)S(1)}, u32[]{:S(2)}, u32[]{:S(2)}) collective-permute-start(bf16[64,4,8,128]{3,2,1,0:T(8,128)(2,1)S(1)} %all_to_all.45.own_ref), channel_id=1, source_target_pairs={{0,4},{4,0},{1,5},{5,1},{2,6},{6,2},{3,7},{7,3},{8,12},{12,8},{9,1... | collective-permute-start | bytes 1572872 | tf_op jit(solution)/shard_map/ppermute | solution.py:289
  142.2 2.1 %own.5 = (f32[64,64]{1,0:T(8,128)S(1)}, f32[64,960]{1,0:T(8,128)S(1)}) custom-call(bf16[64,4,8,128]{3,2,1,0:T(8,128)(2,1)S(1)} %all_to_all.45.own_ref, bf16[960,6144]{1,0:T(8,128)(2,1)S(1)} %get-tuple-element.24.b_ref.a_ref), custom_call_target="tpu_custom_call" | custom-call | tf_op jit(solution)/shard_map/own/pallas_call | solution.py:318
  144.3 0.0 collective-permute-done.5.other_ref
  144.3 3.6 %step.5 = (bf16[64,3,8,128]{3,2,1,0:T(8,128)(2,1)S(1)}, bf16[64,960]{1,0:T(8,128)(2,1)S(1)}, f32[64,64]{1,0:T(8,128)S(1)}) custom-call(bf16[64,4,8,128]{3,2,1,0:T(8,128)(2,1)S(1)} %collective-permute-done.5.other_ref, f32[64,64]{1,0:T(8,128)S(1)} %get-tuple-element.35.gram_ref, f32[64,960]{1,0:T(8,128)S(1)} %get-tuple-element.36.raw_ref, ...), custom_call_target="tpu_custom_call" | custom-call | tf_op jit(solution)/shard_map/step/pallas_call | solution.py:322
  147.9 0.0 copy-start
  148.0 0.1 collective-permute-start.6
  148.1 1.2 keep.7
  149.3 0.5 collective-permute-done.6
  149.8 0.1 add_convert_fusion
  149.8 15.4 %all_to_all.46.terms_ref = bf16[64,3,8,128]{3,2,1,0:T(8,128)(2,1)S(1)} all-to-all(bf16[64,3,8,128]{3,2,1,0:T(8,128)(2,1)S(1)} %add_convert_fusion), channel_id=1, replica_groups=mesh['y'=4,'xh'=2,'xl'=2,'core'=2,'z'=4] {'xl','z','y','xh'}, dimensions={0} | all-to-all | bytes 786432 | tf_op jit(solution)/shard_map/all_to_all | solution.py:278
  165.2 0.1 spread.3
  165.3 15.3 %all_to_all.47.own_ref = bf16[64,4,8,128]{3,2,1,0:T(8,128)(2,1)S(1)} all-to-all(bf16[64,4,8,128]{3,2,1,0:T(8,128)(2,1)S(1)} %spread.3), channel_id=1, replica_groups=mesh['y'=4,'xh'=2,'xl'=2,'core'=2,'z'=4] {'xl','z','y','xh'}, dimensions={0} | all-to-all | bytes 1048576 | tf_op jit(solution)/shard_map/all_to_all | solution.py:288
  180.6 3.2 %collective-permute-start.7 = (bf16[64,4,8,128]{3,2,1,0:T(8,128)(2,1)S(1)}, bf16[64,4,8,128]{3,2,1,0:T(8,128)(2,1)S(1)}, u32[]{:S(2)}, u32[]{:S(2)}) collective-permute-start(bf16[64,4,8,128]{3,2,1,0:T(8,128)(2,1)S(1)} %all_to_all.47.own_ref), channel_id=1, source_target_pairs={{0,4},{4,0},{1,5},{5,1},{2,6},{6,2},{3,7},{7,3},{8,12},{12,8},{9,1... | collective-permute-start | bytes 1572872 | tf_op jit(solution)/shard_map/ppermute | solution.py:289
  183.8 0.3 left.1.left_ref
  184.1 0.3 own_gram.1.gram_ref
  184.4 1.0 collective-permute-done.7.other_ref
  185.4 4.1 %last.1 = (f32[192,1536]{1,0:T(8,128)}, f32[64,192]{1,0:T(8,128)}, f32[64,1536]{1,0:T(8,128)}) custom-call(bf16[64,4,8,128]{3,2,1,0:T(8,128)(2,1)S(1)} %all_to_all.47.own_ref, bf16[64,4,8,128]{3,2,1,0:T(8,128)(2,1)S(1)} %collective-permute-done.7.other_ref, f32[64,64]{1,0:T(8,128)S(1)} %own_gram.1.gram_ref, f32[64,192]{1,0:T(8,128)S(1)} %left.1.left_ref, ...), custom_call_target="tpu_custom_call" | custom-call | tf_op jit(solution)/shard_map/last/pallas_call | solution.py:343
  (2 shorter events, 0.0 us)
Async XLA Ops:
  12.8 2.9 %collective-permute-start = (bf16[64,3,8,128]{3,2,1,0:T(8,128)(2,1)S(1)}, bf16[64,3,8,128]{3,2,1,0:T(8,128)(2,1)S(1)}, u32[]{:S(2)}, u32[]{:S(2)}) collective-permute-start(bf16[64,3,8,128]{3,2,1,0:T(8,128)(2,1)S(1)} %get-tuple-element.25), channel_id=1, source_target_pairs={{0,4},{4,0},{1,5},{5,1},{2,6},{6,2},{3,7},{7,3},{8,12},{12,8},{9,1... | collective-permute-start | bytes 1179656 | tf_op jit(solution)/shard_map/ppermute | solution.py:276
  56.1 5.4 %collective-permute-start.1 = (f32[64,3,8,128]{3,2,1,0:T(8,128)S(1)}, f32[64,3,8,128]{3,2,1,0:T(8,128)S(1)}, u32[]{:S(2)}, u32[]{:S(2)}) collective-permute-start(f32[64,3,8,128]{3,2,1,0:T(8,128)S(1)} %all_to_all.41.own_ref), channel_id=1, source_target_pairs={{0,4},{4,0},{1,5},{5,1},{2,6},{6,2},{3,7},{7,3},{8,12},{12,8},{9,1... | collective-permute-start | bytes 2359304 | tf_op jit(solution)/shard_map/ppermute | solution.py:289
  65.9 1.8 collective-permute-start.2
  97.5 5.1 %collective-permute-start.3 = (bf16[64,3,8,128]{3,2,1,0:T(8,128)(2,1)S(1)}, bf16[64,3,8,128]{3,2,1,0:T(8,128)(2,1)S(1)}, u32[]{:S(2)}, u32[]{:S(2)}) collective-permute-start(bf16[64,3,8,128]{3,2,1,0:T(8,128)(2,1)S(1)} %all_to_all.43.own_ref), channel_id=1, source_target_pairs={{0,4},{4,0},{1,5},{5,1},{2,6},{6,2},{3,7},{7,3},{8,12},{12,8},{9,1... | collective-permute-start | bytes 1179656 | tf_op jit(solution)/shard_map/ppermute | solution.py:289
  106.3 1.8 collective-permute-start.4
  139.0 5.3 %collective-permute-start.5 = (bf16[64,4,8,128]{3,2,1,0:T(8,128)(2,1)S(1)}, bf16[64,4,8,128]{3,2,1,0:T(8,128)(2,1)S(1)}, u32[]{:S(2)}, u32[]{:S(2)}) collective-permute-start(bf16[64,4,8,128]{3,2,1,0:T(8,128)(2,1)S(1)} %all_to_all.45.own_ref), channel_id=1, source_target_pairs={{0,4},{4,0},{1,5},{5,1},{2,6},{6,2},{3,7},{7,3},{8,12},{12,8},{9,1... | collective-permute-start | bytes 1572872 | tf_op jit(solution)/shard_map/ppermute | solution.py:289
  147.9 37.4 %copy-start = (bf16[192,1536]{1,0:T(8,128)(2,1)S(1)}, bf16[192,1536]{1,0:T(8,128)(2,1)}, u32[]{:S(2)}) copy-start(bf16[192,1536]{1,0:T(8,128)(2,1)} %weight_ref.1) | copy-start | bytes 1769476
  148.0 1.8 collective-permute-start.6
  180.6 4.7 %collective-permute-start.7 = (bf16[64,4,8,128]{3,2,1,0:T(8,128)(2,1)S(1)}, bf16[64,4,8,128]{3,2,1,0:T(8,128)(2,1)S(1)}, u32[]{:S(2)}, u32[]{:S(2)}) collective-permute-start(bf16[64,4,8,128]{3,2,1,0:T(8,128)(2,1)S(1)} %all_to_all.47.own_ref), channel_id=1, source_target_pairs={{0,4},{4,0},{1,5},{5,1},{2,6},{6,2},{3,7},{7,3},{8,12},{12,8},{9,1... | collective-permute-start | bytes 1572872 | tf_op jit(solution)/shard_map/ppermute | solution.py:289
